TPU v7x, 256 devices: a whole 4x4x8 slice. The times are simulated.
256 devices in a mesh: frame: 64 (over x, z, core), head: 4 (over y).
Axes of the slice: x: 4, y: 4, z: 8, core: 2. Of those that a mesh axis runs over, the one named last changes fastest.
Arguments:
- q_raw: bfloat16 [8192, 5120], P('frame', 'head'), may hold values from -4096 to 4096
- k_raw: bfloat16 [8192, 5120], P('frame', 'head'), may hold values from -4096 to 4096
- v_in: bfloat16 [8192, 5120], P('frame', 'head'), may hold values from -18 to 18
- gain_q: float32 [5120], P('head'), may hold values from 0.5 to 1.5
- gain_k: float32 [5120], P('head'), may hold values from 0.5 to 1.5
- frame_index: int32 [8192], P('frame'), may hold values from 0 to 2, as said below
- reach: int32 [64], P('frame'), may hold values from 0 to 3, as said below
- cotangent: bfloat16 [8192, 5120], P('frame', 'head'), may hold values from -6 to 6
Outputs:
- scaled_out: bfloat16 [8192, 5120], P('frame', 'head')
- grad_q: bfloat16 [8192, 5120], P('frame', 'head')
- grad_k: bfloat16 [8192, 5120], P('frame', 'head')
- grad_v: bfloat16 [8192, 5120], P('frame', 'head')
- grad_gain_q: float32 [5120], P('head')
- grad_gain_k: float32 [5120], P('head')
Inputs may be any that keep to these rules, and one draw needn't show every extreme that they name: `frame_index`: within each group of 128 tokens the frame never falls, and all 3 frames are present. reach[c] <= c; reach[1] is 0; the last group has 3.
All inputs are finite; a program needn't handle non-finite values. Where the computation divides by a largest or mean magnitude, that divisor is 1e-20 or more.
Results may differ from a plain program's by a relative error of at most 0.035.
Values may be sent and summed in bfloat16 or wider, within the bound.
No kernel may reach another device: no remote copies, remote signals or barrier semaphores. Data moves between devices by JAX's collectives and lax.ppermute only.
A program may use at most 64 MiB of HBM per device.

v0:
```python
import jax
import jax.numpy as jnp
from jax import lax
from jax.sharding import PartitionSpec as P

D = 5120
HD = 128
LAGS = 3


EPSILON = 1e-06


def from_behind(shard, axis, by):
    length = lax.axis_size(axis)
    pairs = [(i, i + by) for i in range(length) if 0 <= i + by < length]
    return lax.ppermute(shard, axis, pairs)


def spread(block, axis, holder):
    block = jnp.where(lax.axis_index(axis) == holder, block, jnp.zeros_like(block))
    return lax.psum(block, axis)


def block_scores(query_rows, key_rows, allowed_now):
    heads_here = query_rows.shape[1]
    split_keys = key_rows.reshape(key_rows.shape[0], heads_here, HD)
    scores = jnp.einsum(
        "thd,shd->hts", query_rows, split_keys, preferred_element_type=jnp.float32
    ) * HD ** (-0.5)
    return jnp.where(allowed_now, scores, -jnp.inf)


def finish_norm(grad_norm, values, row_rates, gain_row, inner_sum):
    cubed = row_rates * row_rates * row_rates
    grad_raw = (
        row_rates[:, None] * gain_row[None, :] * grad_norm
        - values * (cubed * inner_sum / D)[:, None]
    )
    return grad_raw.astype(jnp.bfloat16)


def per_device(q_raw, k_raw, v_in, gain_q, gain_k, frame_index, reach, cotangent):
    tok_rows = q_raw.shape[0]
    feature_width = q_raw.shape[1]
    heads_here = feature_width // HD
    q_vals = q_raw.astype(jnp.float32)
    k_vals = k_raw.astype(jnp.float32)
    sums_q, sums_k = lax.psum(
        (jnp.sum(q_vals * q_vals, axis=1), jnp.sum(k_vals * k_vals, axis=1)), "head"
    )
    rate_q = lax.rsqrt(sums_q / D + EPSILON)
    rate_k = lax.rsqrt(sums_k / D + EPSILON)
    q_norm = (q_vals * rate_q[:, None] * gain_q[None, :]).astype(jnp.bfloat16)
    k_norm = (k_vals * rate_k[:, None] * gain_k[None, :]).astype(jnp.bfloat16)
    query_rows = q_norm.reshape(tok_rows, heads_here, HD)
    packed = jnp.stack([k_norm, v_in])
    group_id = lax.axis_index("frame")
    reach_here = reach[0]
    remote = []
    for offset in range(1, LAGS + 1):
        remote.append(from_behind(packed, "frame", offset))
    sink_pair = spread(packed, "frame", 0)
    own_mask = (frame_index[None, :] <= frame_index[:, None])[None]
    blocks = [(packed, own_mask)]
    for offset in range(1, LAGS + 1):
        blocks.append((remote[offset - 1], offset <= reach_here))
    blocks.append((sink_pair, group_id > reach_here))
    block_count = len(blocks)
    mask_stack = jnp.stack(
        [
            jnp.broadcast_to(allowed_now, (1, tok_rows, tok_rows))[0]
            for key_pair, allowed_now in blocks
        ]
    )
    every_pair = jnp.stack([key_pair for key_pair, allowed_now in blocks])
    split_pairs = every_pair.reshape(block_count, 2, tok_rows, heads_here, HD)
    keys_by_head = jnp.transpose(split_pairs[:, 0], (2, 0, 1, 3))
    values_by_head = jnp.transpose(split_pairs[:, 1], (2, 0, 1, 3))
    queries_by_head = jnp.transpose(query_rows, (1, 0, 2))

    def head_forward(inputs):
        query_head, key_head, value_head = inputs
        scores = jnp.einsum(
            "td,bsd->bts", query_head, key_head, preferred_element_type=jnp.float32
        ) * HD ** (-0.5)
        scores = jnp.where(mask_stack, scores, -jnp.inf)
        top_row = jnp.max(jnp.max(scores, axis=2), axis=0)
        weights = jnp.exp(scores - top_row[None, :, None])
        total_row = jnp.sum(jnp.sum(weights, axis=2), axis=0)
        summed = jnp.einsum(
            "bts,bsd->td",
            weights.astype(jnp.bfloat16),
            value_head,
            preferred_element_type=jnp.float32,
        )
        return (summed, top_row, total_row)

    head_sums, highest, row_totals = lax.map(
        head_forward, (queries_by_head, keys_by_head, values_by_head)
    )
    accumulated = jnp.transpose(head_sums, (1, 0, 2))
    attn_out = (
        (accumulated / jnp.transpose(row_totals)[:, :, None])
        .astype(jnp.bfloat16)
        .reshape(tok_rows, feature_width)
    )
    local_max = jnp.max(jnp.abs(attn_out.astype(jnp.float32)), axis=0)
    chan_max = lax.pmax(local_max, "frame")
    scaled_out = (attn_out.astype(jnp.float32) / (chan_max + EPSILON)).astype(jnp.bfloat16)
    grad_attn = (
        (cotangent.astype(jnp.float32) / (chan_max + EPSILON))
        .astype(jnp.bfloat16)
        .reshape(tok_rows, heads_here, HD)
    )
    out_heads = attn_out.reshape(tok_rows, heads_here, HD)
    row_delta = jnp.einsum("thd,thd->ht", grad_attn, out_heads, preferred_element_type=jnp.float32)
    grad_query = jnp.zeros((tok_rows, heads_here, HD), jnp.float32)
    block_grads = []
    for key_pair, allowed_now in blocks:
        split_keys = key_pair[0].reshape(tok_rows, heads_here, HD)
        split_values = key_pair[1].reshape(tok_rows, heads_here, HD)
        attn_probs = (
            jnp.exp(block_scores(query_rows, key_pair[0], allowed_now) - highest[:, :, None])
            / row_totals[:, :, None]
        )
        grad_value = jnp.einsum(
            "hts,thd->shd",
            attn_probs.astype(jnp.bfloat16),
            grad_attn,
            preferred_element_type=jnp.float32,
        )
        grad_prob = jnp.einsum(
            "thd,shd->hts", grad_attn, split_values, preferred_element_type=jnp.float32
        )
        grad_score = (attn_probs * (grad_prob - row_delta[:, :, None])).astype(jnp.bfloat16)
        grad_query = grad_query + jnp.einsum(
            "hts,shd->thd", grad_score, split_keys, preferred_element_type=jnp.float32
        ) * HD ** (-0.5)
        grad_key = jnp.einsum(
            "hts,thd->shd", grad_score, query_rows, preferred_element_type=jnp.float32
        ) * HD ** (-0.5)
        block_grads.append(
            jnp.stack(
                [
                    grad_key.reshape(tok_rows, feature_width),
                    grad_value.reshape(tok_rows, feature_width),
                ]
            )
        )
    returned = jnp.zeros_like(block_grads[0])
    for offset in range(1, LAGS + 1):
        returned = returned + from_behind(
            block_grads[offset].astype(jnp.bfloat16), "frame", -offset
        ).astype(jnp.float32)
    sink_total = lax.psum(block_grads[LAGS + 1], "frame")
    key_total = block_grads[0] + returned + jnp.where(group_id == 0, sink_total, 0.0)
    grad_qn = grad_query.reshape(tok_rows, feature_width)
    grad_kn = key_total[0]
    grad_v = key_total[1].astype(jnp.bfloat16)
    inner_q, inner_k = lax.psum(
        (
            jnp.sum(gain_q[None, :] * grad_qn * q_vals, axis=1),
            jnp.sum(gain_k[None, :] * grad_kn * k_vals, axis=1),
        ),
        "head",
    )
    grad_gain_q, grad_gain_k = lax.psum(
        (
            jnp.sum(grad_qn * q_vals * rate_q[:, None], axis=0),
            jnp.sum(grad_kn * k_vals * rate_k[:, None], axis=0),
        ),
        "frame",
    )
    grad_q = finish_norm(grad_qn, q_vals, rate_q, gain_q, inner_q)
    grad_k = finish_norm(grad_kn, k_vals, rate_k, gain_k, inner_k)
    return (scaled_out, grad_q, grad_k, grad_v, grad_gain_q, grad_gain_k)


def solution(mesh):
    placed = (
        P("frame", "head"),
        P("frame", "head"),
        P("frame", "head"),
        P("head"),
        P("head"),
        P("frame"),
        P("frame"),
        P("frame", "head"),
    )
    return jax.shard_map(
        per_device,
        mesh=mesh,
        in_specs=placed,
        out_specs=(
            P("frame", "head"),
            P("frame", "head"),
            P("frame", "head"),
            P("frame", "head"),
            P("head"),
            P("head"),
        ),
        check_vma=False,
    )
```

profile of v0, /device:TPU:1, one launch (start us, length us, event | category | flops | bytes accessed | tf_op | source)
XLA Modules:
  0.0 849.2 jit_solution(2347548015256795798)
XLA Ops:
  10.2 9.6 %all-reduce.2 = (f32[128]{0:T(128)S(1)}, f32[128]{0:T(128)S(1)}) all-reduce(f32[128]{0:T(128)S(1)} %fusion.52, f32[128]{0:T(128)S(1)} %fusion.60), channel_id=1, replica_groups=mesh['frame'=64,'head'=4] {'head'}, use_global_device_ids=true, to_apply=%region_3.0 | all-reduce | flops 256 | bytes 2048 | tf_op jit(solution)/shard_map/psum | solution.py:49
  21.2 6.1 collective-permute-start
  27.4 3.6 collective-permute-start.1
  31.0 3.6 collective-permute-start.2
  37.0 1.9 copy.73
  38.9 177.5 %all-reduce.6.cloned.1.call-done = bf16[2,128,1280]{1,2,0:T(8,128)(2,1)} async-done(((bf16[2,128,1280]{1,2,0:T(8,128)(2,1)}), bf16[2,128,1280]{1,2,0:T(8,128)(2,1)}) %all-reduce.6.cloned.1.call-update) | async-done | bytes 655376 | tf_op jit(solution)/shard_map/psum | solution.py:22
  216.4 1.9 fusion.88
  222.1 3.5 slice_bitcast_fusion
  225.6 22.4 %while.14 = (s32[]{:T(128)}, f32[10,128,128]{1,2,0:T(8,128)}, f32[10,128]{1,0:T(8,128)S(1)}, f32[10,128]{1,0:T(8,128)S(1)}, bf16[10,5,128,128]{2,3,0,1:T(8,128)(...) while((s32[]{:T(128)}, f32[10,128,128]{1,2,0:T(8,128)}, ...), condition=%wide.region_8.9_spmd, body=%wide.region_5.8_spmd.sunk | while | flops 42516224 | bytes 1497197 | solution.py:99
  225.6 1.2 fusion.145
  248.0 1.4 abs_reduce_fusion
  249.4 126.6 %pmax.7 = f32[1280]{0:T(1024)S(1)} all-reduce(f32[1280]{0:T(1024)S(1)} %bitcast.245), channel_id=1, replica_groups=mesh['frame'=64,'head'=4] {'frame'}, use_global_device_ids=true, to_apply=%region_10.11 | all-reduce | flops 1280 | bytes 10240 | tf_op jit(solution)/shard_map/pmax | solution.py:109
  378.1 1.2 fusion.90
  385.4 4.6 collective-permute-start.3
  392.5 1.3 collective-permute-start.4
  394.7 1.5 collective-permute-start.5
  400.0 1.2 convolution_add_fusion.1
  402.2 1.8 fusion.33
  406.7 5.1 collective-permute-done.4
  411.8 19.0 %collective-permute-done.5 = bf16[2,128,1280]{1,2,0:T(8,128)(2,1)} collective-permute-done((bf16[2,128,1280]{1,2,0:T(8,128)(2,1)}, bf16[2,128,1280]{1,2,0:T(8,128)(2,1)}, u32[]{:S(2)}, u32[]{:S(2)}) %collective-permute-start.5) | collective-permute-done | bytes 655392 | tf_op jit(solution)/shard_map/ppermute | solution.py:17
  430.8 151.2 %all-reduce.8.cloned.1.call-done = f32[2,128,1280]{1,2,0:T(8,128)} async-done(((f32[2,128,1280]{1,2,0:T(8,128)}), f32[2,128,1280]{1,2,0:T(8,128)}) %all-reduce.8.cloned.1.call-update) | async-done | bytes 1310736 | tf_op jit(solution)/shard_map/psum | solution.py:156
  582.0 2.2 fusion.15
  584.7 8.5 all-reduce.1
  596.4 245.9 %all-reduce = (f32[1280]{0:T(1024)}, f32[1280]{0:T(1024)}) all-reduce(f32[1280]{0:T(1024)S(1)} %get-tuple-element.69, f32[1280]{0:T(1024)S(1)} %get-tuple-element.67), channel_id=1, replica_groups=mesh['frame'=64,'head'=4] {'frame'}, use_global_device_ids=true, to_apply=%region_17.18 | all-reduce | flops 2560 | bytes 20480 | tf_op jit(solution)/shard_map/psum | solution.py:168
  (168 shorter events, 53.4 us)
Async XLA Ops:
  7.2 2.9 copy-start.18
  7.2 209.2 %all-reduce.6.cloned.1.call-start = ((), (), s32[]{:S(2)}) async-start(), calls=%async_computation | async-start | bytes 1310720 | tf_op jit(solution)/shard_map/psum | solution.py:22
  7.2 12.6 %copy-start.19 = (f32[1280]{0:T(1024)S(1)}, f32[1280]{0:T(1024)}, u32[]{:S(2)}) copy-start(f32[1280]{0:T(1024)} %param.14) | copy-start | bytes 15364
  20.1 14.8 %copy-start.21 = (s32[128]{0:T(128)S(1)}, s32[128]{0:T(128)}, u32[]{:S(2)}) copy-start(s32[128]{0:T(128)} %param.15) | copy-start | bytes 1540
  21.2 197.1 %collective-permute-start = (bf16[2,128,1280]{1,2,0:T(8,128)(2,1)}, bf16[2,128,1280]{1,2,0:T(8,128)(2,1)S(1)}, u32[]{:S(2)}, u32[]{:S(2)}) collective-permute-start(bf16[2,128,1280]{1,2,0:T(8,128)(2,1)} %get-tuple-element.108), channel_id=1, source_target_pairs={{0,4},{4,8},{8,12},{12,16},{16,20},{20,24},{24,28},{28,32},{32,36}... | collective-permute-start | bytes 1966088 | tf_op jit(solution)/shard_map/ppermute | solution.py:17
  27.4 191.9 %collective-permute-start.1 = (bf16[2,128,1280]{1,2,0:T(8,128)(2,1)}, bf16[2,128,1280]{1,2,0:T(8,128)(2,1)S(1)}, u32[]{:S(2)}, u32[]{:S(2)}) collective-permute-start(bf16[2,128,1280]{1,2,0:T(8,128)(2,1)} %get-tuple-element.108), channel_id=1, source_target_pairs={{0,8},{4,12},{8,16},{12,20},{16,24},{20,28},{24,32},{28,36},{32,40... | collective-permute-start | bytes 1966088 | tf_op jit(solution)/shard_map/ppermute | solution.py:17
  31.0 189.2 %collective-permute-start.2 = (bf16[2,128,1280]{1,2,0:T(8,128)(2,1)}, bf16[2,128,1280]{1,2,0:T(8,128)(2,1)S(1)}, u32[]{:S(2)}, u32[]{:S(2)}) collective-permute-start(bf16[2,128,1280]{1,2,0:T(8,128)(2,1)} %get-tuple-element.108), channel_id=1, source_target_pairs={{0,12},{4,16},{8,20},{12,24},{16,28},{20,32},{24,36},{28,40},{32,4... | collective-permute-start | bytes 1966088 | tf_op jit(solution)/shard_map/ppermute | solution.py:17
  34.5 2.1 copy-start.20
  34.6 547.5 %all-reduce.8.cloned.1.call-start = ((), (), s32[]{:S(2)}) async-start(), calls=%async_computation.1 | async-start | bytes 2621440 | tf_op jit(solution)/shard_map/psum | solution.py:156
  34.9 1.8 copy-start
  218.3 1.8 copy-start.6
  219.3 1.8 copy-start.4
  219.3 1.9 copy-start.10
  225.6 150.5 %copy-start.14 = (bf16[128,1280]{0,1:T(8,128)(2,1)S(1)}, bf16[128,1280]{0,1:T(8,128)(2,1)}, u32[]{:S(2)}) copy-start(bf16[128,1280]{0,1:T(8,128)(2,1)} %copy.73) | copy-start | bytes 983044
  248.0 128.4 %copy-start.9 = (bf16[2,128,1280]{1,2,0:T(8,128)(2,1)S(1)}, bf16[2,128,1280]{1,2,0:T(8,128)(2,1)}, u32[]{:S(2)}) copy-start(bf16[2,128,1280]{1,2,0:T(8,128)(2,1)} %copy-done.8) | copy-start | bytes 1966084
  377.8 1.5 copy-start.11
  381.3 1.5 copy-start.7
  384.2 5.7 copy-start.5
  385.4 21.3 %collective-permute-start.3 = (bf16[2,128,1280]{1,2,0:T(8,128)(2,1)}, bf16[2,128,1280]{1,2,0:T(8,128)(2,1)}, u32[]{:S(2)}, u32[]{:S(2)}) collective-permute-start(bf16[2,128,1280]{1,2,0:T(8,128)(2,1)} %pad_maximum_fusion.2), channel_id=1, source_target_pairs={{4,0},{8,4},{12,8},{16,12},{20,16},{24,20},{28,24},{32,28},{36,32}... | collective-permute-start | bytes 1966088 | tf_op jit(solution)/shard_map/ppermute | solution.py:17
  392.5 19.3 %collective-permute-start.4 = (bf16[2,128,1280]{1,2,0:T(8,128)(2,1)}, bf16[2,128,1280]{1,2,0:T(8,128)(2,1)}, u32[]{:S(2)}, u32[]{:S(2)}) collective-permute-start(bf16[2,128,1280]{1,2,0:T(8,128)(2,1)} %pad_maximum_fusion.3), channel_id=1, source_target_pairs={{8,0},{12,4},{16,8},{20,12},{24,16},{28,20},{32,24},{36,28},{40,32... | collective-permute-start | bytes 1966088 | tf_op jit(solution)/shard_map/ppermute | solution.py:17
  394.7 36.1 %collective-permute-start.5 = (bf16[2,128,1280]{1,2,0:T(8,128)(2,1)}, bf16[2,128,1280]{1,2,0:T(8,128)(2,1)}, u32[]{:S(2)}, u32[]{:S(2)}) collective-permute-start(bf16[2,128,1280]{1,2,0:T(8,128)(2,1)} %pad_maximum_fusion.4), channel_id=1, source_target_pairs={{12,0},{16,4},{20,8},{24,12},{28,16},{32,20},{36,24},{40,28},{44,3... | collective-permute-start | bytes 1966088 | tf_op jit(solution)/shard_map/ppermute | solution.py:17
  398.8 1.2 copy-start.17
  400.0 2.2 copy-start.13
  404.0 1.5 copy-start.3
  (6 other events, 5.4 us)
Sparse Core Ops, SparseCore 0:
  34.7 181.6 all-reduce.5
  397.4 184.5 all-reduce.7
where the time goes:
time: 852 us; the launch traced here: 849 us
  blocking collectives  391 us (46%)
  waiting for transfers between devices  353 us (41%)
  matrix products  35.7 us (4%)
  starting transfers between devices  20.6 us (2%)
  local copies, waits for them, and re-layouts  20.4 us (2%)
  between operations  15.3 us (2%)
  other arithmetic  13.6 us (2%)
    psum x1, blocking collectives, per_device(): lax.psum((jnp.sum(grad_qn * q_vals * rate_q[:, None], axis=0), jnp.sum(gr...  246 us
    psum x1, waiting for transfers between devices, spread(): return lax.psum(block, axis)  178 us
    psum x1, waiting for transfers between devices, per_device(): sink_total = lax.psum(block_grads[LAGS + 1], 'frame')  151 us
    pmax x1, blocking collectives, per_device(): chan_max = lax.pmax(local_max, 'frame')  127 us
    ppermute x6, waiting for transfers between devices, from_behind(): return lax.ppermute(shard, axis, pairs)  24.1 us
    ppermute x6, starting transfers between devices, from_behind(): return lax.ppermute(shard, axis, pairs)  20.5 us
  transfers between devices with their start and end apart: 8, of which 4 were waited for; matrix products, arithmetic and copies ran while one was open for 2% of the time, Pallas kernels for 0%

commit v1 on v0

v1 whole, which is shorter than its diff:
```python
import jax
import jax.numpy as jnp
from jax import lax
from jax.experimental import pallas as pl
from jax.experimental.pallas import tpu as pltpu
from jax.sharding import PartitionSpec as P

D = 5120
HD = 128
XS = 4
ZS = 8
TOK = 128
HALF = 640
HEADS = HALF // HD
KEYS = 6 * TOK
QUARTER = TOK // XS
EPSILON = 1e-06
HIDDEN = -1e30
F32 = jnp.float32
BF16 = jnp.bfloat16


def chip_pairs(move):
    pairs = []
    for x in range(XS):
        for z in range(ZS):
            to = move(x, z)
            if to is not None:
                for core in range(2):
                    pairs.append(((x * ZS + z) * 2 + core, (to[0] * ZS + to[1]) * 2 + core))
    return pairs


def move_chips(value, move):
    return lax.ppermute(value, "frame", chip_pairs(move))


def line_shift(by):
    def move(x, z):
        chip = x * ZS + z + by
        return divmod(chip, ZS) if 0 <= chip < XS * ZS else None

    return move


def shift_x(value, by):
    return move_chips(value, lambda x, z: ((x + by) % XS, z))


def shift_z(value, by):
    return move_chips(value, lambda x, z: (x, (z + by) % ZS))


def swap_z(value, bit):
    return move_chips(value, lambda x, z: (x, z ^ bit))


def other_core(value):
    return lax.ppermute(value, "frame", [(i, i ^ 1) for i in range(2 * XS * ZS)])


def sum_heads(value):
    turns = [lax.ppermute(value, "head", [(i, (i + by) % 4) for i in range(4)]) for by in (2, 1, 3)]
    return (value + turns[0]) + (turns[1] + turns[2])


def pairs_of(turn):
    return lambda x, z: turn.get((x, z))


def column(moves, xs):
    return {(x, a): (x, b) for x in xs for a, b in moves.items()}


def row(a, b, zs):
    return {(a, z): (b, z) for z in zs}


SCATTER_X = tuple(row(0, to, (0,)) for to in range(1, XS))
GATHER_X = tuple(row(src, 0, (0,)) for src in range(1, XS))
SPREAD_Z = (
    (column({0: 3}, range(XS)), column({0: 5}, range(XS))),
    (column({0: 1, 3: 4, 5: 6}, range(XS)), column({0: 7, 3: 2}, range(XS))),
)
GATHER_Z = (
    (column({1: 0, 4: 3, 6: 5}, range(XS)), column({7: 0, 2: 3}, range(XS))),
    (column({3: 0}, range(XS)), column({5: 0}, range(XS))),
)


def spread_sink(quarters, root):
    total = jnp.where(root, quarters[0], jnp.zeros_like(quarters[0]))
    for quarter, turn in zip(quarters[1:], SCATTER_X):
        total = total + move_chips(quarter, pairs_of(turn))
    for turns in SPREAD_Z:
        got = [move_chips(total, pairs_of(turn)) for turn in turns]
        total = total + got[0] + got[1]
    return [total] + [shift_x(total, by) for by in (1, 2, 3)]


def gather_z(total, index):
    low = total.astype(BF16)
    got = [move_chips(low, pairs_of(turn)) for turn in GATHER_Z[index]]
    return total + got[0].astype(F32) + got[1].astype(F32)


def after(values, *others):
    return lax.optimization_barrier((values, others))[0]


def pairs_z(value, join):
    return join(value, swap_z(value, 1))


def quads_z(value, join):
    turns = [shift_z(value, by) for by in (4, 2, 6)]
    return join(join(value, turns[0]), join(turns[1], turns[2]))


def quads_x(value, join):
    turns = [shift_x(value, by) for by in (2, 1, 3)]
    return join(join(value, turns[0]), join(turns[1], turns[2]))


def contract(a, b, dims, **kw):
    return lax.dot_general(a, b, (dims, ((), ())), preferred_element_type=F32, **kw)


def lane_sums(block):
    ones = jnp.ones((8, HD), F32)
    return contract(ones, block, ((1,), (1,)), precision=lax.Precision.HIGHEST)[:1]


def upright(line):
    return jnp.broadcast_to(line, (TOK, TOK)).T[:, :1]


def fold(block):
    total = block[:, :HD]
    for start in range(HD, block.shape[1], HD):
        total = total + block[:, start : start + HD]
    return total


def sums_kernel(q, k, sums):
    for row, ref in enumerate((q, k)):
        values = ref[...].astype(F32)
        sums[row : row + 1] = lane_sums(fold(values * values))


def split_kernel(core, q, k, v, c, keep, send):
    mine = pl.ds(pl.multiple_of(core[0] * HALF, HD), HALF)
    other = pl.ds(pl.multiple_of((1 - core[0]) * HALF, HD), HALF)
    for index, ref in enumerate((q, k, v, c)):
        keep[index] = ref[:, mine]
        send[index] = ref[:, other]


def norm_kernel(place, keep, got, tags, tags_got, gain_q, gain_k, q_norm, k_norm, bias, *quarters):
    for half, (source, tag) in enumerate(((keep, tags), (got, tags_got))):
        rows = slice(half * TOK, (half + 1) * TOK)
        rate_q = upright(lax.rsqrt(tag[0:1] / D + EPSILON))
        rate_k = upright(lax.rsqrt(tag[1:2] / D + EPSILON))
        q_norm[rows] = (source[0].astype(F32) * rate_q * gain_q[...]).astype(BF16)
        k_norm[rows] = (source[1].astype(F32) * rate_k * gain_k[...]).astype(BF16)
    core = place[0] % 2

    def fill(source, start):
        for index, quarter in enumerate(quarters):
            quarter[:, :HALF] = k_norm[start + index * QUARTER : start + (index + 1) * QUARTER]
            quarter[:, HALF:] = source[2, index * QUARTER : (index + 1) * QUARTER]

    @pl.when(core == 0)
    def _():
        fill(keep, 0)

    @pl.when(core == 1)
    def _():
        fill(got, TOK)

    chip = place[0] // 2
    groups = (place[0], place[0] + 1 - 2 * core)
    ahead = 2 * chip - 2 + core
    key_groups = groups + (ahead, 4 * chip - 3 - ahead, 2 * chip - 3)
    nothing = jnp.zeros((TOK, TOK), F32)
    for half, tag in enumerate((tags, tags_got)):
        rows = slice(half * TOK, (half + 1) * TOK)
        frames = tag[2:3]
        reach = jnp.broadcast_to(tag[3:4], (TOK, TOK))
        for block in range(6):
            cols = slice(block * TOK, (block + 1) * TOK)
            if block == half:
                seen = frames <= upright(frames)
            elif block == 5:
                seen = reach < (nothing + groups[half].astype(F32))
            else:
                back = nothing + (groups[half] - key_groups[block]).astype(F32)
                seen = (back >= 1.0) & (back <= reach)
            bias[rows, cols] = jnp.where(seen, 0.0, HIDDEN)


def lanes_of(head):
    return slice(head * HD, (head + 1) * HD)


def key_rows(blocks, lanes):
    return jnp.concatenate([ref[:, lanes] for ref in blocks], axis=0)


def forward_kernel(
    place, bias, q, ko, kp, ke, vo, vp, ve, s0, s1, s2, s3, attn, top, probs, sink
):
    x = place[0] // (2 * ZS)
    for by, part in enumerate((s0, s1, s2, s3)):
        start = pl.multiple_of(((x + XS - by) % XS) * QUARTER, QUARTER)
        sink[pl.ds(start, QUARTER)] = part[...]
    for head in range(HEADS):
        lanes = lanes_of(head)
        keys = jnp.concatenate([key_rows((ko, kp, ke), lanes), sink[:, lanes]], axis=0)
        values = jnp.concatenate(
            [key_rows((vo, vp, ve), lanes), sink[:, lanes_of(HEADS + head)]], axis=0
        )
        scores = contract(q[:, lanes], keys, ((1,), (1,))) * HD ** (-0.5) + bias[...]
        highest = jnp.max(scores, axis=1, keepdims=True)
        weights = jnp.exp(scores - highest)
        total = jnp.sum(weights, axis=1, keepdims=True)
        inverse = 1.0 / total
        summed = contract(weights.astype(BF16), values, ((1,), (0,)))
        rows = (summed * inverse).astype(BF16)
        attn[:, lanes] = rows
        top[:, lanes] = jnp.max(jnp.abs(rows.astype(F32)), axis=0, keepdims=True)
        probs[head] = (weights * inverse).astype(BF16)


def value_kernel(probs, keep, got, own, prev, early, sink):
    for head in range(HEADS):
        lanes = lanes_of(head)
        cot = jnp.concatenate([keep[3, :, lanes], got[3, :, lanes]], axis=0)
        grads = contract(probs[head], cot, ((0,), (0,)))
        own[:, lanes] = grads[: 2 * TOK]
        prev[:, lanes] = grads[2 * TOK : 4 * TOK].astype(BF16)
        early[:, lanes] = grads[4 * TOK : 5 * TOK].astype(BF16)
        sink[:, lanes] = grads[5 * TOK :].astype(BF16)


def sink_kernel(
    place, probs, keep, got, attn, chan, q, sink, v_low, p0, p1, p2, p3, grad_attn, delta, scaled, rows
):
    for head in range(HEADS):
        lanes = lanes_of(head)
        scale = chan[:, lanes] + EPSILON
        cot = jnp.concatenate([keep[3, :, lanes], got[3, :, lanes]], axis=0).astype(F32)
        grads = (cot / scale).astype(BF16)
        grad_attn[:, lanes] = grads
        out = attn[:, lanes].astype(F32)
        scaled[:, lanes] = (out / scale).astype(BF16)
        sums = jnp.sum(grads.astype(F32) * out, axis=1, keepdims=True)
        delta[:, lanes] = jnp.broadcast_to(sums, (2 * TOK, HD))
        grad_prob = contract(grads, sink[:, lanes_of(HEADS + head)], ((1,), (1,)))
        grad_score = (probs[head, :, 5 * TOK :].astype(F32) * (grad_prob - sums)).astype(BF16)
        rows[:, lanes] = contract(grad_score, q[:, lanes], ((0,), (0,))) * HD ** (-0.5)
    x = place[0] // (2 * ZS)
    for by, part in enumerate((p0, p1, p2, p3)):
        take = pl.ds(pl.multiple_of(((x + by) % XS) * QUARTER, QUARTER), QUARTER)
        part[:, :HALF] = rows[take].astype(BF16)
        part[:, HALF:] = v_low[take]


def backward_kernel(
    probs, grad_attn, delta, q, ko, kp, ke, vo, vp, ve, sink,
    grad_q, own, prev, early, gain_sum, inner,
):
    inner_q = jnp.zeros((2 * TOK, HD), F32)
    inner_k = jnp.zeros((KEYS, HD), F32)
    for head in range(HEADS):
        lanes = lanes_of(head)
        keys = jnp.concatenate([key_rows((ko, kp, ke), lanes), sink[:, lanes]], axis=0)
        values = jnp.concatenate(
            [key_rows((vo, vp, ve), lanes), sink[:, lanes_of(HEADS + head)]], axis=0
        )
        query = q[:, lanes]
        grad_prob = contract(grad_attn[:, lanes], values, ((1,), (1,)))
        row_delta = jnp.concatenate([delta[:, lanes]] * 6, axis=1)
        grad_score = (probs[head].astype(F32) * (grad_prob - row_delta)).astype(BF16)
        rows = contract(grad_score, keys, ((1,), (0,))) * HD ** (-0.5)
        grad_q[:, lanes] = rows
        product = rows * query.astype(F32)
        gain_sum[:, lanes] = jnp.sum(product, axis=0, keepdims=True)
        inner_q = inner_q + product
        grads = contract(grad_score, query, ((0,), (0,))) * HD ** (-0.5)
        inner_k = inner_k + grads * keys.astype(F32)
        own[:, lanes] = grads[: 2 * TOK]
        prev[:, lanes] = grads[2 * TOK : 4 * TOK].astype(BF16)
        early[:, lanes] = grads[4 * TOK : 5 * TOK].astype(BF16)
    for block in range(2):
        inner[block : block + 1] = lane_sums(inner_q[block * TOK : (block + 1) * TOK])
    for block in range(6):
        inner[block + 2 : block + 3] = lane_sums(inner_k[block * TOK : (block + 1) * TOK])


def pack_kernel(k_prev, k_early, inner, near, far):
    near[:, :HALF] = k_prev[...]
    far[:, :HALF] = k_early[...]
    lane = lax.broadcasted_iota(jnp.int32, (TOK, HD), 1)
    for block in range(3):
        tall = jnp.broadcast_to(inner[4 + block : 5 + block], (TOK, TOK)).T
        whole = tall.astype(BF16).astype(F32)
        both = jnp.where(lane == 0, whole, tall - whole).astype(BF16)
        if block < 2:
            near[block * TOK : (block + 1) * TOK, HALF:] = both
        else:
            far[:, HALF:] = both


def finish(grad, raw, rate, gains, inner):
    return (rate * gains * grad - raw.astype(F32) * (rate * rate * inner / D)).astype(BF16)


def query_kernel(grad, keep, got, tags, tags_got, gain_q, inner, mine, other):
    for half, (source, tag, out) in enumerate(((keep, tags, mine), (got, tags_got, other))):
        rows = slice(half * TOK, (half + 1) * TOK)
        rate = upright(lax.rsqrt(tag[0:1] / D + EPSILON))
        sums = upright(inner[half : half + 1])
        out[...] = finish(grad[rows], source[0], rate, gain_q[...], sums)


def key_kernel(
    place, k_own, v_own, near, far, v_near, v_far, s0, s1, s2, s3, inner, sink_inner, chan,
    keep, got, tags, tags_got, gain_k, mine, other,
):
    sunk = jnp.concatenate([ref[...].astype(F32) for ref in (s0, s1, s2, s3)], axis=0)
    core = place[0] % 2
    scale = chan[...] + EPSILON
    for half, (source, tag, out) in enumerate(((keep, tags, mine), (got, tags_got, other))):
        rows = slice(half * TOK, (half + 1) * TOK)
        use_far = jnp.where((core + half) == 1, 1.0, 0.0)
        use_sink = jnp.where(place[0] < 2, 1.0, 0.0) * (1.0 - use_far)
        rate = upright(lax.rsqrt(tag[1:2] / D + EPSILON))
        grad = k_own[rows] + near[rows, :HALF].astype(F32)
        grad = grad + use_far * far[:, :HALF].astype(F32) + use_sink * sunk[:, :HALF]
        sums = upright(inner[2 + half : 3 + half] + use_sink * sink_inner[...])
        extra = near[rows, HALF:].astype(F32) + use_far * far[:, HALF:].astype(F32)
        sums = sums + extra[:, 0:1] + extra[:, 1:2]
        out[0] = finish(grad, source[1], rate, gain_k[...], sums)
        grad = v_own[rows] + v_near[rows].astype(F32)
        grad = grad + use_far * v_far[...].astype(F32) + use_sink * sunk[:, HALF:]
        out[1] = (grad / scale).astype(BF16)


def shape(*dims, kind=F32):
    return jax.ShapeDtypeStruct(dims, kind)


def call(kernel, outs, flops=0, moved=2 * 1024 * 1024, exps=0, scalar=False, args=0):
    more = {}
    if scalar:
        more["in_specs"] = [pl.BlockSpec(memory_space=pltpu.SMEM)] + [
            pl.BlockSpec(memory_space=pltpu.VMEM)
        ] * args
    return pl.pallas_call(
        kernel,
        out_shape=outs,
        compiler_params=pltpu.CompilerParams(vmem_limit_bytes=48 * 1024 * 1024),
        cost_estimate=pl.CostEstimate(flops=flops, bytes_accessed=moved, transcendentals=exps),
        **more,
    )


def per_device(q_raw, k_raw, v_in, gain_q, gain_k, frame_index, reach, cotangent):
    place = lax.axis_index("frame")
    places = place.reshape(1)
    core = place % 2
    first = core == 0
    root = place < 2
    block_flops = 2 * 2 * TOK * KEYS * HALF
    low_half = lambda rows: shape(rows, HALF, kind=BF16)
    sums = call(sums_kernel, shape(2, TOK), moved=700000)(q_raw, k_raw)
    totals = sum_heads(sums)
    keep, send = call(
        split_kernel, (shape(4, TOK, HALF, kind=BF16),) * 2, scalar=True, args=4
    )(core.reshape(1), q_raw, k_raw, v_in, cotangent)
    got = other_core(send)
    second_group = lambda both: jnp.where(first, both[TOK:], both[:TOK])
    v2 = jnp.concatenate([keep[2], got[2]], axis=0)
    v_prev = move_chips(v2, line_shift(1))
    v_early = move_chips(second_group(v_prev), line_shift(1))
    tags = jnp.concatenate(
        [totals, frame_index.astype(F32)[None], jnp.broadcast_to(reach.astype(F32), (1, TOK))]
    )
    tags_got = other_core(tags)
    pick = lambda value: jnp.where(first, value[:HALF], value[HALF:])[None, :]
    gains_q, gains_k = pick(gain_q), pick(gain_k)
    quarter = shape(QUARTER, 2 * HALF, kind=BF16)
    q_norm, k_norm, bias, *quarters = call(
        norm_kernel,
        (low_half(2 * TOK), low_half(2 * TOK), shape(2 * TOK, KEYS)) + (quarter,) * XS,
        scalar=True,
        args=6,
    )(places, keep, got, tags, tags_got, gains_q, gains_k)
    k_prev_in = move_chips(k_norm, line_shift(1))
    k_early_in = move_chips(second_group(k_prev_in), line_shift(1))
    parts = spread_sink(quarters, root)
    blocks = (k_norm, k_prev_in, k_early_in, v2, v_prev, v_early)

    attn, top, probs, sink = call(
        forward_kernel,
        (
            low_half(2 * TOK),
            shape(1, HALF),
            shape(HEADS, 2 * TOK, KEYS, kind=BF16),
            shape(TOK, 2 * HALF, kind=BF16),
        ),
        2 * block_flops,
        6 * 1024 * 1024,
        HEADS * 2 * TOK * KEYS,
        scalar=True,
        args=12,
    )(places, bias, q_norm, *blocks, *parts)

    pair = pairs_z(top, jnp.maximum)
    v_own, v_prev_out, v_early_out, v_low = call(
        value_kernel,
        (shape(2 * TOK, HALF), low_half(2 * TOK), low_half(TOK), low_half(TOK)),
        block_flops,
        4 * 1024 * 1024,
    )(probs, keep, got)
    pair, v_low, v_prev_out, v_early_out = after((pair, v_low, v_prev_out, v_early_out))
    v_near = move_chips(v_prev_out, line_shift(-1))
    v_far = move_chips(v_early_out, line_shift(-2))
    quad = quads_z(pair, jnp.maximum)
    chan = quads_x(quad, jnp.maximum)
    chan, v_near, v_far = after((chan, v_near, v_far))

    *pieces, grad_attn, delta, scaled = pl.pallas_call(
        sink_kernel,
        out_shape=(quarter,) * XS
        + (low_half(2 * TOK), shape(2 * TOK, HALF), low_half(2 * TOK)),
        in_specs=[pl.BlockSpec(memory_space=pltpu.SMEM)]
        + [pl.BlockSpec(memory_space=pltpu.VMEM)] * 8,
        scratch_shapes=[pltpu.VMEM((TOK, HALF), F32)],
        compiler_params=pltpu.CompilerParams(vmem_limit_bytes=48 * 1024 * 1024),
        cost_estimate=pl.CostEstimate(
            flops=block_flops // 3, bytes_accessed=4 * 1024 * 1024, transcendentals=0
        ),
    )(places, probs, keep, got, attn, chan, q_norm, sink, v_low)
    total = pieces[0].astype(F32)
    for by in (1, 2, 3):
        total = total + shift_x(pieces[by], by).astype(F32)
    grad_qn, k_own, k_prev, k_early, gain_sum, inner = call(
        backward_kernel,
        (
            shape(2 * TOK, HALF),
            shape(2 * TOK, HALF),
            low_half(2 * TOK),
            low_half(TOK),
            shape(1, HALF),
            shape(8, TOK),
        ),
        3 * block_flops,
        8 * 1024 * 1024,
    )(probs, grad_attn, delta, q_norm, *blocks, sink)
    inner_got = other_core(inner)
    inner = inner + inner_got[jnp.array([1, 0, 3, 2, 5, 4, 6, 7])]

    inner, total = after((inner, total))
    total = gather_z(total, 0)
    inner = sum_heads(inner)
    near, far = call(
        pack_kernel, (shape(2 * TOK, HALF + HD, kind=BF16), shape(TOK, HALF + HD, kind=BF16))
    )(k_prev, k_early, inner)
    sums = jnp.concatenate([gain_sum.reshape(HEADS, HD), inner[7:8]])

    sums, total, near, far = after((sums, total, near, far))
    near_got = move_chips(near, line_shift(-1))
    total = gather_z(total, 1)
    sums = pairs_z(sums, jnp.add)
    sums, total, far = after((sums, total, far))
    far_got = move_chips(far, line_shift(-2))
    low = total.astype(BF16)
    sunk = [total] + [move_chips(low, pairs_of(turn)) for turn in GATHER_X]
    sums = quads_z(sums, jnp.add)
    sums, sunk, near_got, far_got = after((sums, sunk, near_got, far_got))
    sums = quads_x(sums, jnp.add)

    q_mine, q_other = call(query_kernel, (low_half(TOK), low_half(TOK)))(
        grad_qn, keep, got, tags, tags_got, gains_q, inner
    )
    both = shape(2, TOK, HALF, kind=BF16)
    mine, other = call(key_kernel, (both, both), scalar=True, args=18)(
        places, k_own, v_own, near_got, far_got, v_near, v_far, *sunk, inner, sums[HEADS:], chan,
        keep, got, tags, tags_got, gains_k,
    )

    def cores_out(mine, other):
        theirs = other_core(other)
        return jnp.where(
            first,
            jnp.concatenate([mine, theirs], axis=-1),
            jnp.concatenate([theirs, mine], axis=-1),
        )

    scaled_out = cores_out(scaled[:TOK], scaled[TOK:])
    grad_q = cores_out(q_mine, q_other)
    theirs = other_core(other)
    join = lambda a, b: jnp.where(
        first, jnp.concatenate([a, b], axis=1), jnp.concatenate([b, a], axis=1)
    )
    grad_k = join(mine[0], theirs[0])
    grad_v = join(mine[1], theirs[1])
    gain_total = sums[:HEADS].reshape(1, HALF)
    gain_both = cores_out(gain_total, gain_total)[0]
    return (scaled_out, grad_q, grad_k, grad_v, gain_both / gain_q, gain_both / gain_k)


def solution(mesh):
    rows = P("frame", "head")
    placed = (rows, rows, rows, P("head"), P("head"), P("frame"), P("frame"), rows)
    return jax.shard_map(
        per_device,
        mesh=mesh,
        in_specs=placed,
        out_specs=(rows, rows, rows, rows, P("head"), P("head")),
        check_vma=False,
    )
```

time: 852 us -> 173 us (0.20)
  blocking collectives: 391 us -> 0 us
  waiting for transfers between devices: 353 us -> 35.5 us
  starting transfers between devices: 20.6 us -> 103 us
  matrix products: 35.7 us -> 0 us
  between operations: 15.3 us -> 1.96 us
  Pallas kernels: 0 us -> 10.9 us
  local copies, waits for them, and re-layouts: 20.4 us -> 11.7 us
    psum x2 -> x0, waiting for transfers between devices: 329 us -> none  [the longest x1 178 us: spread(): return lax.psum(block, axis)]
    psum x3 -> x0, blocking collectives: 264 us -> none  [the longest x1 246 us: per_device(): lax.psum((jnp.sum(grad_qn * q_vals * rate_q[:, None], axis=0), jnp.sum(gr...]
    pmax x1 -> x0, blocking collectives: 127 us -> none  [per_device(): chan_max = lax.pmax(local_max, 'frame')]
    ppermute x6 -> x55, starting transfers between devices: 20.5 us -> 103 us  [the longest x42 77.7 us: move_chips(): return lax.ppermute(value, 'frame', chip_pairs(move))]
    dot_general x45 -> x0, matrix products: 35.7 us -> none  [the longest x10 12.1 us: head_forward(): jnp.einsum('td,bsd->bts', query_head, key_head, preferred_element_type=jn...]
    ppermute x6 -> x55, waiting for transfers between devices: 24.1 us -> 35.5 us  [the longest x42 33.3 us: move_chips(): return lax.ppermute(value, 'frame', chip_pairs(move))]
    pallas_call x0 -> x10, Pallas kernels: none -> 10.9 us  [the longest x1 4.31 us: per_device(): call(backward_kernel, (shape(2 * TOK, HALF), shape(2 * TOK, HALF), low_ha...]
  transfers between devices with their start and end apart: 8 -> 55, of which waited for: 4 -> 17; matrix products, arithmetic and copies ran while one was open for 2% -> 5% of each run, Pallas kernels for 0% -> 4%
where the time goes in v1:
time: 173 us; the launch traced here: 172 us
  starting transfers between devices  103 us (60%)
  waiting for transfers between devices  35.5 us (21%)
  local copies, waits for them, and re-layouts  11.7 us (7%)
  Pallas kernels  10.9 us (6%)
  other arithmetic  9.11 us (5%)
  between operations  1.96 us (1%)
    ppermute x42, starting transfers between devices, move_chips(): return lax.ppermute(value, 'frame', chip_pairs(move))  77.7 us
    ppermute x42, waiting for transfers between devices, move_chips(): return lax.ppermute(value, 'frame', chip_pairs(move))  33.3 us
    ppermute x7, starting transfers between devices, other_core(): lax.ppermute(value, 'frame', [(i, i ^ 1) for i in range(2 * XS * ZS)])  16 us
    unnamed x42, local copies, waits for them, and re-layouts  9.18 us
    ppermute x6, starting transfers between devices, sum_heads(): lax.ppermute(value, 'head', [(i, (i + by) % 4) for i in range(4)])  9.13 us
    pallas_call x1, Pallas kernels, per_device(): call(backward_kernel, (shape(2 * TOK, HALF), shape(2 * TOK, HALF), low_ha...  4.31 us
  transfers between devices with their start and end apart: 55, of which 17 were waited for; matrix products, arithmetic and copies ran while one was open for 5% of the time, Pallas kernels for 4%

profile of v1, /device:TPU:1, one launch (start us, length us, event | category | flops | bytes accessed | tf_op | source)
XLA Modules:
  0.0 172.0 jit_solution(6878687316994716927)
XLA Ops:
  3.0 3.8 %collective-permute-start.1 = (f32[2,128]{1,0:T(2,128)S(1)}, f32[2,128]{1,0:T(2,128)S(1)}, u32[]{:S(2)}, u32[]{:S(2)}) collective-permute-start(f32[2,128]{1,0:T(2,128)S(1)} %shard_map.137), channel_id=1, source_target_pairs={{0,2},{1,3},{2,0},{3,1},{4,6},{5,7},{6,4},{7,5},{8,10},{9,11},{10,... | collective-permute-start | bytes 3080 | tf_op jit(solution)/shard_map/ppermute | solution.py:63
  7.2 2.3 %collective-permute-start.3 = (f32[2,128]{1,0:T(2,128)S(1)}, f32[2,128]{1,0:T(2,128)S(1)}, u32[]{:S(2)}, u32[]{:S(2)}) collective-permute-start(f32[2,128]{1,0:T(2,128)S(1)} %shard_map.137), channel_id=1, source_target_pairs={{0,3},{1,0},{2,1},{3,2},{4,7},{5,4},{6,5},{7,6},{8,11},{9,8},{10,9... | collective-permute-start | bytes 3080 | tf_op jit(solution)/shard_map/ppermute | solution.py:63
  17.6 4.7 %collective-permute-start.10 = (bf16[32,1280]{1,0:T(8,128)(2,1)S(1)}, bf16[32,1280]{1,0:T(8,128)(2,1)S(1)}, u32[]{:S(2)}, u32[]{:S(2)}) collective-permute-start(bf16[32,1280]{1,0:T(8,128)(2,1)S(1)} %get-tuple-element.72), channel_id=1, source_target_pairs={{0,128},{4,132},{1,129},{5,133},{2,130},{6,134},{3,131},{7,135}} | collective-permute-start | bytes 245768 | tf_op jit(solution)/shard_map/ppermute | solution.py:35
  33.2 7.1 %collective-permute-start.15 = (bf16[32,1280]{1,0:T(8,128)(2,1)S(1)}, bf16[32,1280]{1,0:T(8,128)(2,1)S(1)}, u32[]{:S(2)}, u32[]{:S(2)}) collective-permute-start(bf16[32,1280]{1,0:T(8,128)(2,1)S(1)} %add_add_fusion.1), channel_id=1, source_target_pairs={{0,56},{4,60},{24,16},{28,20},{64,120},{68,124},{88,80},{92,84},{1... | collective-permute-start | bytes 245768 | tf_op jit(solution)/shard_map/ppermute | solution.py:35
  41.6 2.2 %collective-permute-done.5.kp = bf16[256,640]{1,0:T(8,128)(2,1)S(1)} collective-permute-done((bf16[256,640]{1,0:T(8,128)(2,1)S(1)}, bf16[256,640]{1,0:T(8,128)(2,1)S(1)}, u32[]{:S(2)}, u32[]{:S(2)}) %collective-permute-start.5) | collective-permute-done | bytes 327712 | tf_op jit(solution)/shard_map/ppermute | solution.py:35
  43.9 4.1 %collective-permute-start.6 = (bf16[128,640]{1,0:T(8,128)(2,1)S(1)}, bf16[128,640]{1,0:T(8,128)(2,1)S(1)}, u32[]{:S(2)}, u32[]{:S(2)}) collective-permute-start(bf16[128,640]{1,0:T(8,128)(2,1)S(1)} %slice_select_fusion.1), channel_id=1, source_target_pairs={{0,8},{4,12},{8,16},{12,20},{16,24},{20,28},{24,32},{28,36},{32,40... | collective-permute-start | bytes 491528 | tf_op jit(solution)/shard_map/ppermute | solution.py:35
  48.1 4.7 %collective-permute-start.16 = (bf16[32,1280]{1,0:T(8,128)(2,1)S(1)}, bf16[32,1280]{1,0:T(8,128)(2,1)S(1)}, u32[]{:S(2)}, u32[]{:S(2)}) collective-permute-start(bf16[32,1280]{1,0:T(8,128)(2,1)S(1)} %add_add_fusion.s0), channel_id=1, source_target_pairs={{0,64},{4,68},{8,72},{12,76},{16,80},{20,84},{24,88},{28,92},{32,9... | collective-permute-start | bytes 245768 | tf_op jit(solution)/shard_map/ppermute | solution.py:35
  55.6 4.4 %collective-permute-done.17.s2 = bf16[32,1280]{1,0:T(8,128)(2,1)S(1)} collective-permute-done((bf16[32,1280]{1,0:T(8,128)(2,1)S(1)}, bf16[32,1280]{1,0:T(8,128)(2,1)S(1)}, u32[]{:S(2)}, u32[]{:S(2)}) %collective-permute-start.17) | collective-permute-done | bytes 81952 | tf_op jit(solution)/shard_map/ppermute | solution.py:35
  60.0 2.4 %shard_map.139 = (bf16[256,640]{1,0:T(8,128)(2,1)S(1)}, f32[1,640]{1,0:T(1,128)S(1)}, bf16[5,256,768]{2,1,0:T(8,128)(2,1)S(1)}, bf16[128,1280]{1,0:T(8,128)(2,1)S(1)}) custom-call(s32[1]{0:T(128)} %bitcast.place, f32[256,768]{1,0:T(8,128)S(1)} %get-tuple-element.67.bias, bf16[256,640]{1,0:T(8,128)(2,1)S(1)} %get-tuple-element.68.q, ...), custom_call_target="tpu_custom_call" | custom-call | flops 503316480 | bytes 6291456 | tf_op jit(solution)/shard_map/pallas_call | solution.py:405
  65.0 2.9 %collective-permute-start.21 = (f32[1,640]{1,0:T(1,128)S(1)}, f32[1,640]{1,0:T(1,128)S(1)}, u32[]{:S(2)}, u32[]{:S(2)}) collective-permute-start(f32[1,640]{1,0:T(1,128)S(1)} %max.21), channel_id=1, source_target_pairs={{0,16},{4,20},{8,24},{12,28},{16,32},{20,36},{24,40},{28,44},{32,4... | collective-permute-start | bytes 7688 | tf_op jit(solution)/shard_map/ppermute | solution.py:35
  77.1 10.0 %collective-permute-done.27.v_far = bf16[128,640]{1,0:T(8,128)(2,1)S(1)} collective-permute-done((bf16[128,640]{1,0:T(8,128)(2,1)S(1)}, bf16[128,640]{1,0:T(8,128)(2,1)S(1)}, u32[]{:S(2)}, u32[]{:S(2)}) %collective-permute-start.27) | collective-permute-done | bytes 163872 | tf_op jit(solution)/shard_map/ppermute | solution.py:35
  89.5 1.9 %collective-permute-start.32 = (bf16[32,1280]{1,0:T(8,128)(2,1)}, bf16[32,1280]{1,0:T(8,128)(2,1)}, u32[]{:S(2)}, u32[]{:S(2)}) collective-permute-start(bf16[32,1280]{1,0:T(8,128)(2,1)} %get-tuple-element.94), channel_id=1, source_target_pairs={{0,192},{4,196},{8,200},{12,204},{16,208},{20,212},{24,216},{28,22... | collective-permute-start | bytes 245768 | tf_op jit(solution)/shard_map/ppermute | solution.py:35
  91.4 4.3 %shard_map.142 = (f32[256,640]{1,0:T(8,128)S(1)}, f32[256,640]{1,0:T(8,128)S(1)}, bf16[256,640]{1,0:T(8,128)(2,1)S(1)}, bf16[128,640]{1,0:T(8,128)(2,1)S(1)}, f3...) custom-call(bf16[5,256,768]{2,1,0:T(8,128)(2,1)} %copy-done, bf16[256,640]{1,0:T(8,128)(2,1)S(1)} %get-tuple-element.87.grad_attn, ...), custom_call_target="tpu_custom_call" | custom-call | flops 754974720 | bytes 8388608 | tf_op jit(solution)/shard_map/pallas_call | solution.py:449
  97.1 7.7 %collective-permute-start.29 = (f32[8,128]{1,0:T(8,128)S(1)}, f32[8,128]{1,0:T(8,128)S(1)}, u32[]{:S(2)}, u32[]{:S(2)}) collective-permute-start(f32[8,128]{1,0:T(8,128)S(1)} %get-tuple-element.90), channel_id=1, source_target_pairs={{0,4},{4,0},{8,12},{12,8},{16,20},{20,16},{24,28},{28,24},{32,36},... | collective-permute-start | bytes 12296 | tf_op jit(solution)/shard_map/ppermute | solution.py:59
  109.6 2.4 %collective-permute-start.35 = (f32[8,128]{1,0:T(8,128)S(1)}, f32[8,128]{1,0:T(8,128)}, u32[]{:S(2)}, u32[]{:S(2)}) collective-permute-start(f32[8,128]{1,0:T(8,128)S(1)} %add.103), channel_id=1, source_target_pairs={{0,3},{1,0},{2,1},{3,2},{4,7},{5,4},{6,5},{7,6},{8,11},{9,8},{10,9... | collective-permute-start | bytes 12296 | tf_op jit(solution)/shard_map/ppermute | solution.py:63
  118.3 2.3 %collective-permute-done.38 = bf16[32,1280]{1,0:T(8,128)(2,1)S(1)} collective-permute-done((bf16[32,1280]{1,0:T(8,128)(2,1)S(1)}, bf16[32,1280]{1,0:T(8,128)(2,1)S(1)}, u32[]{:S(2)}, u32[]{:S(2)}) %collective-permute-start.38) | collective-permute-done | bytes 81952 | tf_op jit(solution)/shard_map/ppermute | solution.py:35
  125.3 2.4 %collective-permute-start.28 = (bf16[128,640]{1,0:T(8,128)(2,1)S(1)}, bf16[128,640]{1,0:T(8,128)(2,1)S(1)}, u32[]{:S(2)}, u32[]{:S(2)}) collective-permute-start(bf16[128,640]{1,0:T(8,128)(2,1)S(1)} %get-tuple-element.129), channel_id=1, source_target_pairs={{0,4},{4,0},{8,12},{12,8},{16,20},{20,16},{24,28},{28,24},{32,36},... | collective-permute-start | bytes 491528 | tf_op jit(solution)/shard_map/ppermute | solution.py:59
  131.1 5.8 %collective-permute-start.42 = (f32[6,128]{1,0:T(8,128)S(1)}, f32[6,128]{1,0:T(8,128)S(1)}, u32[]{:S(2)}, u32[]{:S(2)}) collective-permute-start(f32[6,128]{1,0:T(8,128)S(1)} %add.112), channel_id=1, source_target_pairs={{0,32},{4,36},{8,40},{12,44},{16,48},{20,52},{24,56},{28,60},{32,0... | collective-permute-start | bytes 9224 | tf_op jit(solution)/shard_map/ppermute | solution.py:35
  137.8 2.7 %collective-permute-start.44 = (f32[6,128]{1,0:T(8,128)S(1)}, f32[6,128]{1,0:T(8,128)S(1)}, u32[]{:S(2)}, u32[]{:S(2)}) collective-permute-start(f32[6,128]{1,0:T(8,128)S(1)} %add.112), channel_id=1, source_target_pairs={{0,48},{4,52},{8,56},{12,60},{16,0},{20,4},{24,8},{28,12},{32,16},... | collective-permute-start | bytes 9224 | tf_op jit(solution)/shard_map/ppermute | solution.py:35
  147.4 3.5 %collective-permute-done.46.s2 = bf16[32,1280]{1,0:T(8,128)(2,1)S(1)} collective-permute-done((bf16[32,1280]{1,0:T(8,128)(2,1)S(1)}, bf16[32,1280]{1,0:T(8,128)(2,1)S(1)}, u32[]{:S(2)}, u32[]{:S(2)}) %collective-permute-start.46) | collective-permute-done | bytes 81952 | tf_op jit(solution)/shard_map/ppermute | solution.py:35
  150.9 2.1 %collective-permute-done.47.s3 = bf16[32,1280]{1,0:T(8,128)(2,1)S(1)} collective-permute-done((bf16[32,1280]{1,0:T(8,128)(2,1)S(1)}, bf16[32,1280]{1,0:T(8,128)(2,1)S(1)}, u32[]{:S(2)}, u32[]{:S(2)}) %collective-permute-start.47) | collective-permute-done | bytes 81952 | tf_op jit(solution)/shard_map/ppermute | solution.py:35
  153.4 4.8 %collective-permute-start.50 = (f32[6,128]{1,0:T(8,128)S(1)}, f32[6,128]{1,0:T(8,128)S(1)}, u32[]{:S(2)}, u32[]{:S(2)}) collective-permute-start(f32[6,128]{1,0:T(8,128)S(1)} %add_add_fusion.4), channel_id=1, source_target_pairs={{0,128},{4,132},{8,136},{12,140},{16,144},{20,148},{24,152},{28,15... | collective-permute-start | bytes 9224 | tf_op jit(solution)/shard_map/ppermute | solution.py:35
  158.1 4.7 %collective-permute-start.51 = (f32[6,128]{1,0:T(8,128)S(1)}, f32[6,128]{1,0:T(8,128)S(1)}, u32[]{:S(2)}, u32[]{:S(2)}) collective-permute-start(f32[6,128]{1,0:T(8,128)S(1)} %add_add_fusion.4), channel_id=1, source_target_pairs={{0,64},{4,68},{8,72},{12,76},{16,80},{20,84},{24,88},{28,92},{32,9... | collective-permute-start | bytes 9224 | tf_op jit(solution)/shard_map/ppermute | solution.py:35
  165.3 3.3 %collective-permute-start.54 = (f32[1,640]{1,0:T(1,128)S(1)}, f32[1,640]{1,0:T(1,128)S(1)}, u32[]{:S(2)}, u32[]{:S(2)}) collective-permute-start(f32[1,640]{1,0:T(1,128)S(1)} %bitcast.27), channel_id=1, source_target_pairs={{0,4},{4,0},{8,12},{12,8},{16,20},{20,16},{24,28},{28,24},{32,36},... | collective-permute-start | bytes 7688 | tf_op jit(solution)/shard_map/ppermute | solution.py:59
  (182 shorter events, 73.7 us)
Async XLA Ops:
  3.0 12.8 %collective-permute-start.1 = (f32[2,128]{1,0:T(2,128)S(1)}, f32[2,128]{1,0:T(2,128)S(1)}, u32[]{:S(2)}, u32[]{:S(2)}) collective-permute-start(f32[2,128]{1,0:T(2,128)S(1)} %shard_map.137), channel_id=1, source_target_pairs={{0,2},{1,3},{2,0},{3,1},{4,6},{5,7},{6,4},{7,5},{8,10},{9,11},{10,... | collective-permute-start | bytes 3080 | tf_op jit(solution)/shard_map/ppermute | solution.py:63
  6.8 9.1 %collective-permute-start.2 = (f32[2,128]{1,0:T(2,128)S(1)}, f32[2,128]{1,0:T(2,128)S(1)}, u32[]{:S(2)}, u32[]{:S(2)}) collective-permute-start(f32[2,128]{1,0:T(2,128)S(1)} %shard_map.137), channel_id=1, source_target_pairs={{0,1},{1,2},{2,3},{3,0},{4,5},{5,6},{6,7},{7,4},{8,9},{9,10},{10,1... | collective-permute-start | bytes 3080 | tf_op jit(solution)/shard_map/ppermute | solution.py:63
  7.2 8.7 %collective-permute-start.3 = (f32[2,128]{1,0:T(2,128)S(1)}, f32[2,128]{1,0:T(2,128)S(1)}, u32[]{:S(2)}, u32[]{:S(2)}) collective-permute-start(f32[2,128]{1,0:T(2,128)S(1)} %shard_map.137), channel_id=1, source_target_pairs={{0,3},{1,0},{2,1},{3,2},{4,7},{5,4},{6,5},{7,6},{8,11},{9,8},{10,9... | collective-permute-start | bytes 3080 | tf_op jit(solution)/shard_map/ppermute | solution.py:63
  29.2 11.1 %collective-permute-start.7 = (bf16[256,640]{1,0:T(8,128)(2,1)S(1)}, bf16[256,640]{1,0:T(8,128)(2,1)S(1)}, u32[]{:S(2)}, u32[]{:S(2)}) collective-permute-start(bf16[256,640]{1,0:T(8,128)(2,1)S(1)} %pad_maximum_fusion.vo), channel_id=1, source_target_pairs={{0,8},{4,12},{8,16},{12,20},{16,24},{20,28},{24,32},{28,36},{32,40... | collective-permute-start | bytes 983048 | tf_op jit(solution)/shard_map/ppermute | solution.py:35
  30.5 13.3 %collective-permute-start.5 = (bf16[256,640]{1,0:T(8,128)(2,1)S(1)}, bf16[256,640]{1,0:T(8,128)(2,1)S(1)}, u32[]{:S(2)}, u32[]{:S(2)}) collective-permute-start(bf16[256,640]{1,0:T(8,128)(2,1)S(1)} %get-tuple-element.69.ko), channel_id=1, source_target_pairs={{0,8},{4,12},{8,16},{12,20},{16,24},{20,28},{24,32},{28,36},{32,40... | collective-permute-start | bytes 983048 | tf_op jit(solution)/shard_map/ppermute | solution.py:35
  31.9 16.1 %collective-permute-start.14 = (bf16[32,1280]{1,0:T(8,128)(2,1)S(1)}, bf16[32,1280]{1,0:T(8,128)(2,1)S(1)}, u32[]{:S(2)}, u32[]{:S(2)}) collective-permute-start(bf16[32,1280]{1,0:T(8,128)(2,1)S(1)} %add_add_fusion.1), channel_id=1, source_target_pairs={{0,8},{4,12},{24,32},{28,36},{40,48},{44,52},{64,72},{68,76},{88,9... | collective-permute-start | bytes 245768 | tf_op jit(solution)/shard_map/ppermute | solution.py:35
  33.2 14.8 %collective-permute-start.15 = (bf16[32,1280]{1,0:T(8,128)(2,1)S(1)}, bf16[32,1280]{1,0:T(8,128)(2,1)S(1)}, u32[]{:S(2)}, u32[]{:S(2)}) collective-permute-start(bf16[32,1280]{1,0:T(8,128)(2,1)S(1)} %add_add_fusion.1), channel_id=1, source_target_pairs={{0,56},{4,60},{24,16},{28,20},{64,120},{68,124},{88,80},{92,84},{1... | collective-permute-start | bytes 245768 | tf_op jit(solution)/shard_map/ppermute | solution.py:35
  40.3 19.7 %collective-permute-start.8 = (bf16[128,640]{1,0:T(8,128)(2,1)S(1)}, bf16[128,640]{1,0:T(8,128)(2,1)S(1)}, u32[]{:S(2)}, u32[]{:S(2)}) collective-permute-start(bf16[128,640]{1,0:T(8,128)(2,1)S(1)} %slice_select_fusion), channel_id=1, source_target_pairs={{0,8},{4,12},{8,16},{12,20},{16,24},{20,28},{24,32},{28,36},{32,40... | collective-permute-start | bytes 491528 | tf_op jit(solution)/shard_map/ppermute | solution.py:35
  43.9 16.1 %collective-permute-start.6 = (bf16[128,640]{1,0:T(8,128)(2,1)S(1)}, bf16[128,640]{1,0:T(8,128)(2,1)S(1)}, u32[]{:S(2)}, u32[]{:S(2)}) collective-permute-start(bf16[128,640]{1,0:T(8,128)(2,1)S(1)} %slice_select_fusion.1), channel_id=1, source_target_pairs={{0,8},{4,12},{8,16},{12,20},{16,24},{20,28},{24,32},{28,36},{32,40... | collective-permute-start | bytes 491528 | tf_op jit(solution)/shard_map/ppermute | solution.py:35
  48.1 7.5 %collective-permute-start.16 = (bf16[32,1280]{1,0:T(8,128)(2,1)S(1)}, bf16[32,1280]{1,0:T(8,128)(2,1)S(1)}, u32[]{:S(2)}, u32[]{:S(2)}) collective-permute-start(bf16[32,1280]{1,0:T(8,128)(2,1)S(1)} %add_add_fusion.s0), channel_id=1, source_target_pairs={{0,64},{4,68},{8,72},{12,76},{16,80},{20,84},{24,88},{28,92},{32,9... | collective-permute-start | bytes 245768 | tf_op jit(solution)/shard_map/ppermute | solution.py:35
  68.8 18.4 %collective-permute-start.26 = (bf16[256,640]{1,0:T(8,128)(2,1)S(1)}, bf16[256,640]{1,0:T(8,128)(2,1)S(1)}, u32[]{:S(2)}, u32[]{:S(2)}) collective-permute-start(bf16[256,640]{1,0:T(8,128)(2,1)S(1)} %get-tuple-element.81), channel_id=1, source_target_pairs={{8,0},{12,4},{16,8},{20,12},{24,16},{28,20},{32,24},{36,28},{40,32... | collective-permute-start | bytes 983048 | tf_op jit(solution)/shard_map/ppermute | solution.py:35
  75.8 11.4 %collective-permute-start.27 = (bf16[128,640]{1,0:T(8,128)(2,1)S(1)}, bf16[128,640]{1,0:T(8,128)(2,1)S(1)}, u32[]{:S(2)}, u32[]{:S(2)}) collective-permute-start(bf16[128,640]{1,0:T(8,128)(2,1)S(1)} %get-tuple-element.82), channel_id=1, source_target_pairs={{16,0},{20,4},{24,8},{28,12},{32,16},{36,20},{40,24},{44,28},{48,3... | collective-permute-start | bytes 491528 | tf_op jit(solution)/shard_map/ppermute | solution.py:35
  88.6 19.0 %collective-permute-start.30 = (bf16[32,1280]{1,0:T(8,128)(2,1)}, bf16[32,1280]{1,0:T(8,128)(2,1)}, u32[]{:S(2)}, u32[]{:S(2)}) collective-permute-start(bf16[32,1280]{1,0:T(8,128)(2,1)} %get-tuple-element.92), channel_id=1, source_target_pairs={{0,64},{4,68},{8,72},{12,76},{16,80},{20,84},{24,88},{28,92},{32,9... | collective-permute-start | bytes 245768 | tf_op jit(solution)/shard_map/ppermute | solution.py:35
  88.7 18.9 %collective-permute-start.31 = (bf16[32,1280]{1,0:T(8,128)(2,1)}, bf16[32,1280]{1,0:T(8,128)(2,1)}, u32[]{:S(2)}, u32[]{:S(2)}) collective-permute-start(bf16[32,1280]{1,0:T(8,128)(2,1)} %get-tuple-element.93), channel_id=1, source_target_pairs={{0,128},{4,132},{8,136},{12,140},{16,144},{20,148},{24,152},{28,15... | collective-permute-start | bytes 245768 | tf_op jit(solution)/shard_map/ppermute | solution.py:35
  89.5 18.1 %collective-permute-start.32 = (bf16[32,1280]{1,0:T(8,128)(2,1)}, bf16[32,1280]{1,0:T(8,128)(2,1)}, u32[]{:S(2)}, u32[]{:S(2)}) collective-permute-start(bf16[32,1280]{1,0:T(8,128)(2,1)} %get-tuple-element.94), channel_id=1, source_target_pairs={{0,192},{4,196},{8,200},{12,204},{16,208},{20,212},{24,216},{28,22... | collective-permute-start | bytes 245768 | tf_op jit(solution)/shard_map/ppermute | solution.py:35
  97.1 8.5 %collective-permute-start.29 = (f32[8,128]{1,0:T(8,128)S(1)}, f32[8,128]{1,0:T(8,128)S(1)}, u32[]{:S(2)}, u32[]{:S(2)}) collective-permute-start(f32[8,128]{1,0:T(8,128)S(1)} %get-tuple-element.90), channel_id=1, source_target_pairs={{0,4},{4,0},{8,12},{12,8},{16,20},{20,16},{24,28},{28,24},{32,36},... | collective-permute-start | bytes 12296 | tf_op jit(solution)/shard_map/ppermute | solution.py:59
  121.6 7.7 %collective-permute-start.40 = (bf16[32,1280]{1,0:T(8,128)(2,1)S(1)}, bf16[32,1280]{1,0:T(8,128)(2,1)S(1)}, u32[]{:S(2)}, u32[]{:S(2)}) collective-permute-start(bf16[32,1280]{1,0:T(8,128)(2,1)S(1)} %convert_element_type.51), channel_id=1, source_target_pairs={{24,0},{28,4},{88,64},{92,68},{152,128},{156,132},{216,192},{220,1... | collective-permute-start | bytes 245768 | tf_op jit(solution)/shard_map/ppermute | solution.py:35
  122.9 8.2 %collective-permute-start.41 = (bf16[32,1280]{1,0:T(8,128)(2,1)S(1)}, bf16[32,1280]{1,0:T(8,128)(2,1)S(1)}, u32[]{:S(2)}, u32[]{:S(2)}) collective-permute-start(bf16[32,1280]{1,0:T(8,128)(2,1)S(1)} %convert_element_type.51), channel_id=1, source_target_pairs={{40,0},{44,4},{104,64},{108,68},{168,128},{172,132},{232,192},{236... | collective-permute-start | bytes 245768 | tf_op jit(solution)/shard_map/ppermute | solution.py:35
  125.3 15.2 %collective-permute-start.28 = (bf16[128,640]{1,0:T(8,128)(2,1)S(1)}, bf16[128,640]{1,0:T(8,128)(2,1)S(1)}, u32[]{:S(2)}, u32[]{:S(2)}) collective-permute-start(bf16[128,640]{1,0:T(8,128)(2,1)S(1)} %get-tuple-element.129), channel_id=1, source_target_pairs={{0,4},{4,0},{8,12},{12,8},{16,20},{20,16},{24,28},{28,24},{32,36},... | collective-permute-start | bytes 491528 | tf_op jit(solution)/shard_map/ppermute | solution.py:59
  128.0 25.4 %collective-permute-start.48 = (bf16[256,768]{1,0:T(8,128)(2,1)S(1)}, bf16[256,768]{1,0:T(8,128)(2,1)S(1)}, u32[]{:S(2)}, u32[]{:S(2)}) collective-permute-start(bf16[256,768]{1,0:T(8,128)(2,1)S(1)} %get-tuple-element.111), channel_id=1, source_target_pairs={{8,0},{12,4},{16,8},{20,12},{24,16},{28,20},{32,24},{36,28},{40,32... | collective-permute-start | bytes 1179656 | tf_op jit(solution)/shard_map/ppermute | solution.py:35
  131.1 11.5 %collective-permute-start.42 = (f32[6,128]{1,0:T(8,128)S(1)}, f32[6,128]{1,0:T(8,128)S(1)}, u32[]{:S(2)}, u32[]{:S(2)}) collective-permute-start(f32[6,128]{1,0:T(8,128)S(1)} %add.112), channel_id=1, source_target_pairs={{0,32},{4,36},{8,40},{12,44},{16,48},{20,52},{24,56},{28,60},{32,0... | collective-permute-start | bytes 9224 | tf_op jit(solution)/shard_map/ppermute | solution.py:35
  142.6 20.2 %collective-permute-start.36 = (bf16[128,640]{1,0:T(8,128)(2,1)S(1)}, bf16[128,640]{1,0:T(8,128)(2,1)S(1)}, u32[]{:S(2)}, u32[]{:S(2)}) collective-permute-start(bf16[128,640]{1,0:T(8,128)(2,1)S(1)} %get-tuple-element.97), channel_id=1, source_target_pairs={{0,4},{4,0},{8,12},{12,8},{16,20},{20,16},{24,28},{28,24},{32,36},... | collective-permute-start | bytes 491528 | tf_op jit(solution)/shard_map/ppermute | solution.py:59
  144.8 8.3 %collective-permute-start.47 = (bf16[32,1280]{1,0:T(8,128)(2,1)S(1)}, bf16[32,1280]{1,0:T(8,128)(2,1)S(1)}, u32[]{:S(2)}, u32[]{:S(2)}) collective-permute-start(bf16[32,1280]{1,0:T(8,128)(2,1)S(1)} %convert_element_type.54), channel_id=1, source_target_pairs={{192,0},{196,4},{193,1},{197,5},{194,2},{198,6},{195,3},{199,7}} | collective-permute-start | bytes 245768 | tf_op jit(solution)/shard_map/ppermute | solution.py:35
  153.4 10.3 %collective-permute-start.50 = (f32[6,128]{1,0:T(8,128)S(1)}, f32[6,128]{1,0:T(8,128)S(1)}, u32[]{:S(2)}, u32[]{:S(2)}) collective-permute-start(f32[6,128]{1,0:T(8,128)S(1)} %add_add_fusion.4), channel_id=1, source_target_pairs={{0,128},{4,132},{8,136},{12,140},{16,144},{20,148},{24,152},{28,15... | collective-permute-start | bytes 9224 | tf_op jit(solution)/shard_map/ppermute | solution.py:35
  (51 other events, 293.3 us)

commit v2 on v1

--- a/solution.py
+++ b/solution.py
@@ -14,6 +14,7 @@
 HEADS = HALF // HD
 KEYS = 6 * TOK
 QUARTER = TOK // XS
+CUTS = 2
 EPSILON = 1e-06
 HIDDEN = -1e30
 F32 = jnp.float32
@@ -59,8 +60,12 @@
     return lax.ppermute(value, "frame", [(i, i ^ 1) for i in range(2 * XS * ZS)])
 
 
+def head_turns(value):
+    return [lax.ppermute(value, "head", [(i, (i + by) % 4) for i in range(4)]) for by in (2, 1, 3)]
+
+
 def sum_heads(value):
-    turns = [lax.ppermute(value, "head", [(i, (i + by) % 4) for i in range(4)]) for by in (2, 1, 3)]
+    turns = head_turns(value)
     return (value + turns[0]) + (turns[1] + turns[2])
 
 
@@ -77,31 +82,28 @@
 
 
 SCATTER_X = tuple(row(0, to, (0,)) for to in range(1, XS))
-GATHER_X = tuple(row(src, 0, (0,)) for src in range(1, XS))
+GATHER_X = tuple(row(src, 0, range(ZS)) for src in (2, 1, 3))
 SPREAD_Z = (
-    (column({0: 3}, range(XS)), column({0: 5}, range(XS))),
-    (column({0: 1, 3: 4, 5: 6}, range(XS)), column({0: 7, 3: 2}, range(XS))),
+    (column({0: 5}, range(XS)), column({0: 6}, range(XS))),
+    (column({0: 7, 5: 3, 6: 4}, range(XS)), column({0: 1, 5: 2}, range(XS))),
 )
 GATHER_Z = (
-    (column({1: 0, 4: 3, 6: 5}, range(XS)), column({7: 0, 2: 3}, range(XS))),
-    (column({3: 0}, range(XS)), column({5: 0}, range(XS))),
+    (column({1: 0, 4: 3, 6: 5}, (0,)), column({7: 0, 2: 3}, (0,))),
+    (column({3: 0}, (0,)), column({5: 0}, (0,))),
 )
 
 
-def spread_sink(quarters, root):
-    total = jnp.where(root, quarters[0], jnp.zeros_like(quarters[0]))
-    for quarter, turn in zip(quarters[1:], SCATTER_X):
-        total = total + move_chips(quarter, pairs_of(turn))
-    for turns in SPREAD_Z:
-        got = [move_chips(total, pairs_of(turn)) for turn in turns]
-        total = total + got[0] + got[1]
-    return [total] + [shift_x(total, by) for by in (1, 2, 3)]
-
-
-def gather_z(total, index):
-    low = total.astype(BF16)
-    got = [move_chips(low, pairs_of(turn)) for turn in GATHER_Z[index]]
-    return total + got[0].astype(F32) + got[1].astype(F32)
+def add_parts(*parts, moved=0):
+    first = parts[0]
+    return call(
+        add_kernel,
+        jax.ShapeDtypeStruct(first.shape, BF16),
+        moved=moved or 2 * (len(parts) + 1) * first.size,
+    )(*parts)
+
+
+def rounds(turns, low):
+    return [move_chips(low, pairs_of(turn)) for turn in turns]
 
 
 def after(values, *others):
@@ -142,18 +144,34 @@
     return total
 
 
-def sums_kernel(q, k, sums):
-    for row, ref in enumerate((q, k)):
-        values = ref[...].astype(F32)
-        sums[row : row + 1] = lane_sums(fold(values * values))
-
-
-def split_kernel(core, q, k, v, c, keep, send):
+def entry_kernel(core, q, k, v, c, keep, send, sums, held, sems):
+    step = TOK // CUTS
+    copies = []
+    for index, ref in enumerate((q, k, v, c)):
+        for cut in range(CUTS):
+            rows = pl.ds(cut * step, step)
+            copies.append(
+                pltpu.make_async_copy(ref.at[rows], held.at[index, rows], sems.at[index, cut])
+            )
+    for copy in copies:
+        copy.start()
     mine = pl.ds(pl.multiple_of(core[0] * HALF, HD), HALF)
     other = pl.ds(pl.multiple_of((1 - core[0]) * HALF, HD), HALF)
-    for index, ref in enumerate((q, k, v, c)):
-        keep[index] = ref[:, mine]
-        send[index] = ref[:, other]
+    for index in range(4):
+        for copy in copies[index * CUTS : (index + 1) * CUTS]:
+            copy.wait()
+        keep[index] = held[index, :, mine]
+        send[index] = held[index, :, other]
+        if index < 2:
+            values = held[index].astype(F32)
+            sums[index : index + 1] = lane_sums(fold(values * values))
+
+
+def add_kernel(*refs):
+    value = refs[0][...].astype(F32)
+    for part in refs[1:-1]:
+        value = value + part[...].astype(F32)
+    refs[-1][...] = value.astype(BF16)
 
 
 def norm_kernel(place, keep, got, tags, tags_got, gain_q, gain_k, q_norm, k_norm, bias, *quarters):
@@ -167,8 +185,9 @@
 
     def fill(source, start):
         for index, quarter in enumerate(quarters):
-            quarter[:, :HALF] = k_norm[start + index * QUARTER : start + (index + 1) * QUARTER]
-            quarter[:, HALF:] = source[2, index * QUARTER : (index + 1) * QUARTER]
+            rows = slice(index * QUARTER, (index + 1) * QUARTER)
+            quarter[:, :HALF] = k_norm[start + rows.start : start + rows.stop]
+            quarter[:, HALF:] = source[2, rows]
 
     @pl.when(core == 0)
     def _():
@@ -177,6 +196,10 @@
     @pl.when(core == 1)
     def _():
         fill(got, TOK)
+
+    @pl.when(place[0] >= 2)
+    def _():
+        quarters[0][...] = jnp.zeros((QUARTER, 2 * HALF), BF16)
 
     chip = place[0] // 2
     groups = (place[0], place[0] + 1 - 2 * core)
@@ -216,7 +239,7 @@
         sink[pl.ds(start, QUARTER)] = part[...]
     for head in range(HEADS):
         lanes = lanes_of(head)
-        keys = jnp.concatenate([key_rows((ko, kp, ke), lanes), sink[:, lanes]], axis=0)
+        keys = key_rows((ko, kp, ke, sink), lanes)
         values = jnp.concatenate(
             [key_rows((vo, vp, ve), lanes), sink[:, lanes_of(HEADS + head)]], axis=0
         )
@@ -243,35 +266,12 @@
         sink[:, lanes] = grads[5 * TOK :].astype(BF16)
 
 
-def sink_kernel(
-    place, probs, keep, got, attn, chan, q, sink, v_low, p0, p1, p2, p3, grad_attn, delta, scaled, rows
-):
-    for head in range(HEADS):
-        lanes = lanes_of(head)
-        scale = chan[:, lanes] + EPSILON
-        cot = jnp.concatenate([keep[3, :, lanes], got[3, :, lanes]], axis=0).astype(F32)
-        grads = (cot / scale).astype(BF16)
-        grad_attn[:, lanes] = grads
-        out = attn[:, lanes].astype(F32)
-        scaled[:, lanes] = (out / scale).astype(BF16)
-        sums = jnp.sum(grads.astype(F32) * out, axis=1, keepdims=True)
-        delta[:, lanes] = jnp.broadcast_to(sums, (2 * TOK, HD))
-        grad_prob = contract(grads, sink[:, lanes_of(HEADS + head)], ((1,), (1,)))
-        grad_score = (probs[head, :, 5 * TOK :].astype(F32) * (grad_prob - sums)).astype(BF16)
-        rows[:, lanes] = contract(grad_score, q[:, lanes], ((0,), (0,))) * HD ** (-0.5)
-    x = place[0] // (2 * ZS)
-    for by, part in enumerate((p0, p1, p2, p3)):
-        take = pl.ds(pl.multiple_of(((x + by) % XS) * QUARTER, QUARTER), QUARTER)
-        part[:, :HALF] = rows[take].astype(BF16)
-        part[:, HALF:] = v_low[take]
-
-
 def backward_kernel(
-    probs, grad_attn, delta, q, ko, kp, ke, vo, vp, ve, sink,
-    grad_q, own, prev, early, gain_sum, inner,
+    probs, keep, got, attn, chan, q, ko, kp, ke, vo, vp, ve, sink, v_low, v_early,
+    low, grad_q, own, prev, early, scaled, gain_sum, inner,
 ):
     inner_q = jnp.zeros((2 * TOK, HD), F32)
-    inner_k = jnp.zeros((KEYS, HD), F32)
+    inner_sink = jnp.zeros((TOK, HD), F32)
     for head in range(HEADS):
         lanes = lanes_of(head)
         keys = jnp.concatenate([key_rows((ko, kp, ke), lanes), sink[:, lanes]], axis=0)
@@ -279,37 +279,53 @@
             [key_rows((vo, vp, ve), lanes), sink[:, lanes_of(HEADS + head)]], axis=0
         )
         query = q[:, lanes]
-        grad_prob = contract(grad_attn[:, lanes], values, ((1,), (1,)))
-        row_delta = jnp.concatenate([delta[:, lanes]] * 6, axis=1)
-        grad_score = (probs[head].astype(F32) * (grad_prob - row_delta)).astype(BF16)
+        scale = chan[:, lanes] + EPSILON
+        cot = jnp.concatenate([keep[3, :, lanes], got[3, :, lanes]], axis=0).astype(F32)
+        grad_attn = (cot / scale).astype(BF16)
+        out = attn[:, lanes].astype(F32)
+        scaled[:, lanes] = (out / scale).astype(BF16)
+        delta = jnp.sum(grad_attn.astype(F32) * out, axis=1, keepdims=True)
+        grad_prob = contract(grad_attn, values, ((1,), (1,)))
+        grad_score = (probs[head].astype(F32) * (grad_prob - delta)).astype(BF16)
         rows = contract(grad_score, keys, ((1,), (0,))) * HD ** (-0.5)
         grad_q[:, lanes] = rows
         product = rows * query.astype(F32)
         gain_sum[:, lanes] = jnp.sum(product, axis=0, keepdims=True)
         inner_q = inner_q + product
         grads = contract(grad_score, query, ((0,), (0,))) * HD ** (-0.5)
-        inner_k = inner_k + grads * keys.astype(F32)
+        inner_sink = inner_sink + grads[5 * TOK :] * keys[5 * TOK :].astype(F32)
         own[:, lanes] = grads[: 2 * TOK]
         prev[:, lanes] = grads[2 * TOK : 4 * TOK].astype(BF16)
         early[:, lanes] = grads[4 * TOK : 5 * TOK].astype(BF16)
-    for block in range(2):
-        inner[block : block + 1] = lane_sums(inner_q[block * TOK : (block + 1) * TOK])
-    for block in range(6):
-        inner[block + 2 : block + 3] = lane_sums(inner_k[block * TOK : (block + 1) * TOK])
-
-
-def pack_kernel(k_prev, k_early, inner, near, far):
-    near[:, :HALF] = k_prev[...]
-    far[:, :HALF] = k_early[...]
-    lane = lax.broadcasted_iota(jnp.int32, (TOK, HD), 1)
-    for block in range(3):
-        tall = jnp.broadcast_to(inner[4 + block : 5 + block], (TOK, TOK)).T
-        whole = tall.astype(BF16).astype(F32)
-        both = jnp.where(lane == 0, whole, tall - whole).astype(BF16)
-        if block < 2:
-            near[block * TOK : (block + 1) * TOK, HALF:] = both
-        else:
-            far[:, HALF:] = both
+        low[:, lanes] = grads[5 * TOK :].astype(BF16)
+    low[:, HALF:] = v_low[...]
+    early[:, HALF:] = v_early[...]
+    inner[0:1] = lane_sums(inner_q[:TOK])
+    inner[1:2] = lane_sums(inner_q[TOK:])
+    inner[2:3] = lane_sums(inner_sink)
+
+
+def key_sum_kernel(
+    place, own, near, far, k_norm, inner, p0, p1, p2, p3, total, low, mine, other
+):
+    core = place[0] % 2
+    rows = [inner[0:1], inner[1:2]]
+    for half in range(2):
+        part = slice(half * TOK, (half + 1) * TOK)
+        use_far = jnp.where((core + half) == 1, 1.0, 0.0)
+        grad = own[part] + near[part].astype(F32) + use_far * far[:, :HALF].astype(F32)
+        total[part] = grad
+        rows.append(lane_sums(fold(grad * k_norm[part].astype(F32))))
+    parts = (p0[...].astype(F32) + p1[...].astype(F32)) + (
+        p2[...].astype(F32) + p3[...].astype(F32)
+    )
+    low[...] = parts.astype(BF16)
+    rows.append(inner[2:3])
+    for row, there in enumerate((1, 0, 3, 2, 4)):
+        mine[row : row + 1] = rows[row]
+        other[there : there + 1] = rows[row]
+    mine[5:8] = jnp.zeros((3, TOK), F32)
+    other[5:8] = jnp.zeros((3, TOK), F32)
 
 
 def finish(grad, raw, rate, gains, inner):
@@ -325,10 +341,9 @@
 
 
 def key_kernel(
-    place, k_own, v_own, near, far, v_near, v_far, s0, s1, s2, s3, inner, sink_inner, chan,
+    place, k_total, v_own, v_near, far, sunk, inner, sink_inner, chan,
     keep, got, tags, tags_got, gain_k, mine, other,
 ):
-    sunk = jnp.concatenate([ref[...].astype(F32) for ref in (s0, s1, s2, s3)], axis=0)
     core = place[0] % 2
     scale = chan[...] + EPSILON
     for half, (source, tag, out) in enumerate(((keep, tags, mine), (got, tags_got, other))):
@@ -336,14 +351,11 @@
         use_far = jnp.where((core + half) == 1, 1.0, 0.0)
         use_sink = jnp.where(place[0] < 2, 1.0, 0.0) * (1.0 - use_far)
         rate = upright(lax.rsqrt(tag[1:2] / D + EPSILON))
-        grad = k_own[rows] + near[rows, :HALF].astype(F32)
-        grad = grad + use_far * far[:, :HALF].astype(F32) + use_sink * sunk[:, :HALF]
+        grad = k_total[rows] + use_sink * sunk[:, :HALF].astype(F32)
         sums = upright(inner[2 + half : 3 + half] + use_sink * sink_inner[...])
-        extra = near[rows, HALF:].astype(F32) + use_far * far[:, HALF:].astype(F32)
-        sums = sums + extra[:, 0:1] + extra[:, 1:2]
         out[0] = finish(grad, source[1], rate, gain_k[...], sums)
         grad = v_own[rows] + v_near[rows].astype(F32)
-        grad = grad + use_far * v_far[...].astype(F32) + use_sink * sunk[:, HALF:]
+        grad = grad + use_far * far[:, HALF:].astype(F32) + use_sink * sunk[:, HALF:].astype(F32)
         out[1] = (grad / scale).astype(BF16)
 
 
@@ -360,7 +372,7 @@
     return pl.pallas_call(
         kernel,
         out_shape=outs,
-        compiler_params=pltpu.CompilerParams(vmem_limit_bytes=48 * 1024 * 1024),
+        compiler_params=pltpu.CompilerParams(vmem_limit_bytes=20 * 1024 * 1024),
         cost_estimate=pl.CostEstimate(flops=flops, bytes_accessed=moved, transcendentals=exps),
         **more,
     )
@@ -374,16 +386,21 @@
     root = place < 2
     block_flops = 2 * 2 * TOK * KEYS * HALF
     low_half = lambda rows: shape(rows, HALF, kind=BF16)
-    sums = call(sums_kernel, shape(2, TOK), moved=700000)(q_raw, k_raw)
+    keep, send, sums = pl.pallas_call(
+        entry_kernel,
+        out_shape=(shape(4, TOK, HALF, kind=BF16),) * 2 + (shape(2, TOK),),
+        in_specs=[pl.BlockSpec(memory_space=pltpu.SMEM)] + [pl.BlockSpec(memory_space=pltpu.HBM)] * 4,
+        scratch_shapes=[
+            pltpu.VMEM((4, TOK, 2 * HALF), BF16),
+            pltpu.SemaphoreType.DMA((4, CUTS)),
+        ],
+        compiler_params=pltpu.CompilerParams(vmem_limit_bytes=62 * 1024 * 1024),
+    )(core.reshape(1), q_raw, k_raw, v_in, cotangent)
     totals = sum_heads(sums)
-    keep, send = call(
-        split_kernel, (shape(4, TOK, HALF, kind=BF16),) * 2, scalar=True, args=4
-    )(core.reshape(1), q_raw, k_raw, v_in, cotangent)
     got = other_core(send)
     second_group = lambda both: jnp.where(first, both[TOK:], both[:TOK])
     v2 = jnp.concatenate([keep[2], got[2]], axis=0)
     v_prev = move_chips(v2, line_shift(1))
-    v_early = move_chips(second_group(v_prev), line_shift(1))
     tags = jnp.concatenate(
         [totals, frame_index.astype(F32)[None], jnp.broadcast_to(reach.astype(F32), (1, TOK))]
     )
@@ -397,10 +414,19 @@
         scalar=True,
         args=6,
     )(places, keep, got, tags, tags_got, gains_q, gains_k)
-    k_prev_in = move_chips(k_norm, line_shift(1))
-    k_early_in = move_chips(second_group(k_prev_in), line_shift(1))
-    parts = spread_sink(quarters, root)
-    blocks = (k_norm, k_prev_in, k_early_in, v2, v_prev, v_early)
+    parts = [quarters[0]] + [
+        move_chips(part, pairs_of(turn)) for part, turn in zip(quarters[1:], SCATTER_X)
+    ]
+    low, k_sent, v_prev = after((add_parts(*parts), k_norm, v_prev))
+    k_prev = move_chips(k_sent, line_shift(1))
+    low = add_parts(low, *rounds(SPREAD_Z[0], low))
+    low, v_prev = after((low, v_prev))
+    v_early = move_chips(second_group(v_prev), line_shift(1))
+    low = add_parts(low, *rounds(SPREAD_Z[1], low))
+    low, k_prev = after((low, k_prev))
+    k_early = move_chips(second_group(k_prev), line_shift(1))
+    parts = [low] + [shift_x(low, by) for by in (1, 2, 3)]
+    blocks = (k_norm, k_prev, k_early, v2, v_prev, v_early)
 
     attn, top, probs, sink = call(
         forward_kernel,
@@ -426,68 +452,58 @@
     )(probs, keep, got)
     pair, v_low, v_prev_out, v_early_out = after((pair, v_low, v_prev_out, v_early_out))
     v_near = move_chips(v_prev_out, line_shift(-1))
-    v_far = move_chips(v_early_out, line_shift(-2))
     quad = quads_z(pair, jnp.maximum)
     chan = quads_x(quad, jnp.maximum)
-    chan, v_near, v_far = after((chan, v_near, v_far))
-
-    *pieces, grad_attn, delta, scaled = pl.pallas_call(
-        sink_kernel,
-        out_shape=(quarter,) * XS
-        + (low_half(2 * TOK), shape(2 * TOK, HALF), low_half(2 * TOK)),
-        in_specs=[pl.BlockSpec(memory_space=pltpu.SMEM)]
-        + [pl.BlockSpec(memory_space=pltpu.VMEM)] * 8,
-        scratch_shapes=[pltpu.VMEM((TOK, HALF), F32)],
-        compiler_params=pltpu.CompilerParams(vmem_limit_bytes=48 * 1024 * 1024),
-        cost_estimate=pl.CostEstimate(
-            flops=block_flops // 3, bytes_accessed=4 * 1024 * 1024, transcendentals=0
-        ),
-    )(places, probs, keep, got, attn, chan, q_norm, sink, v_low)
-    total = pieces[0].astype(F32)
-    for by in (1, 2, 3):
-        total = total + shift_x(pieces[by], by).astype(F32)
-    grad_qn, k_own, k_prev, k_early, gain_sum, inner = call(
+    chan, v_near = after((chan, v_near))
+
+    low, grad_qn, k_own, k_prev_out, k_early_out, scaled, gain_sum, inner = call(
         backward_kernel,
         (
+            shape(TOK, 2 * HALF, kind=BF16),
             shape(2 * TOK, HALF),
             shape(2 * TOK, HALF),
             low_half(2 * TOK),
-            low_half(TOK),
+            shape(TOK, 2 * HALF, kind=BF16),
+            low_half(2 * TOK),
             shape(1, HALF),
-            shape(8, TOK),
+            shape(3, TOK),
         ),
         3 * block_flops,
         8 * 1024 * 1024,
-    )(probs, grad_attn, delta, q_norm, *blocks, sink)
-    inner_got = other_core(inner)
-    inner = inner + inner_got[jnp.array([1, 0, 3, 2, 5, 4, 6, 7])]
-
-    inner, total = after((inner, total))
-    total = gather_z(total, 0)
-    inner = sum_heads(inner)
-    near, far = call(
-        pack_kernel, (shape(2 * TOK, HALF + HD, kind=BF16), shape(TOK, HALF + HD, kind=BF16))
-    )(k_prev, k_early, inner)
-    sums = jnp.concatenate([gain_sum.reshape(HEADS, HD), inner[7:8]])
-
-    sums, total, near, far = after((sums, total, near, far))
-    near_got = move_chips(near, line_shift(-1))
-    total = gather_z(total, 1)
+    )(probs, keep, got, attn, chan, q_norm, *blocks, sink, v_low, v_early_out)
+
+    near = move_chips(k_prev_out, line_shift(-1))
+    far = move_chips(k_early_out, line_shift(-2))
+    from_x = rounds(GATHER_X, low)
+    near, far, from_x = after((near, far, from_x))
+    k_total, low, inner, swapped = call(
+        key_sum_kernel,
+        (
+            shape(2 * TOK, HALF),
+            shape(TOK, 2 * HALF, kind=BF16),
+            shape(8, TOK),
+            shape(8, TOK),
+        ),
+        scalar=True,
+        args=9,
+    )(places, k_own, near, far, k_norm, inner, low, *from_x)
+    inner = sum_heads(inner + other_core(swapped))
+    low = add_parts(low, *rounds(GATHER_Z[0], low))
+    sums = jnp.concatenate([gain_sum.reshape(HEADS, HD), inner[4:5]])
+
+    sums, low = after((sums, low))
+    low = add_parts(low, *rounds(GATHER_Z[1], low))
+    sums = quads_x(sums, jnp.add)
     sums = pairs_z(sums, jnp.add)
-    sums, total, far = after((sums, total, far))
-    far_got = move_chips(far, line_shift(-2))
-    low = total.astype(BF16)
-    sunk = [total] + [move_chips(low, pairs_of(turn)) for turn in GATHER_X]
+    sums, low = after((sums, low))
     sums = quads_z(sums, jnp.add)
-    sums, sunk, near_got, far_got = after((sums, sunk, near_got, far_got))
-    sums = quads_x(sums, jnp.add)
 
     q_mine, q_other = call(query_kernel, (low_half(TOK), low_half(TOK)))(
         grad_qn, keep, got, tags, tags_got, gains_q, inner
     )
     both = shape(2, TOK, HALF, kind=BF16)
-    mine, other = call(key_kernel, (both, both), scalar=True, args=18)(
-        places, k_own, v_own, near_got, far_got, v_near, v_far, *sunk, inner, sums[HEADS:], chan,
+    mine, other = call(key_kernel, (both, both), scalar=True, args=13)(
+        places, k_total, v_own, v_near, far, low, inner, sums[HEADS:], chan,
         keep, got, tags, tags_got, gains_k,
     )
 

time: 173 us -> 164 us (0.948)
  waiting for transfers between devices: 35.5 us -> 57.9 us
  starting transfers between devices: 103 us -> 82.4 us
  local copies, waits for them, and re-layouts: 11.7 us -> 4.81 us
  other arithmetic: 9.11 us -> 5.6 us
    ppermute x42 -> x38, waiting for transfers between devices: 33.3 us -> 55.2 us  [move_chips(): return lax.ppermute(value, 'frame', chip_pairs(move))]
    ppermute x42 -> x38, starting transfers between devices: 77.7 us -> 56.4 us  [move_chips(): return lax.ppermute(value, 'frame', chip_pairs(move))]
    unnamed x42 -> x20, local copies, waits for them, and re-layouts: 9.18 us -> 2.69 us
    add x7 -> x1, other arithmetic: 3.39 us -> 0.01 us  [per_device(): inner = sum_heads(inner + other_core(swapped))]
    pallas_call x6 -> x9, Pallas kernels: 7.02 us -> 6.72 us  [the longest x1 2.98 us: per_device(): pl.pallas_call(entry_kernel, out_shape=(shape(4, TOK, HALF, kind=BF16),)...]
  transfers between devices with their start and end apart: 55 -> 51, of which waited for: 17 -> 21; matrix products, arithmetic and copies ran while one was open for 5% -> 4% of each run, Pallas kernels for 4% -> 1%
where the time goes in v2:
time: 164 us; the launch traced here: 163 us
  starting transfers between devices  82.4 us (50%)
  waiting for transfers between devices  57.9 us (35%)
  Pallas kernels  10.6 us (6%)
  other arithmetic  5.6 us (3%)
  local copies, waits for them, and re-layouts  4.81 us (3%)
  between operations  1.85 us (1%)
    ppermute x38, starting transfers between devices, move_chips(): return lax.ppermute(value, 'frame', chip_pairs(move))  56.4 us
    ppermute x38, waiting for transfers between devices, move_chips(): return lax.ppermute(value, 'frame', chip_pairs(move))  55.2 us
    ppermute x7, starting transfers between devices, other_core(): lax.ppermute(value, 'frame', [(i, i ^ 1) for i in range(2 * XS * ZS)])  17.3 us
    ppermute x6, starting transfers between devices, head_turns(): lax.ppermute(value, 'head', [(i, (i + by) % 4) for i in range(4)])  8.72 us
  transfers between devices with their start and end apart: 51, of which 21 were waited for; matrix products, arithmetic and copies ran while one was open for 4% of the time, Pallas kernels for 1%

profile of v2, /device:TPU:1, one launch (start us, length us, event | category | flops | bytes accessed | tf_op | source)
XLA Modules:
  0.0 163.2 jit_solution(9923383200187134358)
XLA Ops:
  0.7 3.0 %shard_map.127 = (bf16[4,128,640]{2,1,0:T(8,128)(2,1)}, bf16[4,128,640]{2,1,0:T(8,128)(2,1)}, f32[2,128]{1,0:T(2,128)}) custom-call(s32[1]{0:T(128)} %bitcast.1.core, bf16[128,1280]{1,0:T(8,128)(2,1)} %q.1, bf16[128,1280]{1,0:T(8,128)(2,1)} %k.1, bf16[128,1280]{1,0:T(8,128)(2,1)} %v.1, bf16[128,1280]{1,0:T(8,128)(2,1)} %c.1), custom_call_target="tpu_custom_call" | custom-call | tf_op jit(solution)/shard_map/pallas_call | solution.py:389
  3.6 3.6 %collective-permute-start.3 = (f32[2,128]{1,0:T(2,128)}, f32[2,128]{1,0:T(2,128)S(1)}, u32[]{:S(2)}, u32[]{:S(2)}) collective-permute-start(f32[2,128]{1,0:T(2,128)} %get-tuple-element.64), channel_id=1, source_target_pairs={{0,3},{1,0},{2,1},{3,2},{4,7},{5,4},{6,5},{7,6},{8,11},{9,8},{10,9... | collective-permute-start | bytes 3080 | tf_op jit(solution)/shard_map/ppermute | solution.py:64
  14.3 3.6 %collective-permute-start.8 = (bf16[256,640]{1,0:T(8,128)(2,1)S(1)}, bf16[256,640]{1,0:T(8,128)(2,1)S(1)}, u32[]{:S(2)}, u32[]{:S(2)}) collective-permute-start(bf16[256,640]{1,0:T(8,128)(2,1)S(1)} %pad_maximum_fusion.vo), channel_id=1, source_target_pairs={{0,8},{4,12},{8,16},{12,20},{16,24},{20,28},{24,32},{28,36},{32,40... | collective-permute-start | bytes 983048 | tf_op jit(solution)/shard_map/ppermute | solution.py:36
  20.7 3.1 %collective-permute-start.5 = (bf16[32,1280]{1,0:T(8,128)(2,1)S(1)}, bf16[32,1280]{1,0:T(8,128)(2,1)S(1)}, u32[]{:S(2)}, u32[]{:S(2)}) collective-permute-start(bf16[32,1280]{1,0:T(8,128)(2,1)S(1)} %get-tuple-element.69), channel_id=1, source_target_pairs={{0,64},{4,68},{1,65},{5,69},{2,66},{6,70},{3,67},{7,71}} | collective-permute-start | bytes 245768 | tf_op jit(solution)/shard_map/ppermute | solution.py:36
  23.9 2.2 %collective-permute-start.6 = (bf16[32,1280]{1,0:T(8,128)(2,1)S(1)}, bf16[32,1280]{1,0:T(8,128)(2,1)S(1)}, u32[]{:S(2)}, u32[]{:S(2)}) collective-permute-start(bf16[32,1280]{1,0:T(8,128)(2,1)S(1)} %get-tuple-element.70), channel_id=1, source_target_pairs={{0,128},{4,132},{1,129},{5,133},{2,130},{6,134},{3,131},{7,135}} | collective-permute-start | bytes 245768 | tf_op jit(solution)/shard_map/ppermute | solution.py:36
  27.4 3.4 %collective-permute-done.5.refs_1_ = bf16[32,1280]{1,0:T(8,128)(2,1)S(1)} collective-permute-done((bf16[32,1280]{1,0:T(8,128)(2,1)S(1)}, bf16[32,1280]{1,0:T(8,128)(2,1)S(1)}, u32[]{:S(2)}, u32[]{:S(2)}) %collective-permute-start.5) | collective-permute-done | bytes 81952 | tf_op jit(solution)/shard_map/ppermute | solution.py:36
  33.9 2.3 %collective-permute-start.10 = (bf16[32,1280]{1,0:T(8,128)(2,1)S(1)}, bf16[32,1280]{1,0:T(8,128)(2,1)S(1)}, u32[]{:S(2)}, u32[]{:S(2)}) collective-permute-start(bf16[32,1280]{1,0:T(8,128)(2,1)S(1)} %shard_map.129.refs_0_), channel_id=1, source_target_pairs={{0,48},{4,52},{64,112},{68,116},{128,176},{132,180},{192,240},{196... | collective-permute-start | bytes 245768 | tf_op jit(solution)/shard_map/ppermute | solution.py:36
  43.7 2.5 %collective-permute-start.14 = (bf16[128,640]{1,0:T(8,128)(2,1)S(1)}, bf16[128,640]{1,0:T(8,128)(2,1)S(1)}, u32[]{:S(2)}, u32[]{:S(2)}) collective-permute-start(bf16[128,640]{1,0:T(8,128)(2,1)S(1)} %slice_select_fusion.1), channel_id=1, source_target_pairs={{0,8},{4,12},{8,16},{12,20},{16,24},{20,28},{24,32},{28,36},{32,40... | collective-permute-start | bytes 491528 | tf_op jit(solution)/shard_map/ppermute | solution.py:36
  46.1 2.6 %collective-permute-start.18 = (bf16[32,1280]{1,0:T(8,128)(2,1)S(1)}, bf16[32,1280]{1,0:T(8,128)(2,1)S(1)}, u32[]{:S(2)}, u32[]{:S(2)}) collective-permute-start(bf16[32,1280]{1,0:T(8,128)(2,1)S(1)} %shard_map.131.s0), channel_id=1, source_target_pairs={{0,192},{4,196},{8,200},{12,204},{16,208},{20,212},{24,216},{28,22... | collective-permute-start | bytes 245768 | tf_op jit(solution)/shard_map/ppermute | solution.py:36
  48.8 2.4 %collective-permute-start.17 = (bf16[32,1280]{1,0:T(8,128)(2,1)S(1)}, bf16[32,1280]{1,0:T(8,128)(2,1)S(1)}, u32[]{:S(2)}, u32[]{:S(2)}) collective-permute-start(bf16[32,1280]{1,0:T(8,128)(2,1)S(1)} %shard_map.131.s0), channel_id=1, source_target_pairs={{0,128},{4,132},{8,136},{12,140},{16,144},{20,148},{24,152},{28,15... | collective-permute-start | bytes 245768 | tf_op jit(solution)/shard_map/ppermute | solution.py:36
  52.0 7.8 %collective-permute-done.17.s2 = bf16[32,1280]{1,0:T(8,128)(2,1)S(1)} collective-permute-done((bf16[32,1280]{1,0:T(8,128)(2,1)S(1)}, bf16[32,1280]{1,0:T(8,128)(2,1)S(1)}, u32[]{:S(2)}, u32[]{:S(2)}) %collective-permute-start.17) | collective-permute-done | bytes 81952 | tf_op jit(solution)/shard_map/ppermute | solution.py:36
  59.8 2.4 %shard_map.132 = (bf16[256,640]{1,0:T(8,128)(2,1)S(1)}, f32[1,640]{1,0:T(1,128)S(1)}, bf16[5,256,768]{2,1,0:T(8,128)(2,1)S(1)}, bf16[128,1280]{1,0:T(8,128)(2,1)S(1)}) custom-call(s32[1]{0:T(128)} %bitcast.place, f32[256,768]{1,0:T(8,128)S(1)} %get-tuple-element.65.bias, bf16[256,640]{1,0:T(8,128)(2,1)S(1)} %get-tuple-element.66.q, ...), custom_call_target="tpu_custom_call" | custom-call | flops 503316480 | bytes 6291456 | tf_op jit(solution)/shard_map/pallas_call | solution.py:431
  64.7 2.9 %collective-permute-start.21 = (f32[1,640]{1,0:T(1,128)S(1)}, f32[1,640]{1,0:T(1,128)S(1)}, u32[]{:S(2)}, u32[]{:S(2)}) collective-permute-start(f32[1,640]{1,0:T(1,128)S(1)} %max.21), channel_id=1, source_target_pairs={{0,16},{4,20},{8,24},{12,28},{16,32},{20,36},{24,40},{28,44},{32,4... | collective-permute-start | bytes 7688 | tf_op jit(solution)/shard_map/ppermute | solution.py:36
  67.7 3.0 %collective-permute-start.20 = (f32[1,640]{1,0:T(1,128)S(1)}, f32[1,640]{1,0:T(1,128)S(1)}, u32[]{:S(2)}, u32[]{:S(2)}) collective-permute-start(f32[1,640]{1,0:T(1,128)S(1)} %max.21), channel_id=1, source_target_pairs={{0,32},{4,36},{8,40},{12,44},{16,48},{20,52},{24,56},{28,60},{32,0... | collective-permute-start | bytes 7688 | tf_op jit(solution)/shard_map/ppermute | solution.py:36
  74.0 2.2 %collective-permute-start.25 = (f32[1,640]{1,0:T(1,128)S(1)}, f32[1,640]{1,0:T(1,128)S(1)}, u32[]{:S(2)}, u32[]{:S(2)}) collective-permute-start(f32[1,640]{1,0:T(1,128)S(1)} %maximum_maximum_fusion.1), channel_id=1, source_target_pairs={{0,192},{4,196},{8,200},{12,204},{16,208},{20,212},{24,216},{28,22... | collective-permute-start | bytes 7688 | tf_op jit(solution)/shard_map/ppermute | solution.py:36
  81.1 2.2 %shard_map.134 = (bf16[128,1280]{1,0:T(8,128)(2,1)S(1)}, f32[256,640]{1,0:T(8,128)S(1)}, f32[256,640]{1,0:T(8,128)S(1)}, bf16[256,640]{1,0:T(8,128)(2,1)S(1)}, b...) custom-call(bf16[5,256,768]{2,1,0:T(8,128)(2,1)S(1)} %get-tuple-elemen, ...), custom_call_target="tpu_custom_call" | custom-call | flops 754974720 | bytes 8388608 | tf_op jit(solution)/shard_map/pallas_call | solution.py:459
  91.1 9.6 %collective-permute-done.29.far = bf16[128,1280]{1,0:T(8,128)(2,1)S(1)} collective-permute-done((bf16[128,1280]{1,0:T(8,128)(2,1)S(1)}, bf16[128,1280]{1,0:T(8,128)(2,1)S(1)}, u32[]{:S(2)}, u32[]{:S(2)}) %collective-permute-start.29) | collective-permute-done | bytes 327712 | tf_op jit(solution)/shard_map/ppermute | solution.py:36
  102.6 9.3 %collective-permute-start.33 = (f32[8,128]{1,0:T(8,128)S(1)}, f32[8,128]{1,0:T(8,128)S(1)}, u32[]{:S(2)}, u32[]{:S(2)}) collective-permute-start(f32[8,128]{1,0:T(8,128)S(1)} %get-tuple-element.104), channel_id=1, source_target_pairs={{0,4},{4,0},{8,12},{12,8},{16,20},{20,16},{24,28},{28,24},{32,36},... | collective-permute-start | bytes 12296 | tf_op jit(solution)/shard_map/ppermute | solution.py:60
  118.9 9.2 %collective-permute-done.39.refs_2_ = bf16[128,1280]{1,0:T(8,128)(2,1)S(1)} collective-permute-done((bf16[128,1280]{1,0:T(8,128)(2,1)S(1)}, bf16[128,1280]{1,0:T(8,128)(2,1)S(1)}, u32[]{:S(2)}, u32[]{:S(2)}) %collective-permute-start.39) | collective-permute-done | bytes 327712 | tf_op jit(solution)/shard_map/ppermute | solution.py:36
  130.8 2.5 %collective-permute-start.27 = (bf16[128,640]{1,0:T(8,128)(2,1)S(1)}, bf16[128,640]{1,0:T(8,128)(2,1)S(1)}, u32[]{:S(2)}, u32[]{:S(2)}) collective-permute-start(bf16[128,640]{1,0:T(8,128)(2,1)S(1)} %get-tuple-element.123), channel_id=1, source_target_pairs={{0,4},{4,0},{8,12},{12,8},{16,20},{20,16},{24,28},{28,24},{32,36},... | collective-permute-start | bytes 491528 | tf_op jit(solution)/shard_map/ppermute | solution.py:60
  139.0 8.5 %collective-permute-done.45.refs_2_ = bf16[128,1280]{1,0:T(8,128)(2,1)S(1)} collective-permute-done((bf16[128,1280]{1,0:T(8,128)(2,1)S(1)}, bf16[128,1280]{1,0:T(8,128)(2,1)S(1)}, u32[]{:S(2)}, u32[]{:S(2)}) %collective-permute-start.45) | collective-permute-done | bytes 327712 | tf_op jit(solution)/shard_map/ppermute | solution.py:36
  147.9 2.4 %collective-permute-start.47 = (f32[6,128]{1,0:T(8,128)S(1)}, f32[6,128]{1,0:T(8,128)S(1)}, u32[]{:S(2)}, u32[]{:S(2)}) collective-permute-start(f32[6,128]{1,0:T(8,128)S(1)} %add.57), channel_id=1, source_target_pairs={{0,16},{4,20},{8,24},{12,28},{16,32},{20,36},{24,40},{28,44},{32,4... | collective-permute-start | bytes 9224 | tf_op jit(solution)/shard_map/ppermute | solution.py:36
  152.5 4.1 %collective-permute-done.46 = f32[6,128]{1,0:T(8,128)S(1)} collective-permute-done((f32[6,128]{1,0:T(8,128)S(1)}, f32[6,128]{1,0:T(8,128)S(1)}, u32[]{:S(2)}, u32[]{:S(2)}) %collective-permute-start.46) | collective-permute-done | bytes 3104 | tf_op jit(solution)/shard_map/ppermute | solution.py:36
  156.6 3.2 %collective-permute-start.50 = (f32[1,640]{1,0:T(1,128)S(1)}, f32[1,640]{1,0:T(1,128)S(1)}, u32[]{:S(2)}, u32[]{:S(2)}) collective-permute-start(f32[1,640]{1,0:T(1,128)S(1)} %bitcast.27), channel_id=1, source_target_pairs={{0,4},{4,0},{8,12},{12,8},{16,20},{20,16},{24,28},{28,24},{32,36},... | collective-permute-start | bytes 7688 | tf_op jit(solution)/shard_map/ppermute | solution.py:60
  (144 shorter events, 63.4 us)
Async XLA Ops:
  3.6 9.9 %collective-permute-start.3 = (f32[2,128]{1,0:T(2,128)}, f32[2,128]{1,0:T(2,128)S(1)}, u32[]{:S(2)}, u32[]{:S(2)}) collective-permute-start(f32[2,128]{1,0:T(2,128)} %get-tuple-element.64), channel_id=1, source_target_pairs={{0,3},{1,0},{2,1},{3,2},{4,7},{5,4},{6,5},{7,6},{8,11},{9,8},{10,9... | collective-permute-start | bytes 3080 | tf_op jit(solution)/shard_map/ppermute | solution.py:64
  14.3 18.2 %collective-permute-start.8 = (bf16[256,640]{1,0:T(8,128)(2,1)S(1)}, bf16[256,640]{1,0:T(8,128)(2,1)S(1)}, u32[]{:S(2)}, u32[]{:S(2)}) collective-permute-start(bf16[256,640]{1,0:T(8,128)(2,1)S(1)} %pad_maximum_fusion.vo), channel_id=1, source_target_pairs={{0,8},{4,12},{8,16},{12,20},{16,24},{20,28},{24,32},{28,36},{32,40... | collective-permute-start | bytes 983048 | tf_op jit(solution)/shard_map/ppermute | solution.py:36
  20.7 10.0 %collective-permute-start.5 = (bf16[32,1280]{1,0:T(8,128)(2,1)S(1)}, bf16[32,1280]{1,0:T(8,128)(2,1)S(1)}, u32[]{:S(2)}, u32[]{:S(2)}) collective-permute-start(bf16[32,1280]{1,0:T(8,128)(2,1)S(1)} %get-tuple-element.69), channel_id=1, source_target_pairs={{0,64},{4,68},{1,65},{5,69},{2,66},{6,70},{3,67},{7,71}} | collective-permute-start | bytes 245768 | tf_op jit(solution)/shard_map/ppermute | solution.py:36
  23.9 8.6 %collective-permute-start.6 = (bf16[32,1280]{1,0:T(8,128)(2,1)S(1)}, bf16[32,1280]{1,0:T(8,128)(2,1)S(1)}, u32[]{:S(2)}, u32[]{:S(2)}) collective-permute-start(bf16[32,1280]{1,0:T(8,128)(2,1)S(1)} %get-tuple-element.70), channel_id=1, source_target_pairs={{0,128},{4,132},{1,129},{5,133},{2,130},{6,134},{3,131},{7,135}} | collective-permute-start | bytes 245768 | tf_op jit(solution)/shard_map/ppermute | solution.py:36
  32.5 11.1 %collective-permute-start.13 = (bf16[256,640]{1,0:T(8,128)(2,1)S(1)}, bf16[256,640]{1,0:T(8,128)(2,1)S(1)}, u32[]{:S(2)}, u32[]{:S(2)}) collective-permute-start(bf16[256,640]{1,0:T(8,128)(2,1)S(1)} %get-tuple-element.75.ko.k_norm), channel_id=1, source_target_pairs={{0,8},{4,12},{8,16},{12,20},{16,24},{20,28},{24,32},{28,36},{32,40... | collective-permute-start | bytes 983048 | tf_op jit(solution)/shard_map/ppermute | solution.py:36
  42.1 9.9 %collective-permute-start.15 = (bf16[128,640]{1,0:T(8,128)(2,1)S(1)}, bf16[128,640]{1,0:T(8,128)(2,1)S(1)}, u32[]{:S(2)}, u32[]{:S(2)}) collective-permute-start(bf16[128,640]{1,0:T(8,128)(2,1)S(1)} %slice_select_fusion), channel_id=1, source_target_pairs={{0,8},{4,12},{8,16},{12,20},{16,24},{20,28},{24,32},{28,36},{32,40... | collective-permute-start | bytes 491528 | tf_op jit(solution)/shard_map/ppermute | solution.py:36
  43.7 16.1 %collective-permute-start.14 = (bf16[128,640]{1,0:T(8,128)(2,1)S(1)}, bf16[128,640]{1,0:T(8,128)(2,1)S(1)}, u32[]{:S(2)}, u32[]{:S(2)}) collective-permute-start(bf16[128,640]{1,0:T(8,128)(2,1)S(1)} %slice_select_fusion.1), channel_id=1, source_target_pairs={{0,8},{4,12},{8,16},{12,20},{16,24},{20,28},{24,32},{28,36},{32,40... | collective-permute-start | bytes 491528 | tf_op jit(solution)/shard_map/ppermute | solution.py:36
  48.8 11.0 %collective-permute-start.17 = (bf16[32,1280]{1,0:T(8,128)(2,1)S(1)}, bf16[32,1280]{1,0:T(8,128)(2,1)S(1)}, u32[]{:S(2)}, u32[]{:S(2)}) collective-permute-start(bf16[32,1280]{1,0:T(8,128)(2,1)S(1)} %shard_map.131.s0), channel_id=1, source_target_pairs={{0,128},{4,132},{8,136},{12,140},{16,144},{20,148},{24,152},{28,15... | collective-permute-start | bytes 245768 | tf_op jit(solution)/shard_map/ppermute | solution.py:36
  51.2 8.6 %collective-permute-start.16 = (bf16[32,1280]{1,0:T(8,128)(2,1)S(1)}, bf16[32,1280]{1,0:T(8,128)(2,1)S(1)}, u32[]{:S(2)}, u32[]{:S(2)}) collective-permute-start(bf16[32,1280]{1,0:T(8,128)(2,1)S(1)} %shard_map.131.s0), channel_id=1, source_target_pairs={{0,64},{4,68},{8,72},{12,76},{16,80},{20,84},{24,88},{28,92},{32,9... | collective-permute-start | bytes 245768 | tf_op jit(solution)/shard_map/ppermute | solution.py:36
  64.7 7.3 %collective-permute-start.22 = (f32[1,640]{1,0:T(1,128)S(1)}, f32[1,640]{1,0:T(1,128)S(1)}, u32[]{:S(2)}, u32[]{:S(2)}) collective-permute-start(f32[1,640]{1,0:T(1,128)S(1)} %max.21), channel_id=1, source_target_pairs={{0,48},{4,52},{8,56},{12,60},{16,0},{20,4},{24,8},{28,12},{32,16},... | collective-permute-start | bytes 7688 | tf_op jit(solution)/shard_map/ppermute | solution.py:36
  64.7 7.3 %collective-permute-start.21 = (f32[1,640]{1,0:T(1,128)S(1)}, f32[1,640]{1,0:T(1,128)S(1)}, u32[]{:S(2)}, u32[]{:S(2)}) collective-permute-start(f32[1,640]{1,0:T(1,128)S(1)} %max.21), channel_id=1, source_target_pairs={{0,16},{4,20},{8,24},{12,28},{16,32},{20,36},{24,40},{28,44},{32,4... | collective-permute-start | bytes 7688 | tf_op jit(solution)/shard_map/ppermute | solution.py:36
  70.7 9.7 %collective-permute-start.26 = (bf16[256,640]{1,0:T(8,128)(2,1)S(1)}, bf16[256,640]{1,0:T(8,128)(2,1)S(1)}, u32[]{:S(2)}, u32[]{:S(2)}) collective-permute-start(bf16[256,640]{1,0:T(8,128)(2,1)S(1)} %get-tuple-element.86), channel_id=1, source_target_pairs={{8,0},{12,4},{16,8},{20,12},{24,16},{28,20},{32,24},{36,28},{40,32... | collective-permute-start | bytes 983048 | tf_op jit(solution)/shard_map/ppermute | solution.py:36
  83.2 7.8 %collective-permute-start.28 = (bf16[256,640]{1,0:T(8,128)(2,1)S(1)}, bf16[256,640]{1,0:T(8,128)(2,1)S(1)}, u32[]{:S(2)}, u32[]{:S(2)}) collective-permute-start(bf16[256,640]{1,0:T(8,128)(2,1)S(1)} %get-tuple-element.94), channel_id=1, source_target_pairs={{8,0},{12,4},{16,8},{20,12},{24,16},{28,20},{32,24},{36,28},{40,32... | collective-permute-start | bytes 983048 | tf_op jit(solution)/shard_map/ppermute | solution.py:36
  84.6 16.1 %collective-permute-start.29 = (bf16[128,1280]{1,0:T(8,128)(2,1)S(1)}, bf16[128,1280]{1,0:T(8,128)(2,1)S(1)}, u32[]{:S(2)}, u32[]{:S(2)}) collective-permute-start(bf16[128,1280]{1,0:T(8,128)(2,1)S(1)} %get-tuple-element.95), channel_id=1, source_target_pairs={{16,0},{20,4},{24,8},{28,12},{32,16},{36,20},{40,24},{44,28},{48,3... | collective-permute-start | bytes 983048 | tf_op jit(solution)/shard_map/ppermute | solution.py:36
  85.9 15.2 %collective-permute-start.32 = (bf16[128,1280]{1,0:T(8,128)(2,1)S(1)}, bf16[128,1280]{1,0:T(8,128)(2,1)S(1)}, u32[]{:S(2)}, u32[]{:S(2)}) collective-permute-start(bf16[128,1280]{1,0:T(8,128)(2,1)S(1)} %get-tuple-element.96.p0), channel_id=1, source_target_pairs={{192,0},{196,4},{200,8},{204,12},{208,16},{212,20},{216,24},{220,2... | collective-permute-start | bytes 983048 | tf_op jit(solution)/shard_map/ppermute | solution.py:36
  87.2 13.9 %collective-permute-start.31 = (bf16[128,1280]{1,0:T(8,128)(2,1)S(1)}, bf16[128,1280]{1,0:T(8,128)(2,1)S(1)}, u32[]{:S(2)}, u32[]{:S(2)}) collective-permute-start(bf16[128,1280]{1,0:T(8,128)(2,1)S(1)} %get-tuple-element.96.p0), channel_id=1, source_target_pairs={{64,0},{68,4},{72,8},{76,12},{80,16},{84,20},{88,24},{92,28},{96,3... | collective-permute-start | bytes 983048 | tf_op jit(solution)/shard_map/ppermute | solution.py:36
  88.5 12.6 %collective-permute-start.30 = (bf16[128,1280]{1,0:T(8,128)(2,1)S(1)}, bf16[128,1280]{1,0:T(8,128)(2,1)S(1)}, u32[]{:S(2)}, u32[]{:S(2)}) collective-permute-start(bf16[128,1280]{1,0:T(8,128)(2,1)S(1)} %get-tuple-element.96.p0), channel_id=1, source_target_pairs={{128,0},{132,4},{136,8},{140,12},{144,16},{148,20},{152,24},{156,2... | collective-permute-start | bytes 983048 | tf_op jit(solution)/shard_map/ppermute | solution.py:36
  102.6 10.2 %collective-permute-start.33 = (f32[8,128]{1,0:T(8,128)S(1)}, f32[8,128]{1,0:T(8,128)S(1)}, u32[]{:S(2)}, u32[]{:S(2)}) collective-permute-start(f32[8,128]{1,0:T(8,128)S(1)} %get-tuple-element.104), channel_id=1, source_target_pairs={{0,4},{4,0},{8,12},{12,8},{16,20},{20,16},{24,28},{28,24},{32,36},... | collective-permute-start | bytes 12296 | tf_op jit(solution)/shard_map/ppermute | solution.py:60
  116.2 11.9 %collective-permute-start.39 = (bf16[128,1280]{1,0:T(8,128)(2,1)S(1)}, bf16[128,1280]{1,0:T(8,128)(2,1)S(1)}, u32[]{:S(2)}, u32[]{:S(2)}) collective-permute-start(bf16[128,1280]{1,0:T(8,128)(2,1)S(1)} %get-tuple-element.111.refs_0_), channel_id=1, source_target_pairs={{16,24},{20,28},{56,0},{60,4},{17,25},{21,29},{57,1},{61,5},{18,26... | collective-permute-start | bytes 983048 | tf_op jit(solution)/shard_map/ppermute | solution.py:36
  117.5 10.6 %collective-permute-start.38 = (bf16[128,1280]{1,0:T(8,128)(2,1)S(1)}, bf16[128,1280]{1,0:T(8,128)(2,1)S(1)}, u32[]{:S(2)}, u32[]{:S(2)}) collective-permute-start(bf16[128,1280]{1,0:T(8,128)(2,1)S(1)} %get-tuple-element.111.refs_0_), channel_id=1, source_target_pairs={{8,0},{12,4},{32,24},{36,28},{48,40},{52,44},{9,1},{13,5},{33,25},... | collective-permute-start | bytes 983048 | tf_op jit(solution)/shard_map/ppermute | solution.py:36
  128.3 6.9 %collective-permute-start.41 = (f32[6,128]{1,0:T(8,128)S(1)}, f32[6,128]{1,0:T(8,128)S(1)}, u32[]{:S(2)}, u32[]{:S(2)}) collective-permute-start(f32[6,128]{1,0:T(8,128)S(1)} %pad_maximum_fusion.1), channel_id=1, source_target_pairs={{0,64},{4,68},{8,72},{12,76},{16,80},{20,84},{24,88},{28,92},{32,9... | collective-permute-start | bytes 9224 | tf_op jit(solution)/shard_map/ppermute | solution.py:36
  133.5 17.7 %collective-permute-start.37 = (bf16[128,640]{1,0:T(8,128)(2,1)S(1)}, bf16[128,640]{1,0:T(8,128)(2,1)S(1)}, u32[]{:S(2)}, u32[]{:S(2)}) collective-permute-start(bf16[128,640]{1,0:T(8,128)(2,1)S(1)} %get-tuple-element.106), channel_id=1, source_target_pairs={{0,4},{4,0},{8,12},{12,8},{16,20},{20,16},{24,28},{28,24},{32,36},... | collective-permute-start | bytes 491528 | tf_op jit(solution)/shard_map/ppermute | solution.py:60
  133.9 13.7 %collective-permute-start.45 = (bf16[128,1280]{1,0:T(8,128)(2,1)S(1)}, bf16[128,1280]{1,0:T(8,128)(2,1)S(1)}, u32[]{:S(2)}, u32[]{:S(2)}) collective-permute-start(bf16[128,1280]{1,0:T(8,128)(2,1)S(1)} %shard_map.137.refs_0_), channel_id=1, source_target_pairs={{40,0},{44,4},{41,1},{45,5},{42,2},{46,6},{43,3},{47,7}} | collective-permute-start | bytes 983048 | tf_op jit(solution)/shard_map/ppermute | solution.py:36
  135.2 12.5 %collective-permute-start.44 = (bf16[128,1280]{1,0:T(8,128)(2,1)S(1)}, bf16[128,1280]{1,0:T(8,128)(2,1)S(1)}, u32[]{:S(2)}, u32[]{:S(2)}) collective-permute-start(bf16[128,1280]{1,0:T(8,128)(2,1)S(1)} %shard_map.137.refs_0_), channel_id=1, source_target_pairs={{24,0},{28,4},{25,1},{29,5},{26,2},{30,6},{27,3},{31,7}} | collective-permute-start | bytes 983048 | tf_op jit(solution)/shard_map/ppermute | solution.py:36
  (36 other events, 236.3 us)

commit v3 on v2

--- a/solution.py
+++ b/solution.py
@@ -82,14 +82,14 @@
 
 
 SCATTER_X = tuple(row(0, to, (0,)) for to in range(1, XS))
-GATHER_X = tuple(row(src, 0, range(ZS)) for src in (2, 1, 3))
+GATHER_X = tuple(row(src, 0, (0,)) for src in range(1, XS))
 SPREAD_Z = (
     (column({0: 5}, range(XS)), column({0: 6}, range(XS))),
     (column({0: 7, 5: 3, 6: 4}, range(XS)), column({0: 1, 5: 2}, range(XS))),
 )
 GATHER_Z = (
-    (column({1: 0, 4: 3, 6: 5}, (0,)), column({7: 0, 2: 3}, (0,))),
-    (column({3: 0}, (0,)), column({5: 0}, (0,))),
+    (column({1: 0, 4: 3, 6: 5}, range(XS)), column({7: 0, 2: 3}, range(XS))),
+    (column({3: 0}, range(XS)), column({5: 0}, range(XS))),
 )
 
 
@@ -174,12 +174,13 @@
     refs[-1][...] = value.astype(BF16)
 
 
-def norm_kernel(place, keep, got, tags, tags_got, gain_q, gain_k, q_norm, k_norm, bias, *quarters):
+def norm_kernel(place, keep, got, tags, tags_got, gain_q, gain_k, q_norm, k_norm, bias, raw_k, *quarters):
     for half, (source, tag) in enumerate(((keep, tags), (got, tags_got))):
         rows = slice(half * TOK, (half + 1) * TOK)
         rate_q = upright(lax.rsqrt(tag[0:1] / D + EPSILON))
         rate_k = upright(lax.rsqrt(tag[1:2] / D + EPSILON))
         q_norm[rows] = (source[0].astype(F32) * rate_q * gain_q[...]).astype(BF16)
+        raw_k[half] = source[1]
         k_norm[rows] = (source[1].astype(F32) * rate_k * gain_k[...]).astype(BF16)
     core = place[0] % 2
 
@@ -255,20 +256,19 @@
         probs[head] = (weights * inverse).astype(BF16)
 
 
-def value_kernel(probs, keep, got, own, prev, early, sink):
+def value_kernel(probs, keep, got, own, window, sink):
     for head in range(HEADS):
         lanes = lanes_of(head)
         cot = jnp.concatenate([keep[3, :, lanes], got[3, :, lanes]], axis=0)
         grads = contract(probs[head], cot, ((0,), (0,)))
         own[:, lanes] = grads[: 2 * TOK]
-        prev[:, lanes] = grads[2 * TOK : 4 * TOK].astype(BF16)
-        early[:, lanes] = grads[4 * TOK : 5 * TOK].astype(BF16)
+        window[:, lanes] = grads[2 * TOK : 5 * TOK].astype(BF16)
         sink[:, lanes] = grads[5 * TOK :].astype(BF16)
 
 
 def backward_kernel(
-    probs, keep, got, attn, chan, q, ko, kp, ke, vo, vp, ve, sink, v_low, v_early,
-    low, grad_q, own, prev, early, scaled, gain_sum, inner,
+    place, probs, keep, got, attn, chan, q, ko, kp, ke, vo, vp, ve, sink, v_low, v_relayed,
+    p0, p1, p2, p3, grad_q, own, prev, early, scaled, gain_sum, inner, low,
 ):
     inner_q = jnp.zeros((2 * TOK, HD), F32)
     inner_sink = jnp.zeros((TOK, HD), F32)
@@ -295,11 +295,14 @@
         grads = contract(grad_score, query, ((0,), (0,))) * HD ** (-0.5)
         inner_sink = inner_sink + grads[5 * TOK :] * keys[5 * TOK :].astype(F32)
         own[:, lanes] = grads[: 2 * TOK]
-        prev[:, lanes] = grads[2 * TOK : 4 * TOK].astype(BF16)
+        prev[: 2 * TOK, lanes] = grads[2 * TOK : 4 * TOK].astype(BF16)
         early[:, lanes] = grads[4 * TOK : 5 * TOK].astype(BF16)
         low[:, lanes] = grads[5 * TOK :].astype(BF16)
     low[:, HALF:] = v_low[...]
-    early[:, HALF:] = v_early[...]
+    prev[2 * TOK :] = v_relayed[2 * TOK :]
+    x = place[0] // (2 * ZS)
+    for by, part in enumerate((p0, p1, p2, p3)):
+        part[...] = low[pl.ds(pl.multiple_of(((x + by) % XS) * QUARTER, QUARTER), QUARTER)]
     inner[0:1] = lane_sums(inner_q[:TOK])
     inner[1:2] = lane_sums(inner_q[TOK:])
     inner[2:3] = lane_sums(inner_sink)
@@ -313,7 +316,7 @@
     for half in range(2):
         part = slice(half * TOK, (half + 1) * TOK)
         use_far = jnp.where((core + half) == 1, 1.0, 0.0)
-        grad = own[part] + near[part].astype(F32) + use_far * far[:, :HALF].astype(F32)
+        grad = own[part] + near[part].astype(F32) + use_far * far[...].astype(F32)
         total[part] = grad
         rows.append(lane_sums(fold(grad * k_norm[part].astype(F32))))
     parts = (p0[...].astype(F32) + p1[...].astype(F32)) + (
@@ -341,21 +344,22 @@
 
 
 def key_kernel(
-    place, k_total, v_own, v_near, far, sunk, inner, sink_inner, chan,
-    keep, got, tags, tags_got, gain_k, mine, other,
+    place, k_total, v_own, v_near, near, s0, s1, s2, s3, inner, sink_inner, chan,
+    raw_k, tags, tags_got, gain_k, mine, other,
 ):
     core = place[0] % 2
     scale = chan[...] + EPSILON
-    for half, (source, tag, out) in enumerate(((keep, tags, mine), (got, tags_got, other))):
+    sunk = jnp.concatenate([ref[...] for ref in (s0, s1, s2, s3)], axis=0)
+    for half, (tag, out) in enumerate(((tags, mine), (tags_got, other))):
         rows = slice(half * TOK, (half + 1) * TOK)
         use_far = jnp.where((core + half) == 1, 1.0, 0.0)
         use_sink = jnp.where(place[0] < 2, 1.0, 0.0) * (1.0 - use_far)
         rate = upright(lax.rsqrt(tag[1:2] / D + EPSILON))
         grad = k_total[rows] + use_sink * sunk[:, :HALF].astype(F32)
         sums = upright(inner[2 + half : 3 + half] + use_sink * sink_inner[...])
-        out[0] = finish(grad, source[1], rate, gain_k[...], sums)
+        out[0] = finish(grad, raw_k[half], rate, gain_k[...], sums)
         grad = v_own[rows] + v_near[rows].astype(F32)
-        grad = grad + use_far * far[:, HALF:].astype(F32) + use_sink * sunk[:, HALF:].astype(F32)
+        grad = grad + use_far * near[2 * TOK :].astype(F32) + use_sink * sunk[:, HALF:].astype(F32)
         out[1] = (grad / scale).astype(BF16)
 
 
@@ -408,9 +412,11 @@
     pick = lambda value: jnp.where(first, value[:HALF], value[HALF:])[None, :]
     gains_q, gains_k = pick(gain_q), pick(gain_k)
     quarter = shape(QUARTER, 2 * HALF, kind=BF16)
-    q_norm, k_norm, bias, *quarters = call(
+    q_norm, k_norm, bias, raw_k, *quarters = call(
         norm_kernel,
-        (low_half(2 * TOK), low_half(2 * TOK), shape(2 * TOK, KEYS)) + (quarter,) * XS,
+        (low_half(2 * TOK), low_half(2 * TOK), shape(2 * TOK, KEYS))
+        + (shape(2, TOK, HALF, kind=BF16),)
+        + (quarter,) * XS,
         scalar=True,
         args=6,
     )(places, keep, got, tags, tags_got, gains_q, gains_k)
@@ -444,49 +450,54 @@
     )(places, bias, q_norm, *blocks, *parts)
 
     pair = pairs_z(top, jnp.maximum)
-    v_own, v_prev_out, v_early_out, v_low = call(
+    v_own, v_window, v_low = call(
         value_kernel,
-        (shape(2 * TOK, HALF), low_half(2 * TOK), low_half(TOK), low_half(TOK)),
+        (shape(2 * TOK, HALF), low_half(3 * TOK), low_half(TOK)),
         block_flops,
         4 * 1024 * 1024,
     )(probs, keep, got)
-    pair, v_low, v_prev_out, v_early_out = after((pair, v_low, v_prev_out, v_early_out))
-    v_near = move_chips(v_prev_out, line_shift(-1))
+    pair, v_low, v_window = after((pair, v_low, v_window))
+    v_near = move_chips(v_window, line_shift(-1))
     quad = quads_z(pair, jnp.maximum)
     chan = quads_x(quad, jnp.maximum)
     chan, v_near = after((chan, v_near))
 
-    low, grad_qn, k_own, k_prev_out, k_early_out, scaled, gain_sum, inner = call(
+    vmem = pl.BlockSpec(memory_space=pltpu.VMEM)
+    *pieces, grad_qn, k_own, k_prev_out, k_early_out, scaled, gain_sum, inner = pl.pallas_call(
         backward_kernel,
-        (
-            shape(TOK, 2 * HALF, kind=BF16),
+        out_shape=(quarter,) * XS
+        + (
             shape(2 * TOK, HALF),
             shape(2 * TOK, HALF),
-            low_half(2 * TOK),
-            shape(TOK, 2 * HALF, kind=BF16),
+            low_half(3 * TOK),
+            low_half(TOK),
             low_half(2 * TOK),
             shape(1, HALF),
             shape(3, TOK),
         ),
-        3 * block_flops,
-        8 * 1024 * 1024,
-    )(probs, keep, got, attn, chan, q_norm, *blocks, sink, v_low, v_early_out)
+        in_specs=[pl.BlockSpec(memory_space=pltpu.SMEM)] + [vmem] * 15,
+        scratch_shapes=[pltpu.VMEM((TOK, 2 * HALF), BF16)],
+        compiler_params=pltpu.CompilerParams(vmem_limit_bytes=20 * 1024 * 1024),
+        cost_estimate=pl.CostEstimate(
+            flops=3 * block_flops, bytes_accessed=8 * 1024 * 1024, transcendentals=0
+        ),
+    )(places, probs, keep, got, attn, chan, q_norm, *blocks, sink, v_low, v_near)
 
     near = move_chips(k_prev_out, line_shift(-1))
     far = move_chips(k_early_out, line_shift(-2))
-    from_x = rounds(GATHER_X, low)
+    from_x = [pieces[0]] + [shift_x(pieces[by], by) for by in (1, 2, 3)]
     near, far, from_x = after((near, far, from_x))
     k_total, low, inner, swapped = call(
         key_sum_kernel,
         (
             shape(2 * TOK, HALF),
-            shape(TOK, 2 * HALF, kind=BF16),
+            quarter,
             shape(8, TOK),
             shape(8, TOK),
         ),
         scalar=True,
         args=9,
-    )(places, k_own, near, far, k_norm, inner, low, *from_x)
+    )(places, k_own, near, far, k_norm, inner, *from_x)
     inner = sum_heads(inner + other_core(swapped))
     low = add_parts(low, *rounds(GATHER_Z[0], low))
     sums = jnp.concatenate([gain_sum.reshape(HEADS, HD), inner[4:5]])
@@ -496,15 +507,18 @@
     sums = quads_x(sums, jnp.add)
     sums = pairs_z(sums, jnp.add)
     sums, low = after((sums, low))
-    sums = quads_z(sums, jnp.add)
+    sunk = [low] + rounds(GATHER_X, low)
+    turns = [shift_z(sums, by) for by in (4, 2, 6)]
+    sums, turns, sunk = after((sums, turns, sunk))
+    sums = (sums + turns[0]) + (turns[1] + turns[2])
 
     q_mine, q_other = call(query_kernel, (low_half(TOK), low_half(TOK)))(
         grad_qn, keep, got, tags, tags_got, gains_q, inner
     )
     both = shape(2, TOK, HALF, kind=BF16)
-    mine, other = call(key_kernel, (both, both), scalar=True, args=13)(
-        places, k_total, v_own, v_near, far, low, inner, sums[HEADS:], chan,
-        keep, got, tags, tags_got, gains_k,
+    mine, other = call(key_kernel, (both, both), scalar=True, args=15)(
+        places, k_total, v_own, v_near, near, *sunk, inner, sums[HEADS:], chan,
+        raw_k, tags, tags_got, gains_k,
     )
 
     def cores_out(mine, other):

time: 164 us -> 159 us (0.970)
  waiting for transfers between devices: 57.9 us -> 37.5 us
  starting transfers between devices: 82.4 us -> 96.6 us
    ppermute x38 -> x41, waiting for transfers between devices: 55.2 us -> 34.8 us  [move_chips(): return lax.ppermute(value, 'frame', chip_pairs(move))]
    ppermute x38 -> x41, starting transfers between devices: 56.4 us -> 72.8 us  [move_chips(): return lax.ppermute(value, 'frame', chip_pairs(move))]
    ppermute x7, starting transfers between devices: 17.3 us -> 14.3 us  [other_core(): lax.ppermute(value, 'frame', [(i, i ^ 1) for i in range(2 * XS * ZS)])]
  transfers between devices with their start and end apart: 51 -> 54, of which waited for: 21 -> 22; matrix products, arithmetic and copies ran while one was open for 4% -> 4% of each run, Pallas kernels for 1% -> 1%
where the time goes in v3:
time: 159 us; the launch traced here: 158 us
  starting transfers between devices  96.6 us (61%)
  waiting for transfers between devices  37.5 us (24%)
  Pallas kernels  10.3 us (6%)
  local copies, waits for them, and re-layouts  6.08 us (4%)
  other arithmetic  5.6 us (4%)
  between operations  1.85 us (1%)
    ppermute x41, starting transfers between devices, move_chips(): return lax.ppermute(value, 'frame', chip_pairs(move))  72.8 us
    ppermute x41, waiting for transfers between devices, move_chips(): return lax.ppermute(value, 'frame', chip_pairs(move))  34.8 us
    ppermute x7, starting transfers between devices, other_core(): lax.ppermute(value, 'frame', [(i, i ^ 1) for i in range(2 * XS * ZS)])  14.3 us
    ppermute x6, starting transfers between devices, head_turns(): lax.ppermute(value, 'head', [(i, (i + by) % 4) for i in range(4)])  9.53 us
    unnamed x20, local copies, waits for them, and re-layouts  3.96 us
  transfers between devices with their start and end apart: 54, of which 22 were waited for; matrix products, arithmetic and copies ran while one was open for 4% of the time, Pallas kernels for 1%

profile of v3, /device:TPU:1, one launch (start us, length us, event | category | flops | bytes accessed | tf_op | source)
XLA Modules:
  0.0 157.9 jit_solution(4722444179640894295)
XLA Ops:
  0.7 3.0 %shard_map.127 = (bf16[4,128,640]{2,1,0:T(8,128)(2,1)}, bf16[4,128,640]{2,1,0:T(8,128)(2,1)}, f32[2,128]{1,0:T(2,128)}) custom-call(s32[1]{0:T(128)} %bitcast.1.core, bf16[128,1280]{1,0:T(8,128)(2,1)} %q.1, bf16[128,1280]{1,0:T(8,128)(2,1)} %k.1, bf16[128,1280]{1,0:T(8,128)(2,1)} %v.1, bf16[128,1280]{1,0:T(8,128)(2,1)} %c.1), custom_call_target="tpu_custom_call" | custom-call | tf_op jit(solution)/shard_map/pallas_call | solution.py:393
  3.7 3.6 %collective-permute-start.3 = (f32[2,128]{1,0:T(2,128)}, f32[2,128]{1,0:T(2,128)S(1)}, u32[]{:S(2)}, u32[]{:S(2)}) collective-permute-start(f32[2,128]{1,0:T(2,128)} %get-tuple-element.75), channel_id=1, source_target_pairs={{0,3},{1,0},{2,1},{3,2},{4,7},{5,4},{6,5},{7,6},{8,11},{9,8},{10,9... | collective-permute-start | bytes 3080 | tf_op jit(solution)/shard_map/ppermute | solution.py:64
  14.3 3.6 %collective-permute-start.8 = (bf16[256,640]{1,0:T(8,128)(2,1)S(1)}, bf16[256,640]{1,0:T(8,128)(2,1)S(1)}, u32[]{:S(2)}, u32[]{:S(2)}) collective-permute-start(bf16[256,640]{1,0:T(8,128)(2,1)S(1)} %pad_maximum_fusion.vo), channel_id=1, source_target_pairs={{0,8},{4,12},{8,16},{12,20},{16,24},{20,28},{24,32},{28,36},{32,40... | collective-permute-start | bytes 983048 | tf_op jit(solution)/shard_map/ppermute | solution.py:36
  20.8 3.1 %collective-permute-start.5 = (bf16[32,1280]{1,0:T(8,128)(2,1)S(1)}, bf16[32,1280]{1,0:T(8,128)(2,1)S(1)}, u32[]{:S(2)}, u32[]{:S(2)}) collective-permute-start(bf16[32,1280]{1,0:T(8,128)(2,1)S(1)} %get-tuple-element.80), channel_id=1, source_target_pairs={{0,64},{4,68},{1,65},{5,69},{2,66},{6,70},{3,67},{7,71}} | collective-permute-start | bytes 245768 | tf_op jit(solution)/shard_map/ppermute | solution.py:36
  23.9 2.2 %collective-permute-start.6 = (bf16[32,1280]{1,0:T(8,128)(2,1)S(1)}, bf16[32,1280]{1,0:T(8,128)(2,1)S(1)}, u32[]{:S(2)}, u32[]{:S(2)}) collective-permute-start(bf16[32,1280]{1,0:T(8,128)(2,1)S(1)} %get-tuple-element.81), channel_id=1, source_target_pairs={{0,128},{4,132},{1,129},{5,133},{2,130},{6,134},{3,131},{7,135}} | collective-permute-start | bytes 245768 | tf_op jit(solution)/shard_map/ppermute | solution.py:36
  27.4 3.3 %collective-permute-done.5.refs_1_ = bf16[32,1280]{1,0:T(8,128)(2,1)S(1)} collective-permute-done((bf16[32,1280]{1,0:T(8,128)(2,1)S(1)}, bf16[32,1280]{1,0:T(8,128)(2,1)S(1)}, u32[]{:S(2)}, u32[]{:S(2)}) %collective-permute-start.5) | collective-permute-done | bytes 81952 | tf_op jit(solution)/shard_map/ppermute | solution.py:36
  33.9 2.3 %collective-permute-start.10 = (bf16[32,1280]{1,0:T(8,128)(2,1)S(1)}, bf16[32,1280]{1,0:T(8,128)(2,1)S(1)}, u32[]{:S(2)}, u32[]{:S(2)}) collective-permute-start(bf16[32,1280]{1,0:T(8,128)(2,1)S(1)} %shard_map.129.refs_0_), channel_id=1, source_target_pairs={{0,48},{4,52},{64,112},{68,116},{128,176},{132,180},{192,240},{196... | collective-permute-start | bytes 245768 | tf_op jit(solution)/shard_map/ppermute | solution.py:36
  43.7 2.5 %collective-permute-start.14 = (bf16[128,640]{1,0:T(8,128)(2,1)S(1)}, bf16[128,640]{1,0:T(8,128)(2,1)S(1)}, u32[]{:S(2)}, u32[]{:S(2)}) collective-permute-start(bf16[128,640]{1,0:T(8,128)(2,1)S(1)} %slice_select_fusion.1), channel_id=1, source_target_pairs={{0,8},{4,12},{8,16},{12,20},{16,24},{20,28},{24,32},{28,36},{32,40... | collective-permute-start | bytes 491528 | tf_op jit(solution)/shard_map/ppermute | solution.py:36
  46.1 2.6 %collective-permute-start.18 = (bf16[32,1280]{1,0:T(8,128)(2,1)S(1)}, bf16[32,1280]{1,0:T(8,128)(2,1)S(1)}, u32[]{:S(2)}, u32[]{:S(2)}) collective-permute-start(bf16[32,1280]{1,0:T(8,128)(2,1)S(1)} %shard_map.131.s0), channel_id=1, source_target_pairs={{0,192},{4,196},{8,200},{12,204},{16,208},{20,212},{24,216},{28,22... | collective-permute-start | bytes 245768 | tf_op jit(solution)/shard_map/ppermute | solution.py:36
  48.8 2.4 %collective-permute-start.17 = (bf16[32,1280]{1,0:T(8,128)(2,1)S(1)}, bf16[32,1280]{1,0:T(8,128)(2,1)S(1)}, u32[]{:S(2)}, u32[]{:S(2)}) collective-permute-start(bf16[32,1280]{1,0:T(8,128)(2,1)S(1)} %shard_map.131.s0), channel_id=1, source_target_pairs={{0,128},{4,132},{8,136},{12,140},{16,144},{20,148},{24,152},{28,15... | collective-permute-start | bytes 245768 | tf_op jit(solution)/shard_map/ppermute | solution.py:36
  52.0 7.8 %collective-permute-done.17.s2 = bf16[32,1280]{1,0:T(8,128)(2,1)S(1)} collective-permute-done((bf16[32,1280]{1,0:T(8,128)(2,1)S(1)}, bf16[32,1280]{1,0:T(8,128)(2,1)S(1)}, u32[]{:S(2)}, u32[]{:S(2)}) %collective-permute-start.17) | collective-permute-done | bytes 81952 | tf_op jit(solution)/shard_map/ppermute | solution.py:36
  59.8 2.4 %shard_map.132 = (bf16[256,640]{1,0:T(8,128)(2,1)S(1)}, f32[1,640]{1,0:T(1,128)S(1)}, bf16[5,256,768]{2,1,0:T(8,128)(2,1)S(1)}, bf16[128,1280]{1,0:T(8,128)(2,1)S(1)}) custom-call(s32[1]{0:T(128)} %bitcast.place, f32[256,768]{1,0:T(8,128)S(1)} %get-tuple-element.76.bias, bf16[256,640]{1,0:T(8,128)(2,1)S(1)} %get-tuple-element.77.q, ...), custom_call_target="tpu_custom_call" | custom-call | flops 503316480 | bytes 6291456 | tf_op jit(solution)/shard_map/pallas_call | solution.py:437
  67.5 2.2 %collective-permute-start.21 = (f32[1,640]{1,0:T(1,128)S(1)}, f32[1,640]{1,0:T(1,128)S(1)}, u32[]{:S(2)}, u32[]{:S(2)}) collective-permute-start(f32[1,640]{1,0:T(1,128)S(1)} %max.21), channel_id=1, source_target_pairs={{0,16},{4,20},{8,24},{12,28},{16,32},{20,36},{24,40},{28,44},{32,4... | collective-permute-start | bytes 7688 | tf_op jit(solution)/shard_map/ppermute | solution.py:36
  69.7 4.2 %collective-permute-start.20 = (f32[1,640]{1,0:T(1,128)S(1)}, f32[1,640]{1,0:T(1,128)S(1)}, u32[]{:S(2)}, u32[]{:S(2)}) collective-permute-start(f32[1,640]{1,0:T(1,128)S(1)} %max.21), channel_id=1, source_target_pairs={{0,32},{4,36},{8,40},{12,44},{16,48},{20,52},{24,56},{28,60},{32,0... | collective-permute-start | bytes 7688 | tf_op jit(solution)/shard_map/ppermute | solution.py:36
  77.6 2.5 %collective-permute-start.23 = (f32[1,640]{1,0:T(1,128)S(1)}, f32[1,640]{1,0:T(1,128)S(1)}, u32[]{:S(2)}, u32[]{:S(2)}) collective-permute-start(f32[1,640]{1,0:T(1,128)S(1)} %maximum_maximum_fusion.1), channel_id=1, source_target_pairs={{0,128},{4,132},{8,136},{12,140},{16,144},{20,148},{24,152},{28,15... | collective-permute-start | bytes 7688 | tf_op jit(solution)/shard_map/ppermute | solution.py:36
  87.5 8.2 %collective-permute-start.30 = (bf16[32,1280]{1,0:T(8,128)(2,1)S(1)}, bf16[32,1280]{1,0:T(8,128)(2,1)S(1)}, u32[]{:S(2)}, u32[]{:S(2)}) collective-permute-start(bf16[32,1280]{1,0:T(8,128)(2,1)S(1)} %get-tuple-element.107), channel_id=1, source_target_pairs={{0,64},{4,68},{8,72},{12,76},{16,80},{20,84},{24,88},{28,92},{32,9... | collective-permute-start | bytes 245768 | tf_op jit(solution)/shard_map/ppermute | solution.py:36
  95.7 2.7 %collective-permute-start.31 = (bf16[32,1280]{1,0:T(8,128)(2,1)S(1)}, bf16[32,1280]{1,0:T(8,128)(2,1)S(1)}, u32[]{:S(2)}, u32[]{:S(2)}) collective-permute-start(bf16[32,1280]{1,0:T(8,128)(2,1)S(1)} %get-tuple-element.108), channel_id=1, source_target_pairs={{0,128},{4,132},{8,136},{12,140},{16,144},{20,148},{24,152},{28,15... | collective-permute-start | bytes 245768 | tf_op jit(solution)/shard_map/ppermute | solution.py:36
  103.3 7.0 %collective-permute-start.33 = (f32[8,128]{1,0:T(8,128)S(1)}, f32[8,128]{1,0:T(8,128)S(1)}, u32[]{:S(2)}, u32[]{:S(2)}) collective-permute-start(f32[8,128]{1,0:T(8,128)S(1)} %get-tuple-element.118), channel_id=1, source_target_pairs={{0,4},{4,0},{8,12},{12,8},{16,20},{20,16},{24,28},{28,24},{32,36},... | collective-permute-start | bytes 12296 | tf_op jit(solution)/shard_map/ppermute | solution.py:60
  111.1 2.5 %collective-permute-start.36 = (f32[8,128]{1,0:T(8,128)S(1)}, f32[8,128]{1,0:T(8,128)S(1)}, u32[]{:S(2)}, u32[]{:S(2)}) collective-permute-start(f32[8,128]{1,0:T(8,128)S(1)} %add.50), channel_id=1, source_target_pairs={{0,3},{1,0},{2,1},{3,2},{4,7},{5,4},{6,5},{7,6},{8,11},{9,8},{10,9... | collective-permute-start | bytes 12296 | tf_op jit(solution)/shard_map/ppermute | solution.py:64
  118.1 4.8 %collective-permute-done.39.refs_2_ = bf16[32,1280]{1,0:T(8,128)(2,1)S(1)} collective-permute-done((bf16[32,1280]{1,0:T(8,128)(2,1)S(1)}, bf16[32,1280]{1,0:T(8,128)(2,1)S(1)}, u32[]{:S(2)}, u32[]{:S(2)}) %collective-permute-start.39) | collective-permute-done | bytes 81952 | tf_op jit(solution)/shard_map/ppermute | solution.py:36
  127.5 2.7 %collective-permute-start.27 = (bf16[128,640]{1,0:T(8,128)(2,1)S(1)}, bf16[128,640]{1,0:T(8,128)(2,1)S(1)}, u32[]{:S(2)}, u32[]{:S(2)}) collective-permute-start(bf16[128,640]{1,0:T(8,128)(2,1)S(1)} %get-tuple-element.145), channel_id=1, source_target_pairs={{0,4},{4,0},{8,12},{12,8},{16,20},{20,16},{24,28},{28,24},{32,36},... | collective-permute-start | bytes 491528 | tf_op jit(solution)/shard_map/ppermute | solution.py:60
  135.3 3.6 %collective-permute-done.45.refs_2_ = bf16[32,1280]{1,0:T(8,128)(2,1)S(1)} collective-permute-done((bf16[32,1280]{1,0:T(8,128)(2,1)S(1)}, bf16[32,1280]{1,0:T(8,128)(2,1)S(1)}, u32[]{:S(2)}, u32[]{:S(2)}) %collective-permute-start.45) | collective-permute-done | bytes 81952 | tf_op jit(solution)/shard_map/ppermute | solution.py:36
  140.0 2.3 %collective-permute-start.47 = (f32[6,128]{1,0:T(8,128)S(1)}, f32[6,128]{1,0:T(8,128)S(1)}, u32[]{:S(2)}, u32[]{:S(2)}) collective-permute-start(f32[6,128]{1,0:T(8,128)S(1)} %add.57), channel_id=1, source_target_pairs={{0,16},{4,20},{8,24},{12,28},{16,32},{20,36},{24,40},{28,44},{32,4... | collective-permute-start | bytes 9224 | tf_op jit(solution)/shard_map/ppermute | solution.py:36
  152.2 2.4 %collective-permute-start.53 = (f32[1,640]{1,0:T(1,128)S(1)}, f32[1,640]{1,0:T(1,128)S(1)}, u32[]{:S(2)}, u32[]{:S(2)}) collective-permute-start(f32[1,640]{1,0:T(1,128)S(1)} %bitcast.27), channel_id=1, source_target_pairs={{0,4},{4,0},{8,12},{12,8},{16,20},{20,16},{24,28},{28,24},{32,36},... | collective-permute-start | bytes 7688 | tf_op jit(solution)/shard_map/ppermute | solution.py:60
  (150 shorter events, 72.0 us)
Async XLA Ops:
  3.7 9.9 %collective-permute-start.3 = (f32[2,128]{1,0:T(2,128)}, f32[2,128]{1,0:T(2,128)S(1)}, u32[]{:S(2)}, u32[]{:S(2)}) collective-permute-start(f32[2,128]{1,0:T(2,128)} %get-tuple-element.75), channel_id=1, source_target_pairs={{0,3},{1,0},{2,1},{3,2},{4,7},{5,4},{6,5},{7,6},{8,11},{9,8},{10,9... | collective-permute-start | bytes 3080 | tf_op jit(solution)/shard_map/ppermute | solution.py:64
  14.3 18.2 %collective-permute-start.8 = (bf16[256,640]{1,0:T(8,128)(2,1)S(1)}, bf16[256,640]{1,0:T(8,128)(2,1)S(1)}, u32[]{:S(2)}, u32[]{:S(2)}) collective-permute-start(bf16[256,640]{1,0:T(8,128)(2,1)S(1)} %pad_maximum_fusion.vo), channel_id=1, source_target_pairs={{0,8},{4,12},{8,16},{12,20},{16,24},{20,28},{24,32},{28,36},{32,40... | collective-permute-start | bytes 983048 | tf_op jit(solution)/shard_map/ppermute | solution.py:36
  20.8 10.0 %collective-permute-start.5 = (bf16[32,1280]{1,0:T(8,128)(2,1)S(1)}, bf16[32,1280]{1,0:T(8,128)(2,1)S(1)}, u32[]{:S(2)}, u32[]{:S(2)}) collective-permute-start(bf16[32,1280]{1,0:T(8,128)(2,1)S(1)} %get-tuple-element.80), channel_id=1, source_target_pairs={{0,64},{4,68},{1,65},{5,69},{2,66},{6,70},{3,67},{7,71}} | collective-permute-start | bytes 245768 | tf_op jit(solution)/shard_map/ppermute | solution.py:36
  23.9 8.6 %collective-permute-start.6 = (bf16[32,1280]{1,0:T(8,128)(2,1)S(1)}, bf16[32,1280]{1,0:T(8,128)(2,1)S(1)}, u32[]{:S(2)}, u32[]{:S(2)}) collective-permute-start(bf16[32,1280]{1,0:T(8,128)(2,1)S(1)} %get-tuple-element.81), channel_id=1, source_target_pairs={{0,128},{4,132},{1,129},{5,133},{2,130},{6,134},{3,131},{7,135}} | collective-permute-start | bytes 245768 | tf_op jit(solution)/shard_map/ppermute | solution.py:36
  32.5 11.1 %collective-permute-start.13 = (bf16[256,640]{1,0:T(8,128)(2,1)S(1)}, bf16[256,640]{1,0:T(8,128)(2,1)S(1)}, u32[]{:S(2)}, u32[]{:S(2)}) collective-permute-start(bf16[256,640]{1,0:T(8,128)(2,1)S(1)} %get-tuple-element.86.ko.k_norm), channel_id=1, source_target_pairs={{0,8},{4,12},{8,16},{12,20},{16,24},{20,28},{24,32},{28,36},{32,40... | collective-permute-start | bytes 983048 | tf_op jit(solution)/shard_map/ppermute | solution.py:36
  42.1 9.9 %collective-permute-start.15 = (bf16[128,640]{1,0:T(8,128)(2,1)S(1)}, bf16[128,640]{1,0:T(8,128)(2,1)S(1)}, u32[]{:S(2)}, u32[]{:S(2)}) collective-permute-start(bf16[128,640]{1,0:T(8,128)(2,1)S(1)} %slice_select_fusion), channel_id=1, source_target_pairs={{0,8},{4,12},{8,16},{12,20},{16,24},{20,28},{24,32},{28,36},{32,40... | collective-permute-start | bytes 491528 | tf_op jit(solution)/shard_map/ppermute | solution.py:36
  43.7 16.1 %collective-permute-start.14 = (bf16[128,640]{1,0:T(8,128)(2,1)S(1)}, bf16[128,640]{1,0:T(8,128)(2,1)S(1)}, u32[]{:S(2)}, u32[]{:S(2)}) collective-permute-start(bf16[128,640]{1,0:T(8,128)(2,1)S(1)} %slice_select_fusion.1), channel_id=1, source_target_pairs={{0,8},{4,12},{8,16},{12,20},{16,24},{20,28},{24,32},{28,36},{32,40... | collective-permute-start | bytes 491528 | tf_op jit(solution)/shard_map/ppermute | solution.py:36
  48.8 11.0 %collective-permute-start.17 = (bf16[32,1280]{1,0:T(8,128)(2,1)S(1)}, bf16[32,1280]{1,0:T(8,128)(2,1)S(1)}, u32[]{:S(2)}, u32[]{:S(2)}) collective-permute-start(bf16[32,1280]{1,0:T(8,128)(2,1)S(1)} %shard_map.131.s0), channel_id=1, source_target_pairs={{0,128},{4,132},{8,136},{12,140},{16,144},{20,148},{24,152},{28,15... | collective-permute-start | bytes 245768 | tf_op jit(solution)/shard_map/ppermute | solution.py:36
  51.2 8.6 %collective-permute-start.16 = (bf16[32,1280]{1,0:T(8,128)(2,1)S(1)}, bf16[32,1280]{1,0:T(8,128)(2,1)S(1)}, u32[]{:S(2)}, u32[]{:S(2)}) collective-permute-start(bf16[32,1280]{1,0:T(8,128)(2,1)S(1)} %shard_map.131.s0), channel_id=1, source_target_pairs={{0,64},{4,68},{8,72},{12,76},{16,80},{20,84},{24,88},{28,92},{32,9... | collective-permute-start | bytes 245768 | tf_op jit(solution)/shard_map/ppermute | solution.py:36
  64.7 17.1 %collective-permute-start.26 = (bf16[384,640]{1,0:T(8,128)(2,1)S(1)}, bf16[384,640]{1,0:T(8,128)(2,1)S(1)}, u32[]{:S(2)}, u32[]{:S(2)}) collective-permute-start(bf16[384,640]{1,0:T(8,128)(2,1)S(1)} %get-tuple-element.96), channel_id=1, source_target_pairs={{8,0},{12,4},{16,8},{20,12},{24,16},{28,20},{32,24},{36,28},{40,32... | collective-permute-start | bytes 1474568 | tf_op jit(solution)/shard_map/ppermute | solution.py:36
  66.0 9.8 %collective-permute-start.22 = (f32[1,640]{1,0:T(1,128)S(1)}, f32[1,640]{1,0:T(1,128)S(1)}, u32[]{:S(2)}, u32[]{:S(2)}) collective-permute-start(f32[1,640]{1,0:T(1,128)S(1)} %max.21), channel_id=1, source_target_pairs={{0,48},{4,52},{8,56},{12,60},{16,0},{20,4},{24,8},{28,12},{32,16},... | collective-permute-start | bytes 7688 | tf_op jit(solution)/shard_map/ppermute | solution.py:36
  67.5 8.3 %collective-permute-start.21 = (f32[1,640]{1,0:T(1,128)S(1)}, f32[1,640]{1,0:T(1,128)S(1)}, u32[]{:S(2)}, u32[]{:S(2)}) collective-permute-start(f32[1,640]{1,0:T(1,128)S(1)} %max.21), channel_id=1, source_target_pairs={{0,16},{4,20},{8,24},{12,28},{16,32},{20,36},{24,40},{28,44},{32,4... | collective-permute-start | bytes 7688 | tf_op jit(solution)/shard_map/ppermute | solution.py:36
  84.9 17.1 %collective-permute-start.28 = (bf16[384,640]{1,0:T(8,128)(2,1)S(1)}, bf16[384,640]{1,0:T(8,128)(2,1)S(1)}, u32[]{:S(2)}, u32[]{:S(2)}) collective-permute-start(bf16[384,640]{1,0:T(8,128)(2,1)S(1)} %get-tuple-element.104), channel_id=1, source_target_pairs={{8,0},{12,4},{16,8},{20,12},{24,16},{28,20},{32,24},{36,28},{40,32... | collective-permute-start | bytes 1474568 | tf_op jit(solution)/shard_map/ppermute | solution.py:36
  86.2 15.8 %collective-permute-start.29 = (bf16[128,640]{1,0:T(8,128)(2,1)S(1)}, bf16[128,640]{1,0:T(8,128)(2,1)S(1)}, u32[]{:S(2)}, u32[]{:S(2)}) collective-permute-start(bf16[128,640]{1,0:T(8,128)(2,1)S(1)} %get-tuple-element.105), channel_id=1, source_target_pairs={{16,0},{20,4},{24,8},{28,12},{32,16},{36,20},{40,24},{44,28},{48,3... | collective-permute-start | bytes 491528 | tf_op jit(solution)/shard_map/ppermute | solution.py:36
  87.5 12.0 %collective-permute-start.30 = (bf16[32,1280]{1,0:T(8,128)(2,1)S(1)}, bf16[32,1280]{1,0:T(8,128)(2,1)S(1)}, u32[]{:S(2)}, u32[]{:S(2)}) collective-permute-start(bf16[32,1280]{1,0:T(8,128)(2,1)S(1)} %get-tuple-element.107), channel_id=1, source_target_pairs={{0,64},{4,68},{8,72},{12,76},{16,80},{20,84},{24,88},{28,92},{32,9... | collective-permute-start | bytes 245768 | tf_op jit(solution)/shard_map/ppermute | solution.py:36
  103.3 7.8 %collective-permute-start.33 = (f32[8,128]{1,0:T(8,128)S(1)}, f32[8,128]{1,0:T(8,128)S(1)}, u32[]{:S(2)}, u32[]{:S(2)}) collective-permute-start(f32[8,128]{1,0:T(8,128)S(1)} %get-tuple-element.118), channel_id=1, source_target_pairs={{0,4},{4,0},{8,12},{12,8},{16,20},{20,16},{24,28},{28,24},{32,36},... | collective-permute-start | bytes 12296 | tf_op jit(solution)/shard_map/ppermute | solution.py:60
  122.9 8.5 %collective-permute-start.42 = (f32[6,128]{1,0:T(8,128)S(1)}, f32[6,128]{1,0:T(8,128)S(1)}, u32[]{:S(2)}, u32[]{:S(2)}) collective-permute-start(f32[6,128]{1,0:T(8,128)S(1)} %pad_maximum_fusion.1), channel_id=1, source_target_pairs={{0,192},{4,196},{8,200},{12,204},{16,208},{20,212},{24,216},{28,22... | collective-permute-start | bytes 9224 | tf_op jit(solution)/shard_map/ppermute | solution.py:36
  124.6 8.2 %collective-permute-start.41 = (f32[6,128]{1,0:T(8,128)S(1)}, f32[6,128]{1,0:T(8,128)S(1)}, u32[]{:S(2)}, u32[]{:S(2)}) collective-permute-start(f32[6,128]{1,0:T(8,128)S(1)} %pad_maximum_fusion.1), channel_id=1, source_target_pairs={{0,64},{4,68},{8,72},{12,76},{16,80},{20,84},{24,88},{28,92},{32,9... | collective-permute-start | bytes 9224 | tf_op jit(solution)/shard_map/ppermute | solution.py:36
  124.6 8.2 %collective-permute-start.40 = (f32[6,128]{1,0:T(8,128)S(1)}, f32[6,128]{1,0:T(8,128)S(1)}, u32[]{:S(2)}, u32[]{:S(2)}) collective-permute-start(f32[6,128]{1,0:T(8,128)S(1)} %pad_maximum_fusion.1), channel_id=1, source_target_pairs={{0,128},{4,132},{8,136},{12,140},{16,144},{20,148},{24,152},{28,15... | collective-permute-start | bytes 9224 | tf_op jit(solution)/shard_map/ppermute | solution.py:36
  127.5 11.7 %collective-permute-start.27 = (bf16[128,640]{1,0:T(8,128)(2,1)S(1)}, bf16[128,640]{1,0:T(8,128)(2,1)S(1)}, u32[]{:S(2)}, u32[]{:S(2)}) collective-permute-start(bf16[128,640]{1,0:T(8,128)(2,1)S(1)} %get-tuple-element.145), channel_id=1, source_target_pairs={{0,4},{4,0},{8,12},{12,8},{16,20},{20,16},{24,28},{28,24},{32,36},... | collective-permute-start | bytes 491528 | tf_op jit(solution)/shard_map/ppermute | solution.py:60
  130.2 8.8 %collective-permute-start.45 = (bf16[32,1280]{1,0:T(8,128)(2,1)S(1)}, bf16[32,1280]{1,0:T(8,128)(2,1)S(1)}, u32[]{:S(2)}, u32[]{:S(2)}) collective-permute-start(bf16[32,1280]{1,0:T(8,128)(2,1)S(1)} %shard_map.137.refs_0_), channel_id=1, source_target_pairs={{40,0},{44,4},{104,64},{108,68},{168,128},{172,132},{232,192},{236... | collective-permute-start | bytes 245768 | tf_op jit(solution)/shard_map/ppermute | solution.py:36
  131.5 7.6 %collective-permute-start.44 = (bf16[32,1280]{1,0:T(8,128)(2,1)S(1)}, bf16[32,1280]{1,0:T(8,128)(2,1)S(1)}, u32[]{:S(2)}, u32[]{:S(2)}) collective-permute-start(bf16[32,1280]{1,0:T(8,128)(2,1)S(1)} %shard_map.137.refs_0_), channel_id=1, source_target_pairs={{24,0},{28,4},{88,64},{92,68},{152,128},{156,132},{216,192},{220,1... | collective-permute-start | bytes 245768 | tf_op jit(solution)/shard_map/ppermute | solution.py:36
  134.3 12.4 %collective-permute-start.37 = (bf16[128,640]{1,0:T(8,128)(2,1)S(1)}, bf16[128,640]{1,0:T(8,128)(2,1)S(1)}, u32[]{:S(2)}, u32[]{:S(2)}) collective-permute-start(bf16[128,640]{1,0:T(8,128)(2,1)S(1)} %get-tuple-element.120), channel_id=1, source_target_pairs={{0,4},{4,0},{8,12},{12,8},{16,20},{20,16},{24,28},{28,24},{32,36},... | collective-permute-start | bytes 491528 | tf_op jit(solution)/shard_map/ppermute | solution.py:60
  140.0 8.8 %collective-permute-start.47 = (f32[6,128]{1,0:T(8,128)S(1)}, f32[6,128]{1,0:T(8,128)S(1)}, u32[]{:S(2)}, u32[]{:S(2)}) collective-permute-start(f32[6,128]{1,0:T(8,128)S(1)} %add.57), channel_id=1, source_target_pairs={{0,16},{4,20},{8,24},{12,28},{16,32},{20,36},{24,40},{28,44},{32,4... | collective-permute-start | bytes 9224 | tf_op jit(solution)/shard_map/ppermute | solution.py:36
  (39 other events, 237.9 us)

commit v4 on v3

--- a/solution.py
+++ b/solution.py
@@ -85,7 +85,7 @@
 GATHER_X = tuple(row(src, 0, (0,)) for src in range(1, XS))
 SPREAD_Z = (
     (column({0: 5}, range(XS)), column({0: 6}, range(XS))),
-    (column({0: 7, 5: 3, 6: 4}, range(XS)), column({0: 1, 5: 2}, range(XS))),
+    (column({0: 1, 5: 3, 6: 7}, range(XS)), column({0: 2, 5: 4}, range(XS))),
 )
 GATHER_Z = (
     (column({1: 0, 4: 3, 6: 5}, range(XS)), column({7: 0, 2: 3}, range(XS))),
@@ -431,7 +431,8 @@
     low = add_parts(low, *rounds(SPREAD_Z[1], low))
     low, k_prev = after((low, k_prev))
     k_early = move_chips(second_group(k_prev), line_shift(1))
-    parts = [low] + [shift_x(low, by) for by in (1, 2, 3)]
+    turns = {by: shift_x(low, by) for by in (1, 3, 2)}
+    parts = [low, turns[1], turns[2], turns[3]]
     blocks = (k_norm, k_prev, k_early, v2, v_prev, v_early)
 
     attn, top, probs, sink = call(

time: 159 us -> 159 us (level)
  no operation moved by 1% of the time
where the time goes in v4:
time: 159 us; the launch traced here: 158 us
  starting transfers between devices  96.1 us (60%)
  waiting for transfers between devices  38.4 us (24%)
  Pallas kernels  10.3 us (6%)
  local copies, waits for them, and re-layouts  6.08 us (4%)
  other arithmetic  5.6 us (4%)
  between operations  1.86 us (1%)
    ppermute x41, starting transfers between devices, move_chips(): return lax.ppermute(value, 'frame', chip_pairs(move))  73.5 us
    ppermute x41, waiting for transfers between devices, move_chips(): return lax.ppermute(value, 'frame', chip_pairs(move))  35.8 us
    ppermute x7, starting transfers between devices, other_core(): lax.ppermute(value, 'frame', [(i, i ^ 1) for i in range(2 * XS * ZS)])  13.9 us
    ppermute x6, starting transfers between devices, head_turns(): lax.ppermute(value, 'head', [(i, (i + by) % 4) for i in range(4)])  8.69 us
    unnamed x20, local copies, waits for them, and re-layouts  3.96 us
  transfers between devices with their start and end apart: 54, of which 22 were waited for; matrix products, arithmetic and copies ran while one was open for 4% of the time, Pallas kernels for 1%

profile of v4, /device:TPU:1, one launch (start us, length us, event | category | flops | bytes accessed | tf_op | source)
XLA Modules:
  0.0 158.3 jit_solution(10611526329205025470)
XLA Ops:
  0.7 3.0 %shard_map.127 = (bf16[4,128,640]{2,1,0:T(8,128)(2,1)}, bf16[4,128,640]{2,1,0:T(8,128)(2,1)}, f32[2,128]{1,0:T(2,128)}) custom-call(s32[1]{0:T(128)} %bitcast.1.core, bf16[128,1280]{1,0:T(8,128)(2,1)} %q.1, bf16[128,1280]{1,0:T(8,128)(2,1)} %k.1, bf16[128,1280]{1,0:T(8,128)(2,1)} %v.1, bf16[128,1280]{1,0:T(8,128)(2,1)} %c.1), custom_call_target="tpu_custom_call" | custom-call | tf_op jit(solution)/shard_map/pallas_call | solution.py:393
  3.7 3.6 %collective-permute-start.3 = (f32[2,128]{1,0:T(2,128)}, f32[2,128]{1,0:T(2,128)S(1)}, u32[]{:S(2)}, u32[]{:S(2)}) collective-permute-start(f32[2,128]{1,0:T(2,128)} %get-tuple-element.75), channel_id=1, source_target_pairs={{0,3},{1,0},{2,1},{3,2},{4,7},{5,4},{6,5},{7,6},{8,11},{9,8},{10,9... | collective-permute-start | bytes 3080 | tf_op jit(solution)/shard_map/ppermute | solution.py:64
  14.3 3.6 %collective-permute-start.8 = (bf16[256,640]{1,0:T(8,128)(2,1)S(1)}, bf16[256,640]{1,0:T(8,128)(2,1)S(1)}, u32[]{:S(2)}, u32[]{:S(2)}) collective-permute-start(bf16[256,640]{1,0:T(8,128)(2,1)S(1)} %pad_maximum_fusion.vo), channel_id=1, source_target_pairs={{0,8},{4,12},{8,16},{12,20},{16,24},{20,28},{24,32},{28,36},{32,40... | collective-permute-start | bytes 983048 | tf_op jit(solution)/shard_map/ppermute | solution.py:36
  20.8 3.1 %collective-permute-start.5 = (bf16[32,1280]{1,0:T(8,128)(2,1)S(1)}, bf16[32,1280]{1,0:T(8,128)(2,1)S(1)}, u32[]{:S(2)}, u32[]{:S(2)}) collective-permute-start(bf16[32,1280]{1,0:T(8,128)(2,1)S(1)} %get-tuple-element.80), channel_id=1, source_target_pairs={{0,64},{4,68},{1,65},{5,69},{2,66},{6,70},{3,67},{7,71}} | collective-permute-start | bytes 245768 | tf_op jit(solution)/shard_map/ppermute | solution.py:36
  27.4 3.3 %collective-permute-done.5.refs_1_ = bf16[32,1280]{1,0:T(8,128)(2,1)S(1)} collective-permute-done((bf16[32,1280]{1,0:T(8,128)(2,1)S(1)}, bf16[32,1280]{1,0:T(8,128)(2,1)S(1)}, u32[]{:S(2)}, u32[]{:S(2)}) %collective-permute-start.5) | collective-permute-done | bytes 81952 | tf_op jit(solution)/shard_map/ppermute | solution.py:36
  33.9 2.3 %collective-permute-start.10 = (bf16[32,1280]{1,0:T(8,128)(2,1)S(1)}, bf16[32,1280]{1,0:T(8,128)(2,1)S(1)}, u32[]{:S(2)}, u32[]{:S(2)}) collective-permute-start(bf16[32,1280]{1,0:T(8,128)(2,1)S(1)} %shard_map.129.refs_0_), channel_id=1, source_target_pairs={{0,48},{4,52},{64,112},{68,116},{128,176},{132,180},{192,240},{196... | collective-permute-start | bytes 245768 | tf_op jit(solution)/shard_map/ppermute | solution.py:36
  44.1 3.8 %collective-permute-start.14 = (bf16[128,640]{1,0:T(8,128)(2,1)S(1)}, bf16[128,640]{1,0:T(8,128)(2,1)S(1)}, u32[]{:S(2)}, u32[]{:S(2)}) collective-permute-start(bf16[128,640]{1,0:T(8,128)(2,1)S(1)} %slice_select_fusion.1), channel_id=1, source_target_pairs={{0,8},{4,12},{8,16},{12,20},{16,24},{20,28},{24,32},{28,36},{32,40... | collective-permute-start | bytes 491528 | tf_op jit(solution)/shard_map/ppermute | solution.py:36
  47.9 2.6 %collective-permute-start.18 = (bf16[32,1280]{1,0:T(8,128)(2,1)S(1)}, bf16[32,1280]{1,0:T(8,128)(2,1)S(1)}, u32[]{:S(2)}, u32[]{:S(2)}) collective-permute-start(bf16[32,1280]{1,0:T(8,128)(2,1)S(1)} %shard_map.131.s0), channel_id=1, source_target_pairs={{0,192},{4,196},{8,200},{12,204},{16,208},{20,212},{24,216},{28,22... | collective-permute-start | bytes 245768 | tf_op jit(solution)/shard_map/ppermute | solution.py:36
  50.5 2.5 %collective-permute-start.17 = (bf16[32,1280]{1,0:T(8,128)(2,1)S(1)}, bf16[32,1280]{1,0:T(8,128)(2,1)S(1)}, u32[]{:S(2)}, u32[]{:S(2)}) collective-permute-start(bf16[32,1280]{1,0:T(8,128)(2,1)S(1)} %shard_map.131.s0), channel_id=1, source_target_pairs={{0,128},{4,132},{8,136},{12,140},{16,144},{20,148},{24,152},{28,15... | collective-permute-start | bytes 245768 | tf_op jit(solution)/shard_map/ppermute | solution.py:36
  53.7 6.3 %collective-permute-done.17.s2 = bf16[32,1280]{1,0:T(8,128)(2,1)S(1)} collective-permute-done((bf16[32,1280]{1,0:T(8,128)(2,1)S(1)}, bf16[32,1280]{1,0:T(8,128)(2,1)S(1)}, u32[]{:S(2)}, u32[]{:S(2)}) %collective-permute-start.17) | collective-permute-done | bytes 81952 | tf_op jit(solution)/shard_map/ppermute | solution.py:36
  60.1 2.4 %shard_map.132 = (bf16[256,640]{1,0:T(8,128)(2,1)S(1)}, f32[1,640]{1,0:T(1,128)S(1)}, bf16[5,256,768]{2,1,0:T(8,128)(2,1)S(1)}, bf16[128,1280]{1,0:T(8,128)(2,1)S(1)}) custom-call(s32[1]{0:T(128)} %bitcast.place, f32[256,768]{1,0:T(8,128)S(1)} %get-tuple-element.76.bias, bf16[256,640]{1,0:T(8,128)(2,1)S(1)} %get-tuple-element.77.q, ...), custom_call_target="tpu_custom_call" | custom-call | flops 503316480 | bytes 6291456 | tf_op jit(solution)/shard_map/pallas_call | solution.py:438
  69.1 4.2 %collective-permute-start.20 = (f32[1,640]{1,0:T(1,128)S(1)}, f32[1,640]{1,0:T(1,128)S(1)}, u32[]{:S(2)}, u32[]{:S(2)}) collective-permute-start(f32[1,640]{1,0:T(1,128)S(1)} %max.21), channel_id=1, source_target_pairs={{0,32},{4,36},{8,40},{12,44},{16,48},{20,52},{24,56},{28,60},{32,0... | collective-permute-start | bytes 7688 | tf_op jit(solution)/shard_map/ppermute | solution.py:36
  73.3 2.6 %collective-permute-done.22 = f32[1,640]{1,0:T(1,128)S(1)} collective-permute-done((f32[1,640]{1,0:T(1,128)S(1)}, f32[1,640]{1,0:T(1,128)S(1)}, u32[]{:S(2)}, u32[]{:S(2)}) %collective-permute-start.22) | collective-permute-done | bytes 2592 | tf_op jit(solution)/shard_map/ppermute | solution.py:36
  75.9 2.5 %collective-permute-start.25 = (f32[1,640]{1,0:T(1,128)S(1)}, f32[1,640]{1,0:T(1,128)S(1)}, u32[]{:S(2)}, u32[]{:S(2)}) collective-permute-start(f32[1,640]{1,0:T(1,128)S(1)} %maximum_maximum_fusion.1), channel_id=1, source_target_pairs={{0,192},{4,196},{8,200},{12,204},{16,208},{20,212},{24,216},{28,22... | collective-permute-start | bytes 7688 | tf_op jit(solution)/shard_map/ppermute | solution.py:36
  78.4 2.6 %collective-permute-start.23 = (f32[1,640]{1,0:T(1,128)S(1)}, f32[1,640]{1,0:T(1,128)S(1)}, u32[]{:S(2)}, u32[]{:S(2)}) collective-permute-start(f32[1,640]{1,0:T(1,128)S(1)} %maximum_maximum_fusion.1), channel_id=1, source_target_pairs={{0,128},{4,132},{8,136},{12,140},{16,144},{20,148},{24,152},{28,15... | collective-permute-start | bytes 7688 | tf_op jit(solution)/shard_map/ppermute | solution.py:36
  88.1 8.5 %collective-permute-start.30 = (bf16[32,1280]{1,0:T(8,128)(2,1)S(1)}, bf16[32,1280]{1,0:T(8,128)(2,1)S(1)}, u32[]{:S(2)}, u32[]{:S(2)}) collective-permute-start(bf16[32,1280]{1,0:T(8,128)(2,1)S(1)} %get-tuple-element.107), channel_id=1, source_target_pairs={{0,64},{4,68},{8,72},{12,76},{16,80},{20,84},{24,88},{28,92},{32,9... | collective-permute-start | bytes 245768 | tf_op jit(solution)/shard_map/ppermute | solution.py:36
  96.6 2.3 %collective-permute-start.31 = (bf16[32,1280]{1,0:T(8,128)(2,1)S(1)}, bf16[32,1280]{1,0:T(8,128)(2,1)S(1)}, u32[]{:S(2)}, u32[]{:S(2)}) collective-permute-start(bf16[32,1280]{1,0:T(8,128)(2,1)S(1)} %get-tuple-element.108), channel_id=1, source_target_pairs={{0,128},{4,132},{8,136},{12,140},{16,144},{20,148},{24,152},{28,15... | collective-permute-start | bytes 245768 | tf_op jit(solution)/shard_map/ppermute | solution.py:36
  103.7 6.6 %collective-permute-start.33 = (f32[8,128]{1,0:T(8,128)S(1)}, f32[8,128]{1,0:T(8,128)S(1)}, u32[]{:S(2)}, u32[]{:S(2)}) collective-permute-start(f32[8,128]{1,0:T(8,128)S(1)} %get-tuple-element.118), channel_id=1, source_target_pairs={{0,4},{4,0},{8,12},{12,8},{16,20},{20,16},{24,28},{28,24},{32,36},... | collective-permute-start | bytes 12296 | tf_op jit(solution)/shard_map/ppermute | solution.py:60
  117.2 5.4 %collective-permute-done.39.refs_2_ = bf16[32,1280]{1,0:T(8,128)(2,1)S(1)} collective-permute-done((bf16[32,1280]{1,0:T(8,128)(2,1)S(1)}, bf16[32,1280]{1,0:T(8,128)(2,1)S(1)}, u32[]{:S(2)}, u32[]{:S(2)}) %collective-permute-start.39) | collective-permute-done | bytes 81952 | tf_op jit(solution)/shard_map/ppermute | solution.py:36
  124.5 2.4 %collective-permute-start.40 = (f32[6,128]{1,0:T(8,128)S(1)}, f32[6,128]{1,0:T(8,128)S(1)}, u32[]{:S(2)}, u32[]{:S(2)}) collective-permute-start(f32[6,128]{1,0:T(8,128)S(1)} %pad_maximum_fusion.1), channel_id=1, source_target_pairs={{0,128},{4,132},{8,136},{12,140},{16,144},{20,148},{24,152},{28,15... | collective-permute-start | bytes 9224 | tf_op jit(solution)/shard_map/ppermute | solution.py:36
  127.9 2.7 %collective-permute-start.27 = (bf16[128,640]{1,0:T(8,128)(2,1)S(1)}, bf16[128,640]{1,0:T(8,128)(2,1)S(1)}, u32[]{:S(2)}, u32[]{:S(2)}) collective-permute-start(bf16[128,640]{1,0:T(8,128)(2,1)S(1)} %get-tuple-element.145), channel_id=1, source_target_pairs={{0,4},{4,0},{8,12},{12,8},{16,20},{20,16},{24,28},{28,24},{32,36},... | collective-permute-start | bytes 491528 | tf_op jit(solution)/shard_map/ppermute | solution.py:60
  135.7 3.6 %collective-permute-done.45.refs_2_ = bf16[32,1280]{1,0:T(8,128)(2,1)S(1)} collective-permute-done((bf16[32,1280]{1,0:T(8,128)(2,1)S(1)}, bf16[32,1280]{1,0:T(8,128)(2,1)S(1)}, u32[]{:S(2)}, u32[]{:S(2)}) %collective-permute-start.45) | collective-permute-done | bytes 81952 | tf_op jit(solution)/shard_map/ppermute | solution.py:36
  140.4 2.3 %collective-permute-start.47 = (f32[6,128]{1,0:T(8,128)S(1)}, f32[6,128]{1,0:T(8,128)S(1)}, u32[]{:S(2)}, u32[]{:S(2)}) collective-permute-start(f32[6,128]{1,0:T(8,128)S(1)} %add.57), channel_id=1, source_target_pairs={{0,16},{4,20},{8,24},{12,28},{16,32},{20,36},{24,40},{28,44},{32,4... | collective-permute-start | bytes 9224 | tf_op jit(solution)/shard_map/ppermute | solution.py:36
  152.6 2.4 %collective-permute-start.53 = (f32[1,640]{1,0:T(1,128)S(1)}, f32[1,640]{1,0:T(1,128)S(1)}, u32[]{:S(2)}, u32[]{:S(2)}) collective-permute-start(f32[1,640]{1,0:T(1,128)S(1)} %bitcast.27), channel_id=1, source_target_pairs={{0,4},{4,0},{8,12},{12,8},{16,20},{20,16},{24,28},{28,24},{32,36},... | collective-permute-start | bytes 7688 | tf_op jit(solution)/shard_map/ppermute | solution.py:60
  (150 shorter events, 71.9 us)
Async XLA Ops:
  3.7 9.9 %collective-permute-start.3 = (f32[2,128]{1,0:T(2,128)}, f32[2,128]{1,0:T(2,128)S(1)}, u32[]{:S(2)}, u32[]{:S(2)}) collective-permute-start(f32[2,128]{1,0:T(2,128)} %get-tuple-element.75), channel_id=1, source_target_pairs={{0,3},{1,0},{2,1},{3,2},{4,7},{5,4},{6,5},{7,6},{8,11},{9,8},{10,9... | collective-permute-start | bytes 3080 | tf_op jit(solution)/shard_map/ppermute | solution.py:64
  14.3 18.2 %collective-permute-start.8 = (bf16[256,640]{1,0:T(8,128)(2,1)S(1)}, bf16[256,640]{1,0:T(8,128)(2,1)S(1)}, u32[]{:S(2)}, u32[]{:S(2)}) collective-permute-start(bf16[256,640]{1,0:T(8,128)(2,1)S(1)} %pad_maximum_fusion.vo), channel_id=1, source_target_pairs={{0,8},{4,12},{8,16},{12,20},{16,24},{20,28},{24,32},{28,36},{32,40... | collective-permute-start | bytes 983048 | tf_op jit(solution)/shard_map/ppermute | solution.py:36
  20.8 10.0 %collective-permute-start.5 = (bf16[32,1280]{1,0:T(8,128)(2,1)S(1)}, bf16[32,1280]{1,0:T(8,128)(2,1)S(1)}, u32[]{:S(2)}, u32[]{:S(2)}) collective-permute-start(bf16[32,1280]{1,0:T(8,128)(2,1)S(1)} %get-tuple-element.80), channel_id=1, source_target_pairs={{0,64},{4,68},{1,65},{5,69},{2,66},{6,70},{3,67},{7,71}} | collective-permute-start | bytes 245768 | tf_op jit(solution)/shard_map/ppermute | solution.py:36
  23.9 8.6 %collective-permute-start.6 = (bf16[32,1280]{1,0:T(8,128)(2,1)S(1)}, bf16[32,1280]{1,0:T(8,128)(2,1)S(1)}, u32[]{:S(2)}, u32[]{:S(2)}) collective-permute-start(bf16[32,1280]{1,0:T(8,128)(2,1)S(1)} %get-tuple-element.81), channel_id=1, source_target_pairs={{0,128},{4,132},{1,129},{5,133},{2,130},{6,134},{3,131},{7,135}} | collective-permute-start | bytes 245768 | tf_op jit(solution)/shard_map/ppermute | solution.py:36
  32.5 11.5 %collective-permute-start.13 = (bf16[256,640]{1,0:T(8,128)(2,1)S(1)}, bf16[256,640]{1,0:T(8,128)(2,1)S(1)}, u32[]{:S(2)}, u32[]{:S(2)}) collective-permute-start(bf16[256,640]{1,0:T(8,128)(2,1)S(1)} %get-tuple-element.86.ko.k_norm), channel_id=1, source_target_pairs={{0,8},{4,12},{8,16},{12,20},{16,24},{20,28},{24,32},{28,36},{32,40... | collective-permute-start | bytes 983048 | tf_op jit(solution)/shard_map/ppermute | solution.py:36
  42.1 11.6 %collective-permute-start.15 = (bf16[128,640]{1,0:T(8,128)(2,1)S(1)}, bf16[128,640]{1,0:T(8,128)(2,1)S(1)}, u32[]{:S(2)}, u32[]{:S(2)}) collective-permute-start(bf16[128,640]{1,0:T(8,128)(2,1)S(1)} %slice_select_fusion), channel_id=1, source_target_pairs={{0,8},{4,12},{8,16},{12,20},{16,24},{20,28},{24,32},{28,36},{32,40... | collective-permute-start | bytes 491528 | tf_op jit(solution)/shard_map/ppermute | solution.py:36
  44.1 15.9 %collective-permute-start.14 = (bf16[128,640]{1,0:T(8,128)(2,1)S(1)}, bf16[128,640]{1,0:T(8,128)(2,1)S(1)}, u32[]{:S(2)}, u32[]{:S(2)}) collective-permute-start(bf16[128,640]{1,0:T(8,128)(2,1)S(1)} %slice_select_fusion.1), channel_id=1, source_target_pairs={{0,8},{4,12},{8,16},{12,20},{16,24},{20,28},{24,32},{28,36},{32,40... | collective-permute-start | bytes 491528 | tf_op jit(solution)/shard_map/ppermute | solution.py:36
  50.5 9.6 %collective-permute-start.17 = (bf16[32,1280]{1,0:T(8,128)(2,1)S(1)}, bf16[32,1280]{1,0:T(8,128)(2,1)S(1)}, u32[]{:S(2)}, u32[]{:S(2)}) collective-permute-start(bf16[32,1280]{1,0:T(8,128)(2,1)S(1)} %shard_map.131.s0), channel_id=1, source_target_pairs={{0,128},{4,132},{8,136},{12,140},{16,144},{20,148},{24,152},{28,15... | collective-permute-start | bytes 245768 | tf_op jit(solution)/shard_map/ppermute | solution.py:36
  65.0 17.4 %collective-permute-start.26 = (bf16[384,640]{1,0:T(8,128)(2,1)S(1)}, bf16[384,640]{1,0:T(8,128)(2,1)S(1)}, u32[]{:S(2)}, u32[]{:S(2)}) collective-permute-start(bf16[384,640]{1,0:T(8,128)(2,1)S(1)} %get-tuple-element.96), channel_id=1, source_target_pairs={{8,0},{12,4},{16,8},{20,12},{24,16},{28,20},{32,24},{36,28},{40,32... | collective-permute-start | bytes 1474568 | tf_op jit(solution)/shard_map/ppermute | solution.py:36
  66.3 9.6 %collective-permute-start.22 = (f32[1,640]{1,0:T(1,128)S(1)}, f32[1,640]{1,0:T(1,128)S(1)}, u32[]{:S(2)}, u32[]{:S(2)}) collective-permute-start(f32[1,640]{1,0:T(1,128)S(1)} %max.21), channel_id=1, source_target_pairs={{0,48},{4,52},{8,56},{12,60},{16,0},{20,4},{24,8},{28,12},{32,16},... | collective-permute-start | bytes 7688 | tf_op jit(solution)/shard_map/ppermute | solution.py:36
  67.0 8.9 %collective-permute-start.21 = (f32[1,640]{1,0:T(1,128)S(1)}, f32[1,640]{1,0:T(1,128)S(1)}, u32[]{:S(2)}, u32[]{:S(2)}) collective-permute-start(f32[1,640]{1,0:T(1,128)S(1)} %max.21), channel_id=1, source_target_pairs={{0,16},{4,20},{8,24},{12,28},{16,32},{20,36},{24,40},{28,44},{32,4... | collective-permute-start | bytes 7688 | tf_op jit(solution)/shard_map/ppermute | solution.py:36
  85.5 16.9 %collective-permute-start.28 = (bf16[384,640]{1,0:T(8,128)(2,1)S(1)}, bf16[384,640]{1,0:T(8,128)(2,1)S(1)}, u32[]{:S(2)}, u32[]{:S(2)}) collective-permute-start(bf16[384,640]{1,0:T(8,128)(2,1)S(1)} %get-tuple-element.104), channel_id=1, source_target_pairs={{8,0},{12,4},{16,8},{20,12},{24,16},{28,20},{32,24},{36,28},{40,32... | collective-permute-start | bytes 1474568 | tf_op jit(solution)/shard_map/ppermute | solution.py:36
  86.8 15.6 %collective-permute-start.29 = (bf16[128,640]{1,0:T(8,128)(2,1)S(1)}, bf16[128,640]{1,0:T(8,128)(2,1)S(1)}, u32[]{:S(2)}, u32[]{:S(2)}) collective-permute-start(bf16[128,640]{1,0:T(8,128)(2,1)S(1)} %get-tuple-element.105), channel_id=1, source_target_pairs={{16,0},{20,4},{24,8},{28,12},{32,16},{36,20},{40,24},{44,28},{48,3... | collective-permute-start | bytes 491528 | tf_op jit(solution)/shard_map/ppermute | solution.py:36
  88.1 11.4 %collective-permute-start.30 = (bf16[32,1280]{1,0:T(8,128)(2,1)S(1)}, bf16[32,1280]{1,0:T(8,128)(2,1)S(1)}, u32[]{:S(2)}, u32[]{:S(2)}) collective-permute-start(bf16[32,1280]{1,0:T(8,128)(2,1)S(1)} %get-tuple-element.107), channel_id=1, source_target_pairs={{0,64},{4,68},{8,72},{12,76},{16,80},{20,84},{24,88},{28,92},{32,9... | collective-permute-start | bytes 245768 | tf_op jit(solution)/shard_map/ppermute | solution.py:36
  103.7 7.4 %collective-permute-start.33 = (f32[8,128]{1,0:T(8,128)S(1)}, f32[8,128]{1,0:T(8,128)S(1)}, u32[]{:S(2)}, u32[]{:S(2)}) collective-permute-start(f32[8,128]{1,0:T(8,128)S(1)} %get-tuple-element.118), channel_id=1, source_target_pairs={{0,4},{4,0},{8,12},{12,8},{16,20},{20,16},{24,28},{28,24},{32,36},... | collective-permute-start | bytes 12296 | tf_op jit(solution)/shard_map/ppermute | solution.py:60
  114.6 8.1 %collective-permute-start.39 = (bf16[32,1280]{1,0:T(8,128)(2,1)S(1)}, bf16[32,1280]{1,0:T(8,128)(2,1)S(1)}, u32[]{:S(2)}, u32[]{:S(2)}) collective-permute-start(bf16[32,1280]{1,0:T(8,128)(2,1)S(1)} %get-tuple-element.124.refs_0_), channel_id=1, source_target_pairs={{16,24},{20,28},{56,0},{60,4},{80,88},{84,92},{120,64},{124,68},{1... | collective-permute-start | bytes 245768 | tf_op jit(solution)/shard_map/ppermute | solution.py:36
  122.7 9.1 %collective-permute-start.42 = (f32[6,128]{1,0:T(8,128)S(1)}, f32[6,128]{1,0:T(8,128)S(1)}, u32[]{:S(2)}, u32[]{:S(2)}) collective-permute-start(f32[6,128]{1,0:T(8,128)S(1)} %pad_maximum_fusion.1), channel_id=1, source_target_pairs={{0,192},{4,196},{8,200},{12,204},{16,208},{20,212},{24,216},{28,22... | collective-permute-start | bytes 9224 | tf_op jit(solution)/shard_map/ppermute | solution.py:36
  124.5 8.7 %collective-permute-start.41 = (f32[6,128]{1,0:T(8,128)S(1)}, f32[6,128]{1,0:T(8,128)S(1)}, u32[]{:S(2)}, u32[]{:S(2)}) collective-permute-start(f32[6,128]{1,0:T(8,128)S(1)} %pad_maximum_fusion.1), channel_id=1, source_target_pairs={{0,64},{4,68},{8,72},{12,76},{16,80},{20,84},{24,88},{28,92},{32,9... | collective-permute-start | bytes 9224 | tf_op jit(solution)/shard_map/ppermute | solution.py:36
  124.5 8.7 %collective-permute-start.40 = (f32[6,128]{1,0:T(8,128)S(1)}, f32[6,128]{1,0:T(8,128)S(1)}, u32[]{:S(2)}, u32[]{:S(2)}) collective-permute-start(f32[6,128]{1,0:T(8,128)S(1)} %pad_maximum_fusion.1), channel_id=1, source_target_pairs={{0,128},{4,132},{8,136},{12,140},{16,144},{20,148},{24,152},{28,15... | collective-permute-start | bytes 9224 | tf_op jit(solution)/shard_map/ppermute | solution.py:36
  127.9 11.7 %collective-permute-start.27 = (bf16[128,640]{1,0:T(8,128)(2,1)S(1)}, bf16[128,640]{1,0:T(8,128)(2,1)S(1)}, u32[]{:S(2)}, u32[]{:S(2)}) collective-permute-start(bf16[128,640]{1,0:T(8,128)(2,1)S(1)} %get-tuple-element.145), channel_id=1, source_target_pairs={{0,4},{4,0},{8,12},{12,8},{16,20},{20,16},{24,28},{28,24},{32,36},... | collective-permute-start | bytes 491528 | tf_op jit(solution)/shard_map/ppermute | solution.py:60
  130.6 8.8 %collective-permute-start.45 = (bf16[32,1280]{1,0:T(8,128)(2,1)S(1)}, bf16[32,1280]{1,0:T(8,128)(2,1)S(1)}, u32[]{:S(2)}, u32[]{:S(2)}) collective-permute-start(bf16[32,1280]{1,0:T(8,128)(2,1)S(1)} %shard_map.137.refs_0_), channel_id=1, source_target_pairs={{40,0},{44,4},{104,64},{108,68},{168,128},{172,132},{232,192},{236... | collective-permute-start | bytes 245768 | tf_op jit(solution)/shard_map/ppermute | solution.py:36
  131.9 7.6 %collective-permute-start.44 = (bf16[32,1280]{1,0:T(8,128)(2,1)S(1)}, bf16[32,1280]{1,0:T(8,128)(2,1)S(1)}, u32[]{:S(2)}, u32[]{:S(2)}) collective-permute-start(bf16[32,1280]{1,0:T(8,128)(2,1)S(1)} %shard_map.137.refs_0_), channel_id=1, source_target_pairs={{24,0},{28,4},{88,64},{92,68},{152,128},{156,132},{216,192},{220,1... | collective-permute-start | bytes 245768 | tf_op jit(solution)/shard_map/ppermute | solution.py:36
  134.7 12.4 %collective-permute-start.37 = (bf16[128,640]{1,0:T(8,128)(2,1)S(1)}, bf16[128,640]{1,0:T(8,128)(2,1)S(1)}, u32[]{:S(2)}, u32[]{:S(2)}) collective-permute-start(bf16[128,640]{1,0:T(8,128)(2,1)S(1)} %get-tuple-element.120), channel_id=1, source_target_pairs={{0,4},{4,0},{8,12},{12,8},{16,20},{20,16},{24,28},{28,24},{32,36},... | collective-permute-start | bytes 491528 | tf_op jit(solution)/shard_map/ppermute | solution.py:60
  140.4 8.8 %collective-permute-start.47 = (f32[6,128]{1,0:T(8,128)S(1)}, f32[6,128]{1,0:T(8,128)S(1)}, u32[]{:S(2)}, u32[]{:S(2)}) collective-permute-start(f32[6,128]{1,0:T(8,128)S(1)} %add.57), channel_id=1, source_target_pairs={{0,16},{4,20},{8,24},{12,28},{16,32},{20,36},{24,40},{28,44},{32,4... | collective-permute-start | bytes 9224 | tf_op jit(solution)/shard_map/ppermute | solution.py:36
  (39 other events, 238.2 us)
